TPU v7x, 32 devices: a whole 2x2x4 slice. The times are simulated.
32 devices in a mesh: prow: 4 (over x, core), pcol: 8 (over z, y).
Axes of the slice: x: 2, y: 2, z: 4, core: 2. Of those that a mesh axis runs over, the one named last changes fastest.
Arguments:
- sep_inverse: bfloat16 [2, 4, 256, 1, 8, 256], P(None, 'prow', None, None, 'pcol'), may hold values from -2 to 30, as said below
- panels: bfloat16 [4, 2, 4, 256, 256], P(None, None, 'prow', 'pcol'), may hold values from -0.125 to 0.125
- ancestors: int32 [4, 8], replicated, may hold values from 0 to 1, as said below
- window_factor: bfloat16 [6, 256, 256], replicated, may hold values from -0.1875 to 0.1875
- diag_inverse: bfloat16 [4, 256, 256], replicated, may hold values from -1 to 4, as said below
Outputs:
- ys: float32 [4, 2, 4, 256, 256], P(None, None, 'prow', 'pcol')
- window_inverse: float32 [1024, 1024], P('prow', 'pcol')
Inputs may be any that keep to these rules, and one draw needn't show every extreme that they name: sep_inverse read as in the first step is symmetric. `diag_inverse`: each block is symmetric. ancestors[k + 1, t] <= ancestors[k, t]: a supernode's ancestor tiles lie among those of the one before it.
All inputs are finite; a program needn't handle non-finite values.
Results may differ from a plain program's by a relative error of at most 0.00035.
Values may be sent and summed in bfloat16 or wider, within the bound.
No kernel may reach another device: no remote copies, remote signals or barrier semaphores. Data moves between devices by JAX's collectives and lax.ppermute only.
A program may use at most 64 MiB of HBM per device.

v0:
```python
import jax
import jax.numpy as jnp
from jax import lax
from jax.sharding import PartitionSpec as P


def product(operand_left, operand_right):
    return jnp.dot(
        operand_left,
        operand_right,
        precision=lax.Precision.HIGHEST,
        preferred_element_type=jnp.float32,
    )


def pair_index(earlier, later):
    return later * (later - 1) // 2 + earlier


def window_step(later, window_sums, window_factor, diag_inverse, window_blocks):
    coupled = []
    for earlier in range(later):
        running = window_sums[earlier]
        for partner in range(later):
            running = running + product(
                window_blocks[earlier, partner],
                window_factor[pair_index(partner, later)].astype(jnp.float32),
            )
        upper_block = -running
        window_blocks[earlier, later] = upper_block
        window_blocks[later, earlier] = upper_block.T
        coupled.append(upper_block)
    running = window_sums[later]
    for earlier in range(later):
        running = running + product(
            window_factor[pair_index(earlier, later)].astype(jnp.float32).T, coupled[earlier]
        )
    window_blocks[later, later] = diag_inverse[later].astype(jnp.float32) - running


def assemble_window(window_blocks, supernodes):
    return jnp.block(
        [
            [window_blocks[first, second] for second in range(supernodes)]
            for first in range(supernodes)
        ]
    )


def per_device(sep_inverse, panels, ancestors, window_factor, diag_inverse):
    prow_count = lax.axis_size("prow")
    pcol_count = lax.axis_size("pcol")
    row_index = lax.axis_index("prow")
    column_index = lax.axis_index("pcol")
    tile_rows = sep_inverse.shape[0]
    width = sep_inverse.shape[2]
    owned_count = sep_inverse.shape[3]
    supernodes = panels.shape[0]
    slice_rows = panels.shape[3]
    local_sep = sep_inverse.reshape(tile_rows, width, owned_count, width)
    window_blocks = {}
    columns = []
    for later in range(supernodes):
        tile_flags = lax.dynamic_slice_in_dim(
            ancestors[later].reshape(tile_rows, prow_count), row_index, 1, 1
        )
        keep_tiles = tile_flags.astype(jnp.bfloat16).reshape(tile_rows, 1, 1)
        own_piece = panels[later, :, 0] * keep_tiles
        stacked = lax.all_gather(own_piece[:, None], "prow", axis=1, tiled=True)
        spread = stacked.reshape(owned_count, pcol_count, slice_rows, width)
        owned_tiles = lax.all_to_all(spread, "pcol", split_axis=1, concat_axis=2, tiled=True)[:, 0]

        def row_term(first_row, row_count, owned_tiles=owned_tiles):
            return jnp.einsum(
                "rbcd,cde->bre", local_sep, owned_tiles, preferred_element_type=jnp.float32
            )

        summed = lax.psum_scatter(
            row_term(jnp.int32(0), slice_rows * lax.axis_size("pcol")),
            "pcol",
            scatter_dimension=0,
            tiled=True,
        )
        row_total = jnp.transpose(summed, (1, 0, 2)).reshape(tile_rows * slice_rows, width)
        row_keep = jnp.repeat(
            tile_flags[:, 0].astype(jnp.float32),
            slice_rows,
            total_repeat_length=tile_rows * slice_rows,
        )
        carried = -row_total
        for earlier in range(later):
            carried = carried - product(
                columns[earlier], window_factor[pair_index(earlier, later)].astype(jnp.float32)
            )
        current = carried * row_keep[:, None]
        factor_rows = own_piece.reshape(tile_rows * slice_rows, width).astype(jnp.float32)
        window_parts = [product(columns[earlier].T, factor_rows) for earlier in range(later)]
        window_parts.append(product(factor_rows.T, current))
        window_sums = lax.psum(jnp.stack(window_parts), ("prow", "pcol"))
        window_step(later, window_sums, window_factor, diag_inverse, window_blocks)
        columns.append(current)
    ys = jnp.stack(columns).reshape(supernodes, tile_rows, 1, slice_rows, width)
    whole_window = assemble_window(window_blocks, supernodes)
    rows_each = supernodes * width // prow_count
    cols_each = supernodes * width // pcol_count
    local_window = lax.dynamic_slice(
        whole_window, (row_index * rows_each, column_index * cols_each), (rows_each, cols_each)
    )
    return (ys, local_window)


def solution(mesh):
    placed = (
        P(None, "prow", None, None, "pcol", None),
        P(None, None, "prow", "pcol", None),
        P(),
        P(),
        P(),
    )
    return jax.shard_map(
        per_device,
        mesh=mesh,
        in_specs=placed,
        out_specs=(P(None, None, "prow", "pcol", None), P("prow", "pcol")),
        check_vma=False,
    )
```

profile of v0, /device:TPU:0, one launch (start us, length us, event | category | flops | bytes accessed | tf_op | source)
XLA Modules:
  0.0 353.1 jit_solution(2924952009943328382)
XLA Ops:
  7.2 0.8 slice_reduce_fusion.1
  8.8 0.9 bitcast_multiply_fusion.5
  9.7 7.0 %all_gather.12 = bf16[2,4,32,256]{3,2,1,0:T(8,128)(2,1)} all-gather(bf16[2,1,32,256]{3,2,1,0:T(8,128)(2,1)S(1)} %get-tuple-element.65), channel_id=1, replica_groups=mesh['prow'=4,'pcol'=8] {'prow'}, dimensions={1}, use_global_device_ids=true | all-gather | bytes 163840 | tf_op jit(solution)/shard_map/all_gather | solution.py:69
  16.7 6.2 %all-to-all-start = ((bf16[1,8,32,256]{3,2,0,1:T(8,128)(2,1)}), bf16[1,8,32,256]{3,2,0,1:T(8,128)(2,1)S(1)}, u32[]{:S(2)}, u32[]{:S(2)}) async-start(bf16[1,8,32,256]{3,2,0,1:T(8,128)(2,1)} %bitcast.3), calls=%async_computation | async-start | bytes 262144 | tf_op jit(solution)/shard_map/all_to_all | solution.py:71
  22.9 5.9 %all_gather.14 = bf16[2,4,32,256]{3,2,1,0:T(8,128)(2,1)} all-gather(bf16[2,1,32,256]{3,2,1,0:T(8,128)(2,1)S(1)} %get-tuple-element.62), channel_id=1, replica_groups=mesh['prow'=4,'pcol'=8] {'prow'}, dimensions={1}, use_global_device_ids=true | all-gather | bytes 163840 | tf_op jit(solution)/shard_map/all_gather | solution.py:69
  28.8 5.9 %all_gather.13 = bf16[2,4,32,256]{3,2,1,0:T(8,128)(2,1)} all-gather(bf16[2,1,32,256]{3,2,1,0:T(8,128)(2,1)S(1)} %get-tuple-element.63), channel_id=1, replica_groups=mesh['prow'=4,'pcol'=8] {'prow'}, dimensions={1}, use_global_device_ids=true | all-gather | bytes 163840 | tf_op jit(solution)/shard_map/all_gather | solution.py:69
  34.7 5.9 %all_gather.15 = bf16[2,4,32,256]{3,2,1,0:T(8,128)(2,1)} all-gather(bf16[2,1,32,256]{3,2,1,0:T(8,128)(2,1)S(1)} %get-tuple-element.64), channel_id=1, replica_groups=mesh['prow'=4,'pcol'=8] {'prow'}, dimensions={1}, use_global_device_ids=true | all-gather | bytes 163840 | tf_op jit(solution)/shard_map/all_gather | solution.py:69
  40.6 6.0 %all-to-all-start.3 = ((bf16[1,8,32,256]{3,2,0,1:T(8,128)(2,1)}), bf16[1,8,32,256]{3,2,0,1:T(8,128)(2,1)S(1)}, u32[]{:S(2)}, u32[]{:S(2)}) async-start(bf16[1,8,32,256]{3,2,0,1:T(8,128)(2,1)} %bitcast.46), calls=%async_computation.3 | async-start | bytes 262144 | tf_op jit(solution)/shard_map/all_to_all | solution.py:71
  46.8 1.0 copy.51
  47.8 6.2 %all-to-all-done.3 = bf16[1,8,32,256]{3,2,0,1:T(8,128)(2,1)S(1)} async-done(((bf16[1,8,32,256]{3,2,0,1:T(8,128)(2,1)}), bf16[1,8,32,256]{3,2,0,1:T(8,128)(2,1)S(1)}, u32[]{:S(2)}, u32[]{:S(2)}) %all-to-all-start.3) | async-done | bytes 131104 | tf_op jit(solution)/shard_map/all_to_all | solution.py:71
  54.1 3.4 all-to-all-start.1
  57.7 1.0 copy.66
  58.7 6.0 %all-to-all-done.1 = bf16[1,8,32,256]{3,2,0,1:T(8,128)(2,1)S(1)} async-done(((bf16[1,8,32,256]{3,2,0,1:T(8,128)(2,1)}), bf16[1,8,32,256]{3,2,0,1:T(8,128)(2,1)S(1)}, u32[]{:S(2)}, u32[]{:S(2)}) %all-to-all-start.1) | async-done | bytes 131104 | tf_op jit(solution)/shard_map/all_to_all | solution.py:71
  64.7 3.4 all-to-all-start.2
  68.4 1.0 copy.56
  69.4 5.9 %all-to-all-done.2 = bf16[1,8,32,256]{3,2,0,1:T(8,128)(2,1)S(1)} async-done(((bf16[1,8,32,256]{3,2,0,1:T(8,128)(2,1)}), bf16[1,8,32,256]{3,2,0,1:T(8,128)(2,1)S(1)}, u32[]{:S(2)}, u32[]{:S(2)}) %all-to-all-start.2) | async-done | bytes 131104 | tf_op jit(solution)/shard_map/all_to_all | solution.py:71
  75.6 1.0 copy.61
  76.9 0.4 copy-done.10
  77.3 0.6 dynamic-slice.15
  79.5 0.6 fusion.94
  80.1 0.6 fusion.95
  80.7 0.7 fusion.96
  81.3 0.6 fusion.97
  81.9 5.0 %broadcast_select_fusion = (f32[64]{0:T(128)S(1)}, f32[64]{0:T(128)S(1)}, f32[64]{0:T(128)S(1)}, f32[64]{0:T(128)S(1)}) fusion(pred[64]{0:T(512)(128)(4,1)S(1)} %copy-done.9, f32[]{:T(128)} %bitcast.56, f32[]{:T(128)} %bitcast.55, f32[]{:T(128)} %bitcast.40, f32[]{:T(128)} %bitcast.39, f32[]{:T(128)} %bitcast.25, f32[]{:T(128)} %bitcast.24, f32[]{:T(128)} %bitcast.10, ...), kind=kLoop, calls=%fused_computation.197 | loop fusion | flops 256 | bytes 1120 | tf_op jit(solution)/shard_map/jit(_take)/gather | solution.py:85
  87.3 91.0 %all-reduce.11.cloned.1.call-done = (f32[256,2,256]{2,1,0:T(2,128)}, f32[256,2,256]{2,1,0:T(2,128)}, f32[256,2,256]{2,1,0:T(2,128)}, f32[256,2,256]{2,1,0:T(2,128)}) async-done(((f32[256,2,256]{2,1,0:T(2,128)}, f32[256,2,256]{2,1,0:T(2,128)}, f32[256,2,256]{2,1,0:T(2,128)}, f32[256,2,256]{2,1,0:T(2,128)}), (f32[256,2,256]{2,1,0:T(2,128)}, f32[256,2,256]{2,1,0:T(2,128)}, f32[256,2,256]{2,1,0:T(2,128)}, ...) | async-done | bytes 2097168
  178.3 0.8 constant_dynamic-slice_fusion.3
  179.1 0.8 constant_dynamic-slice_fusion.2
  180.0 0.8 constant_dynamic-slice_fusion.1
  181.4 0.3 convolution_bitcast_fusion.15
  182.2 0.3 convolution_bitcast_fusion.11
  182.6 0.3 convolution_bitcast_fusion.12
  182.9 0.8 constant_dynamic-slice_fusion
  184.2 0.3 convolution_bitcast_fusion.17
  184.5 0.3 convolution_bitcast_fusion.13
  184.8 0.3 convolution_bitcast_fusion.16
  185.2 0.3 convolution_bitcast_fusion.18
  185.5 1.0 convolution_bitcast_fusion.19
  186.7 0.3 convolution_bitcast_fusion.10
  187.1 0.8 pad_maximum_fusion.2
  187.9 0.9 pad_maximum_fusion.1
  188.8 1.1 pad_maximum_fusion
  190.0 0.7 pad_maximum_fusion.3
  190.7 135.3 %all-reduce.9.cloned.1.call-done = (f32[1,256,256]{2,1,0:T(8,128)}, f32[4,256,256]{2,1,0:T(8,128)}, f32[2,256,256]{2,1,0:T(8,128)}, f32[3,256,256]{2,1,0:T(8,128)}) async-done(((f32[1,256,256]{2,1,0:T(8,128)}, f32[4,256,256]{2,1,0:T(8,128)}, f32[2,256,256]{2,1,0:T(8,128)}, f32[3,256,256]{2,1,0:T(8,128)}), (f32[1,256,256]{2,1,0:T(8,128)}, f32[4,256,256]{2,1,0:T(8,128)}, f32[2,256,256]{2,1,0:T(8,128)}, ...) | async-done | bytes 2621456 | tf_op jit(solution)/shard_map/psum | solution.py:99
  326.0 1.0 subtract_bitcast_fusion
  327.1 1.3 fusion.14
  328.4 0.3 fusion.11
  328.7 0.4 convolution_add_fusion.5
  329.4 0.4 copy-done.5
  329.9 0.4 convolution_add_fusion.7
  330.8 1.0 fusion.7
  331.8 0.4 convolution_add_fusion.2
  332.2 0.8 copy.73
  333.9 0.9 copy.77
  334.7 0.9 copy.82
  336.2 0.4 copy-done.4
  336.5 1.2 fusion.6
  337.8 0.8 copy.76
  338.6 2.0 fusion.3
  340.6 0.8 copy.81
  341.4 0.4 convolution_add_fusion.1
  341.8 0.6 copy-done.3
  342.4 0.3 fusion.2
  343.0 1.9 fusion.1
  345.0 1.3 maximum_maximum_fusion
  (68 shorter events, 7.8 us)
Async XLA Ops:
  7.2 39.4 %copy-start = (bf16[2,1,256,1,1,256]{5,2,4,3,1,0:T(8,128)(2,1)S(1)}, bf16[2,1,256,1,1,256]{5,2,4,3,1,0:T(8,128)(2,1)}, u32[]{:S(2)}) copy-start(bf16[2,1,256,1,1,256]{5,2,4,3,1,0:T(8,128)(2,1)} %param.15) | copy-start | bytes 786436
  16.7 23.9 %all-to-all-start = ((bf16[1,8,32,256]{3,2,0,1:T(8,128)(2,1)}), bf16[1,8,32,256]{3,2,0,1:T(8,128)(2,1)S(1)}, u32[]{:S(2)}, u32[]{:S(2)}) async-start(bf16[1,8,32,256]{3,2,0,1:T(8,128)(2,1)} %bitcast.3), calls=%async_computation | async-start | bytes 262144 | tf_op jit(solution)/shard_map/all_to_all | solution.py:71
  40.6 13.5 %all-to-all-start.3 = ((bf16[1,8,32,256]{3,2,0,1:T(8,128)(2,1)}), bf16[1,8,32,256]{3,2,0,1:T(8,128)(2,1)S(1)}, u32[]{:S(2)}, u32[]{:S(2)}) async-start(bf16[1,8,32,256]{3,2,0,1:T(8,128)(2,1)} %bitcast.46), calls=%async_computation.3 | async-start | bytes 262144 | tf_op jit(solution)/shard_map/all_to_all | solution.py:71
  54.1 10.7 %all-to-all-start.1 = ((bf16[1,8,32,256]{3,2,0,1:T(8,128)(2,1)}), bf16[1,8,32,256]{3,2,0,1:T(8,128)(2,1)S(1)}, u32[]{:S(2)}, u32[]{:S(2)}) async-start(bf16[1,8,32,256]{3,2,0,1:T(8,128)(2,1)} %bitcast.16), calls=%async_computation.1 | async-start | bytes 262144 | tf_op jit(solution)/shard_map/all_to_all | solution.py:71
  64.7 10.7 %all-to-all-start.2 = ((bf16[1,8,32,256]{3,2,0,1:T(8,128)(2,1)}), bf16[1,8,32,256]{3,2,0,1:T(8,128)(2,1)S(1)}, u32[]{:S(2)}, u32[]{:S(2)}) async-start(bf16[1,8,32,256]{3,2,0,1:T(8,128)(2,1)} %bitcast.31), calls=%async_computation.2 | async-start | bytes 262144 | tf_op jit(solution)/shard_map/all_to_all | solution.py:71
  68.1 110.2 %all-reduce.11.cloned.1.call-start = ((), (), s32[]{:S(2)}) async-start(), calls=%async_computation.5 | async-start | bytes 4194304
  76.7 0.7 copy-start.10
  76.7 5.2 %copy-start.9 = (pred[64]{0:T(512)(128)(4,1)S(1)}, pred[64]{0:T(512)(128)(4,1)}, u32[]{:S(2)}) copy-start(pred[64]{0:T(512)(128)(4,1)} %constant.158) | copy-start | bytes 196
  76.7 10.3 %copy-start.7 = (bf16[4,2,1,32,256]{4,3,2,1,0:T(8,128)(2,1)S(1)}, bf16[4,2,1,32,256]{4,3,2,1,0:T(8,128)(2,1)}, u32[]{:S(2)}) copy-start(bf16[4,2,1,32,256]{4,3,2,1,0:T(8,128)(2,1)} %param.16) | copy-start | bytes 393220
  76.7 104.2 %copy-start.1 = (bf16[6,256,256]{2,1,0:T(8,128)(2,1)S(1)}, bf16[6,256,256]{2,1,0:T(8,128)(2,1)}, u32[]{:S(2)}) copy-start(bf16[6,256,256]{2,1,0:T(8,128)(2,1)} %param.18) | copy-start | bytes 2359300
  76.7 249.3 %all-reduce.9.cloned.1.call-start = ((), (), s32[]{:S(2)}) async-start(), calls=%async_computation.4 | async-start | bytes 5242880 | tf_op jit(solution)/shard_map/psum | solution.py:99
  189.9 136.1 %copy-start.8 = (bf16[4,256,256]{2,1,0:T(8,128)(2,1)S(1)}, bf16[4,256,256]{2,1,0:T(8,128)(2,1)}, u32[]{:S(2)}) copy-start(bf16[4,256,256]{2,1,0:T(8,128)(2,1)} %param.19) | copy-start | bytes 1572868
  326.0 2.4 copy-start.6
  327.1 1.7 copy-start.2
  328.7 1.1 copy-start.5
  335.6 0.9 copy-start.4
  341.4 0.9 copy-start.3
Sparse Core Ops, SparseCore 0:
  76.8 101.4 all-reduce.10
  190.1 135.9 all-reduce.8
where the time goes:
time: 354 us; the launch traced here: 353 us
  waiting for transfers between devices  244 us (69%)
  blocking collectives  24.6 us (7%)
  starting transfers between devices  19.2 us (5%)
  local copies, waits for them, and re-layouts  18.3 us (5%)
  matrix products  18.2 us (5%)
  between operations  15.1 us (4%)
  other arithmetic  13.2 us (4%)
    psum x1, waiting for transfers between devices, per_device(): window_sums = lax.psum(jnp.stack(window_parts), ('prow', 'pcol'))  135 us
    unnamed x3, waiting for transfers between devices  91 us
    all_gather x4, blocking collectives, per_device(): stacked = lax.all_gather(own_piece[:, None], 'prow', axis=1, tiled=True)  24.6 us
    all_to_all x4, starting transfers between devices, per_device(): lax.all_to_all(spread, 'pcol', split_axis=1, concat_axis=2, tiled=True)  19 us
    all_to_all x4, waiting for transfers between devices, per_device(): lax.all_to_all(spread, 'pcol', split_axis=1, concat_axis=2, tiled=True)  18.2 us
    dot_general x36, matrix products, product(): jnp.dot(operand_left, operand_right, precision=lax.Precision.HIGHEST, pre...  17.2 us
  transfers between devices with their start and end apart: 6, of which 5 were waited for; matrix products, arithmetic and copies ran while one was open for 4% of the time, Pallas kernels for 0%

commit v1 on v0

v1 whole, which is shorter than its diff:
```python
import functools

import jax
import jax.numpy as jnp
from jax import lax
from jax.experimental import pallas as pl
from jax.experimental.pallas import tpu as pltpu
from jax.sharding import PartitionSpec as P

AXES = ("prow", "pcol")
HIGHEST = lax.Precision.HIGHEST
VMEM = pl.BlockSpec(memory_space=pltpu.VMEM)
SMEM = pl.BlockSpec(memory_space=pltpu.SMEM)


def pair_index(earlier, later):
    return later * (later - 1) // 2 + earlier


def exact_dot(left, right):
    return jnp.dot(left, right, precision=HIGHEST, preferred_element_type=jnp.float32)


def dot(left, right):
    return jnp.dot(left, right, preferred_element_type=jnp.float32)


def dot_rows(left, right):
    return lax.dot_general(
        left, right, (((0,), (0,)), ((), ())), preferred_element_type=jnp.float32
    )


def split(value):
    high = value.astype(jnp.bfloat16)
    return high, (value - high.astype(jnp.float32)).astype(jnp.bfloat16)


def move(value, dx, dc, dz, dy):
    prow_count, pcol_count = (lax.axis_size(a) for a in AXES)
    flip_row, flip_col = 2 * dx + dc, 2 * dz + dy
    pairs = [
        (p * pcol_count + q, (p ^ flip_row) * pcol_count + (q ^ flip_col))
        for p in range(prow_count)
        for q in range(pcol_count)
    ]
    return lax.ppermute(value, AXES, pairs)


def inverse_blocks(window_factor, supernodes):
    factor = window_factor.astype(jnp.float32)
    blocks = {}
    for later in range(supernodes):
        for earlier in range(later):
            total = factor[pair_index(earlier, later)]
            for middle in range(earlier + 1, later):
                total = total + exact_dot(
                    blocks[earlier, middle], factor[pair_index(middle, later)]
                )
            blocks[earlier, later] = -total
    return blocks


def products_kernel(place_ref, flags_ref, *refs, pieces, supernodes, tile_rows, prow_count):
    panel_refs, inverse_ref = refs[:pieces], refs[pieces]
    high_ref, low_ref, panel_ref = refs[pieces + 1 :]
    prow, z = place_ref[0], place_ref[4]
    for later in range(supernodes):
        for r in range(tile_rows):
            keep = flags_ref[later, r * prow_count + prow].astype(jnp.float32)
            for d in range(pieces):
                panel_ref[later, r, lax.bitwise_xor(z, d)] = (
                    panel_refs[d][later, r].astype(jnp.float32) * keep
                )
    rows, width = high_ref.shape[1], high_ref.shape[2]
    panels = [panel_ref[k].reshape(rows, width) for k in range(supernodes)]
    for later in range(supernodes):
        total = panels[later]
        for earlier in range(later):
            total = total + exact_dot(panels[earlier], inverse_ref[pair_index(earlier, later)])
        high_ref[later], low_ref[later] = split(total)


def main_kernel(place_ref, flags_ref, *refs, lanes, pieces, supernodes, prow_count, width, steps):
    lane_refs, sep_refs = refs[:lanes], refs[lanes : lanes + pieces]
    high_ref, low_ref = refs[lanes + pieces : lanes + pieces + 2]
    column_refs = refs[lanes + pieces + 2 : lanes + 2 * pieces + 2]
    keep_ref, send_ref, gathered_ref, sums_ref, window_ref = refs[lanes + 2 * pieces + 2 :]
    prow, x, core, y, z = (place_ref[i] for i in range(5))
    _, tile_rows, sub_count, slice_rows, block = lane_refs[0].shape
    kind = gathered_ref.dtype
    for lane, (dx, dc, dy) in enumerate(steps):
        lane_prow = 2 * lax.bitwise_xor(x, dx) + lax.bitwise_xor(core, dc)
        parity = lax.bitwise_xor(y, dy)
        for half in range(2):
            for r in range(tile_rows):
                for sub in range(sub_count):
                    gathered_ref[half, r * prow_count + lane_prow, 2 * sub + parity] = lane_refs[
                        lane
                    ][half, r, sub].astype(kind)
    total = None
    for d in range(pieces):
        for dy in range(2):
            tile = 2 * lax.bitwise_xor(z, d) + lax.bitwise_xor(y, dy)
            sep = sep_refs[d][dy]
            for half in range(2):
                part = gathered_ref[half, tile].reshape(width, block).astype(jnp.bfloat16)
                term = dot(sep, part)
                total = term if total is None else total + term
    later = (z * block) // width
    sums_ref[...] = total.reshape(sums_ref.shape)
    for d in range(pieces):
        for r in range(tile_rows):
            keep = flags_ref[later, r * prow_count + prow].astype(jnp.float32)
            column_refs[d][r] = sums_ref[r, lax.bitwise_xor(z, d)] * -keep
    high, low = split(total)
    for k in range(supernodes):
        left_high, left_low = high_ref[k], low_ref[k]
        window_ref[k * width : (k + 1) * width, :] = (
            dot_rows(left_high, high) + dot_rows(left_high, low) + dot_rows(left_low, high)
        )
    x_count, _, rows_each, cols_each = keep_ref.shape
    for dx in range(x_count):
        for target, dc in ((keep_ref, 0), (send_ref, 1)):
            row_block = 2 * lax.bitwise_xor(x, dx) + lax.bitwise_xor(core, dc)
            rows = window_ref[pl.ds(pl.multiple_of(row_block * rows_each, rows_each), rows_each), :]
            first, second = rows[:, :cols_each], rows[:, cols_each:]
            target[dx, 0] = jnp.where(y == 0, first, second)
            target[dx, 1] = jnp.where(y == 0, second, first)


def add_kernel(keep_ref, received_ref, *out_refs):
    x_count = keep_ref.shape[0]
    for dx in range(x_count):
        for dy in range(2):
            out_refs[2 * dx + dy][...] = keep_ref[dx, dy] + received_ref[dx, dy]


def last_kernel(place_ref, *refs, parts, pieces):
    z = place_ref[4]
    part_refs, own_ref = refs[:parts], refs[parts]
    column_refs = refs[parts + 1 : parts + 1 + pieces]
    window_ref, ys_ref = refs[parts + 1 + pieces :]
    total = own_ref[...]
    for ref in part_refs:
        total = total + ref[...]
    window_ref[...] = total
    for d in range(pieces):
        ys_ref[lax.bitwise_xor(z, d)] = column_refs[d][...]


def call(kernel, operands, scalars, outs, scratch, flops):
    return pl.pallas_call(
        kernel,
        out_shape=outs,
        in_specs=[SMEM] * scalars + [VMEM] * (len(operands) - scalars),
        out_specs=[VMEM] * len(outs),
        scratch_shapes=scratch,
        compiler_params=pltpu.CompilerParams(vmem_limit_bytes=56 * 1024 * 1024),
        cost_estimate=pl.CostEstimate(flops=flops, bytes_accessed=1 << 20, transcendentals=0),
    )(*operands)


def per_device(sep_inverse, panels, ancestors, window_factor, diag_inverse):
    prow_count, pcol_count = (lax.axis_size(a) for a in AXES)
    prow, pcol = (lax.axis_index(a) for a in AXES)
    x_count, z_count = prow_count // 2, pcol_count // 2
    x, core, z, y = prow // 2, prow % 2, pcol // 2, pcol % 2
    tile_rows, width = sep_inverse.shape[0], sep_inverse.shape[2]
    supernodes, slice_rows = panels.shape[0], panels.shape[3]
    order = supernodes * width
    block = order // z_count
    rows_each, cols_each = order // prow_count, order // pcol_count
    rows = tile_rows * z_count * slice_rows
    bf16, f32 = jnp.bfloat16, jnp.float32
    shape = jax.ShapeDtypeStruct
    place = jnp.stack([prow, x, core, y, z]).astype(jnp.int32)

    own_panels = panels.reshape(supernodes, tile_rows, slice_rows, width)
    panel_pieces = [own_panels] + [move(own_panels, 0, 0, d, 0) for d in range(1, z_count)]
    by_parity = sep_inverse.reshape(tile_rows, z_count, 2, slice_rows, width)
    kept = lax.dynamic_index_in_dim(by_parity, y, 2, keepdims=False)
    given = move(lax.dynamic_index_in_dim(by_parity, 1 - y, 2, keepdims=False), 0, 0, 0, 1)
    own_sep = jnp.stack([kept, given]).reshape(2, rows, width)
    sep_pieces = [own_sep] + [move(own_sep, 0, 0, d, 0) for d in range(1, z_count)]

    inverse = inverse_blocks(window_factor, supernodes)
    stacked = jnp.stack([inverse[m, k] for k in range(supernodes) for m in range(k)])
    whole = jnp.block(
        [
            [
                jnp.eye(width, dtype=f32)
                if m == k
                else inverse[m, k]
                if m < k
                else jnp.zeros((width, width), f32)
                for k in range(supernodes)
            ]
            for m in range(supernodes)
        ]
    )
    row_side = lax.dynamic_slice_in_dim(whole, prow * rows_each, rows_each, 1)
    col_side = lax.dynamic_slice_in_dim(whole, pcol * cols_each, cols_each, 1)
    scaled = jnp.einsum(
        "kab,kbc->kac",
        diag_inverse.astype(f32),
        col_side.reshape(supernodes, width, cols_each),
        precision=HIGHEST,
        preferred_element_type=f32,
    ).reshape(order, cols_each)
    own_window = exact_dot(row_side.T, scaled)

    high, low = call(
        functools.partial(
            products_kernel,
            pieces=z_count,
            supernodes=supernodes,
            tile_rows=tile_rows,
            prow_count=prow_count,
        ),
        [place, ancestors, *panel_pieces, stacked],
        2,
        [shape((supernodes, rows, width), bf16)] * 2,
        [pltpu.VMEM((supernodes, tile_rows, z_count, slice_rows, width), f32)],
        6 * rows * order * order,
    )
    both = jnp.stack([high, low])
    if block == width:
        mine = lax.dynamic_index_in_dim(both, z, 1, keepdims=False)
    else:
        chosen = lax.dynamic_index_in_dim(both, (z * block) // width, 1, keepdims=False)
        mine = lax.dynamic_slice_in_dim(chosen, (z * block) % width, block, 2)
    mine = mine.reshape(2, tile_rows, z_count, slice_rows, block)
    steps, lanes = [], []
    for dx in range(x_count):
        for dy in range(2):
            lane = mine if dx + dy == 0 else move(mine, dx, 0, 0, dy)
            lanes.append(lane)
            steps.append((dx, 0, dy))
    for (dx, _, dy), lane in zip(list(steps), list(lanes)):
        lanes.append(move(lane, 0, 1, 0, 0))
        steps.append((dx, 1, dy))

    kind = bf16 if slice_rows % 16 == 0 else f32
    *columns, keep, send = call(
        functools.partial(
            main_kernel,
            lanes=len(lanes),
            pieces=z_count,
            supernodes=supernodes,
            prow_count=prow_count,
            width=width,
            steps=tuple(steps),
        ),
        [place, ancestors, *lanes, *sep_pieces, high, low],
        2,
        [shape((tile_rows, slice_rows, block), f32)] * z_count
        + [shape((x_count, 2, rows_each, cols_each), f32)] * 2,
        [
            pltpu.VMEM((2, tile_rows * prow_count, pcol_count, slice_rows, block), kind),
            pltpu.VMEM((tile_rows, z_count, slice_rows, block), f32),
            pltpu.VMEM((order, block), f32),
        ],
        4 * rows * block * (tile_rows * prow_count * width) + 6 * rows * block * order,
    )
    received = move(send, 0, 1, 0, 0)
    parts = call(
        add_kernel,
        [keep, received],
        0,
        [shape((rows_each, cols_each), f32)] * (2 * x_count),
        [],
        order * block,
    )
    column_pieces = [columns[0]] + [move(columns[d], 0, 0, d, 0) for d in range(1, z_count)]
    summed = [parts[0]] + [
        move(parts[2 * dx + dy], dx, 0, 0, dy)
        for dx in range(x_count)
        for dy in range(2)
        if dx + dy > 0
    ]
    window, ys = call(
        functools.partial(last_kernel, parts=len(summed), pieces=z_count),
        [place, *summed, own_window, *column_pieces],
        1,
        [
            shape((rows_each, cols_each), f32),
            shape((z_count, tile_rows, slice_rows, block), f32),
        ],
        [],
        order * block,
    )
    if block != width:
        ys = ys.reshape(supernodes, width // block, tile_rows, slice_rows, block)
        ys = jnp.transpose(ys, (0, 2, 3, 1, 4))
    return ys.reshape(supernodes, tile_rows, 1, slice_rows, width), window


def solution(mesh):
    placed = (
        P(None, "prow", None, None, "pcol", None),
        P(None, None, "prow", "pcol", None),
        P(),
        P(),
        P(),
    )
    return jax.shard_map(
        per_device,
        mesh=mesh,
        in_specs=placed,
        out_specs=(P(None, None, "prow", "pcol", None), P("prow", "pcol")),
        check_vma=False,
    )
```

time: 354 us -> 95.4 us (0.27)
  waiting for transfers between devices: 244 us -> 21.1 us
  blocking collectives: 24.6 us -> 0 us
  between operations: 15.1 us -> 1 us
  Pallas kernels: 0 us -> 13.7 us
  local copies, waits for them, and re-layouts: 18.3 us -> 6.67 us
  matrix products: 18.2 us -> 10.3 us
  starting transfers between devices: 19.2 us -> 26.7 us
    psum x1 -> x0, waiting for transfers between devices: 135 us -> none  [per_device(): window_sums = lax.psum(jnp.stack(window_parts), ('prow', 'pcol'))]
    unnamed x3 -> x0, waiting for transfers between devices: 91 us -> none
    ppermute x0 -> x21, starting transfers between devices: none -> 26.7 us  [move(): return lax.ppermute(value, AXES, pairs)]
    all_gather x4 -> x0, blocking collectives: 24.6 us -> none  [per_device(): stacked = lax.all_gather(own_piece[:, None], 'prow', axis=1, tiled=True)]
    ppermute x0 -> x21, waiting for transfers between devices: none -> 21.1 us  [move(): return lax.ppermute(value, AXES, pairs)]
    all_to_all x4 -> x0, starting transfers between devices: 19 us -> none  [per_device(): lax.all_to_all(spread, 'pcol', split_axis=1, concat_axis=2, tiled=True)]
    all_to_all x4 -> x0, waiting for transfers between devices: 18.2 us -> none  [per_device(): lax.all_to_all(spread, 'pcol', split_axis=1, concat_axis=2, tiled=True)]
    pallas_call x0 -> x4, Pallas kernels: none -> 13.7 us  [call(): pl.pallas_call(kernel, out_shape=outs, in_specs=[SMEM] * scalars + [VMEM]...]
  transfers between devices with their start and end apart: 6 -> 21, of which waited for: 5 -> 5; matrix products, arithmetic and copies ran while one was open for 4% -> 31% of each run, Pallas kernels for 0% -> 7%
where the time goes in v1:
time: 95.4 us; the launch traced here: 94.9 us
  starting transfers between devices  26.7 us (28%)
  waiting for transfers between devices  21.1 us (22%)
  other arithmetic  15.5 us (16%)
  Pallas kernels  13.7 us (14%)
  matrix products  10.3 us (11%)
  local copies, waits for them, and re-layouts  6.67 us (7%)
  between operations  1 us (1%)
    ppermute x21, starting transfers between devices, move(): return lax.ppermute(value, AXES, pairs)  26.7 us
    ppermute x21, waiting for transfers between devices, move(): return lax.ppermute(value, AXES, pairs)  21.1 us
    pallas_call x4, Pallas kernels, call(): pl.pallas_call(kernel, out_shape=outs, in_specs=[SMEM] * scalars + [VMEM]...  13.7 us
    concatenate x1, other arithmetic, per_device(): jnp.block([[jnp.eye(width, dtype=f32) if m == k else inverse[m, k] if m <...  9.83 us
    dot_general x5, matrix products, exact_dot(): jnp.dot(left, right, precision=HIGHEST, preferred_element_type=jnp.float32)  9.62 us
    unnamed x56, local copies, waits for them, and re-layouts  3.08 us
  transfers between devices with their start and end apart: 21, of which 5 were waited for; matrix products, arithmetic and copies ran while one was open for 31% of the time, Pallas kernels for 7%

profile of v1, /device:TPU:0, one launch (start us, length us, event | category | flops | bytes accessed | tf_op | source)
XLA Modules:
  0.0 94.9 jit_solution(18361367559611315392)
XLA Ops:
  0.6 0.0 copy-start
  0.6 0.0 copy-start.1
  0.7 3.1 %collective-permute-start = (bf16[4,2,32,256]{3,2,1,0:T(8,128)(2,1)}, bf16[4,2,32,256]{3,2,1,0:T(8,128)(2,1)}, u32[]{:S(2)}, u32[]{:S(2)}) collective-permute-start(bf16[4,2,32,256]{3,2,1,0:T(8,128)(2,1)} %bitcast.87), channel_id=1, source_target_pairs={{0,2},{1,3},{2,0},{3,1},{4,6},{5,7},{6,4},{7,5},{8,10},{9,11},{10,... | collective-permute-start | bytes 393224 | tf_op jit(solution)/shard_map/ppermute | solution.py:47
  3.7 2.6 %collective-permute-start.1 = (bf16[4,2,32,256]{3,2,1,0:T(8,128)(2,1)}, bf16[4,2,32,256]{3,2,1,0:T(8,128)(2,1)}, u32[]{:S(2)}, u32[]{:S(2)}) collective-permute-start(bf16[4,2,32,256]{3,2,1,0:T(8,128)(2,1)} %bitcast.88), channel_id=1, source_target_pairs={{0,4},{1,5},{2,6},{3,7},{4,0},{5,1},{6,2},{7,3},{8,12},{9,13},{10,... | collective-permute-start | bytes 393224 | tf_op jit(solution)/shard_map/ppermute | solution.py:47
  6.3 0.0 collective-permute-start.2
  6.3 1.6 %constant_dynamic-slice_fusion.1 = (bf16[2,4,1,32,256]{4,3,2,1,0:T(8,128)(2,1)S(1)}, bf16[2,4,32,256]{3,2,1,0:T(8,128)(2,1)}) fusion(bf16[2,4,2,32,256]{4,3,2,1,0:T(8,128)(2,1)} %bitcast.85, s32[]{:T(128)S(6)} %select_n.40, s32[]{:T(128)S(6)} %select_n.41), kind=kLoop, calls=%fused_computation.43 | loop fusion | bytes 524296 | tf_op jit(solution)/shard_map/jit(dynamic_index_in_dim)/dynamic_slice | solution.py:182
  8.0 1.7 %collective-permute-start.10 = (bf16[2,4,32,256]{3,2,1,0:T(8,128)(2,1)}, bf16[2,4,32,256]{3,2,1,0:T(8,128)(2,1)}, u32[]{:S(2)}, u32[]{:S(2)}) collective-permute-start(bf16[2,4,32,256]{3,2,1,0:T(8,128)(2,1)} %get-tuple-element.39), channel_id=1, source_target_pairs={{0,1},{1,0},{2,3},{3,2},{4,5},{5,4},{6,7},{7,6},{8,9},{9,8},{10,11... | collective-permute-start | bytes 393224 | tf_op jit(solution)/shard_map/ppermute | solution.py:47
  9.7 1.3 %convert_element_type.16 = f32[6,256,256]{2,1,0:T(8,128)S(1)} convert(bf16[6,256,256]{2,1,0:T(8,128)(2,1)} %param.8) | non-fusion elementwise | flops 393216 | bytes 2359296 | tf_op jit(solution)/shard_map/convert_element_type | solution.py:51
  11.0 0.7 fusion.7
  11.7 1.9 %convolution_add_fusion.2 = f32[256,256]{1,0:T(8,128)} fusion(f32[6,256,256]{2,1,0:T(8,128)S(1)} %convert_element_type.16, bf16[6,256,256]{2,1,0:T(8,128)(2,1)} %param.8), kind=kOutput, calls=%fused_computation.6 | convolution fusion | flops 201457664 | bytes 917504 | tf_op jit(solution)/shard_map/dot_general | solution.py:21
  13.6 1.0 %bitcast_dynamic-update-slice_fusion.2 = (f32[6,256,256]{2,1,0:T(8,128)}, f32[256,256]{1,0:T(8,128)S(1)}) fusion(f32[6,256,256]{2,1,0:T(8,128)} %fusion.7, bf16[6,256,256]{2,1,0:T(8,128)(2,1)S(1)} %copy-done.1, f32[6,256,256]{2,1,0:T(8,128)S(1)} %convert_element_type.16), kind=kOutput, calls=%fused_computation.23 | convolution fusion | flops 201523200 | bytes 1179648 | tf_op jit(solution)/shard_map/dot_general | solution.py:21
  14.6 0.9 fusion.8
  15.5 2.0 %bitcast_dynamic-update-slice_fusion.1 = (f32[6,256,256]{2,1,0:T(8,128)}, f32[256,256]{1,0:T(8,128)}) fusion(f32[6,256,256]{2,1,0:T(8,128)} %get-tuple-element.36, f32[256,256]{1,0:T(8,128)} %convolution_add_fusion.2, f32[256,256]{1,0:T(8,128)S(1)} %get-tuple-element.41, bf16[6,256,256]{2,1,0:T(8,128)(2,1)S(1)} %copy-done.1), kind=kOutput, calls=%fused_computation.22 | convolution fusion | flops 201457664 | bytes 1179648 | tf_op jit(solution)/shard_map/dot_general | solution.py:21
  17.5 1.1 %bitcast_dynamic-update-slice_fusion = (f32[6,256,256]{2,1,0:T(8,128)}, f32[256,256]{1,0:T(8,128)}) fusion(f32[6,256,256]{2,1,0:T(8,128)} %get-tuple-element.42, bf16[6,256,256]{2,1,0:T(8,128)(2,1)S(1)} %copy-done.1, f32[6,256,256]{2,1,0:T(8,128)S(1)} %convert_element_type.16), kind=kOutput, calls=%fused_computation.21 | convolution fusion | flops 201523200 | bytes 1179648 | tf_op jit(solution)/shard_map/dot_general | solution.py:21
  18.6 0.7 stack.56.place_ref
  19.3 0.7 fusion.12.refs_4_
  20.0 0.0 collective-permute-done.refs_1_
  20.0 0.0 collective-permute-done.1.refs_2_
  20.0 0.0 collective-permute-done.2.refs_3_
  20.0 4.3 %shard_map.68 = (bf16[4,256,256]{2,1,0:T(8,128)(2,1)}, bf16[4,256,256]{2,1,0:T(8,128)(2,1)}) custom-call(s32[5]{0:T(128)} %stack.56.place_ref, s32[4,8]{1,0:T(4,128)} %flags_ref.3, bf16[4,2,32,256]{3,2,1,0:T(8,128)(2,1)} %bitcast.90, bf16[4,2,32,256]{3,2,1,0:T(8,128)(2,1)} %collective-permute-done.refs_1_, ...), custom_call_target="tpu_custom_call" | custom-call | flops 1610612736 | bytes 1048576 | tf_op jit(solution)/shard_map/pallas_call | solution.py:153
  24.3 1.1 %fusion.5 = bf16[2,1,256,256]{3,2,1,0:T(8,128)(2,1)S(1)} fusion(s32[]{:T(128)S(6)} %select_n.39, bf16[1,4,256,256]{3,2,1,0:T(8,128)(2,1)} %bitcast.77, bf16[1,4,256,256]{3,2,1,0:T(8,128)(2,1)} %bitcast.78), kind=kLoop, calls=%fused_computation.13 | loop fusion | flops 131072 | bytes 1310724 | tf_op jit(solution)/shard_map/stack | solution.py:227
  25.4 0.4 collective-permute-start.3
  25.7 1.7 %collective-permute-start.4 = (bf16[2,2,4,32,256]{4,3,2,1,0:T(8,128)(2,1)S(1)}, bf16[2,2,4,32,256]{4,3,2,1,0:T(8,128)(2,1)S(1)}, u32[]{:S(2)}, u32[]{:S(2)}) collective-permute-start(bf16[2,2,4,32,256]{4,3,2,1,0:T(8,128)(2,1)S(1)} %bitcast.80), channel_id=1, source_target_pairs={{0,16},{1,17},{2,18},{3,19},{4,20},{5,21},{6,22},{7,23},{8,24},{9,... | collective-permute-start | bytes 786440 | tf_op jit(solution)/shard_map/ppermute | solution.py:47
  27.5 1.5 %collective-permute-start.5 = (bf16[2,2,4,32,256]{4,3,2,1,0:T(8,128)(2,1)S(1)}, bf16[2,2,4,32,256]{4,3,2,1,0:T(8,128)(2,1)S(1)}, u32[]{:S(2)}, u32[]{:S(2)}) collective-permute-start(bf16[2,2,4,32,256]{4,3,2,1,0:T(8,128)(2,1)S(1)} %bitcast.81), channel_id=1, source_target_pairs={{0,17},{1,16},{2,19},{3,18},{4,21},{5,20},{6,23},{7,22},{8,25},{9,... | collective-permute-start | bytes 786440 | tf_op jit(solution)/shard_map/ppermute | solution.py:47
  28.9 0.0 collective-permute-start.6
  29.0 0.9 pad_maximum_fusion.refs_8_
  29.9 0.7 collective-permute-start.11
  30.6 3.2 %collective-permute-done.3.refs_1_ = bf16[2,2,4,32,256]{4,3,2,1,0:T(8,128)(2,1)S(1)} collective-permute-done((bf16[2,2,4,32,256]{4,3,2,1,0:T(8,128)(2,1)S(1)}, bf16[2,2,4,32,256]{4,3,2,1,0:T(8,128)(2,1)S(1)}, u32[]{:S(2)}, u32[]{:S(2)}) %collective-permute-start.3) | collective-permute-done | bytes 262176 | tf_op jit(solution)/shard_map/ppermute | solution.py:47
  33.8 1.7 %collective-permute-start.12 = (bf16[2,256,256]{2,1,0:T(8,128)(2,1)S(1)}, bf16[2,256,256]{2,1,0:T(8,128)(2,1)S(1)}, u32[]{:S(2)}, u32[]{:S(2)}) collective-permute-start(bf16[2,256,256]{2,1,0:T(8,128)(2,1)S(1)} %pad_maximum_fusion.refs_8_), channel_id=1, source_target_pairs={{0,4},{1,5},{2,6},{3,7},{4,0},{5,1},{6,2},{7,3},{8,12},{9,13},{10,... | collective-permute-start | bytes 786440 | tf_op jit(solution)/shard_map/ppermute | solution.py:47
  35.5 3.3 %collective-permute-start.13 = (bf16[2,256,256]{2,1,0:T(8,128)(2,1)S(1)}, bf16[2,256,256]{2,1,0:T(8,128)(2,1)S(1)}, u32[]{:S(2)}, u32[]{:S(2)}) collective-permute-start(bf16[2,256,256]{2,1,0:T(8,128)(2,1)S(1)} %pad_maximum_fusion.refs_8_), channel_id=1, source_target_pairs={{0,6},{1,7},{2,4},{3,5},{4,2},{5,3},{6,0},{7,1},{8,14},{9,15},{10,... | collective-permute-start | bytes 786440 | tf_op jit(solution)/shard_map/ppermute | solution.py:47
  38.8 0.4 collective-permute-done.5.refs_3_
  39.3 0.5 collective-permute-start.8
  39.8 2.9 %collective-permute-done.11.refs_9_ = bf16[2,256,256]{2,1,0:T(8,128)(2,1)S(1)} collective-permute-done((bf16[2,256,256]{2,1,0:T(8,128)(2,1)S(1)}, bf16[2,256,256]{2,1,0:T(8,128)(2,1)S(1)}, u32[]{:S(2)}, u32[]{:S(2)}) %collective-permute-start.11) | collective-permute-done | bytes 262176 | tf_op jit(solution)/shard_map/ppermute | solution.py:47
  42.6 0.0 collective-permute-start.9
  42.7 12.2 %collective-permute-done.12.refs_10_ = bf16[2,256,256]{2,1,0:T(8,128)(2,1)S(1)} collective-permute-done((bf16[2,256,256]{2,1,0:T(8,128)(2,1)S(1)}, bf16[2,256,256]{2,1,0:T(8,128)(2,1)S(1)}, u32[]{:S(2)}, u32[]{:S(2)}) %collective-permute-start.12) | collective-permute-done | bytes 262176 | tf_op jit(solution)/shard_map/ppermute | solution.py:47
  54.9 0.0 collective-permute-done.13.refs_11_
  54.9 0.0 collective-permute-done.7.refs_5_
  54.9 0.0 collective-permute-done.8.refs_6_
  55.0 0.0 collective-permute-done.9.refs_7_
  55.0 0.6 copy-done.14
  55.6 0.1 copy-done.15
  55.7 0.1 copy-done.16
  55.8 0.1 copy-done.17
  55.9 0.7 copy-done.18
  56.6 5.4 %shard_map.69 = (f32[2,32,256]{2,1,0:T(8,128)}, f32[2,32,256]{2,1,0:T(8,128)}, f32[2,32,256]{2,1,0:T(8,128)}, f32[2,32,256]{2,1,0:T(8,128)}, f32[2,2,256,128]{3,2,1,0:T(8,128)}, /*index=5*/f32[2,2,256,128]{3,2,1,0:T(8,128)}) custom-call(s32[5]{0:T(128)} %stack.56.place_ref, s32[4,8]{1,0:T(4,128)} %flags_ref.3, bf16[2,2,4,32,256]{4,3,2,1,0:T(8,128)(2,1)} %bitcast.83, ...), custom_call_target="tpu_custom_call" | custom-call | flops 939524096 | bytes 1048576 | tf_op jit(solution)/shard_map/pallas_call | solution.py:153
  62.0 0.1 collective-permute-start.14
  62.1 9.8 %maximum_maximum_fusion = f32[1024,1024]{1,0:T(8,128)} fusion(f32[256,256]{1,0:T(8,128)S(1)} %fusion.6, f32[256,256]{1,0:T(8,128)S(1)} %broadcast.7, f32[256,256]{1,0:T(8,128)S(1)} %copy-done.2, f32[256,256]{1,0:T(8,128)S(1)} %copy-done.4, f32[256,256]{1,0:T(8,128)S(1)} %copy-done.3, f32[256,256]{1,0:T(8,128)S(1)} %copy-done.7, ...), kind=kLoop, calls=%fused_computation | loop fusion | flops 15728640 | bytes 6291456 | tf_op jit(solution)/shard_map/jit(block)/concatenate | solution.py:189
  72.0 1.1 %constant_dynamic-slice_fusion = f32[1024,128]{1,0:T(8,128)S(1)} fusion(f32[1024,1024]{1,0:T(8,128)} %maximum_maximum_fusion, s32[]{:T(128)S(6)} %select_n.43), kind=kLoop, calls=%fused_computation.41 | loop fusion | bytes 1048580 | tf_op jit(solution)/shard_map/dynamic_slice | solution.py:203
  73.1 3.4 %collective-permute-start.18 = (f32[2,32,256]{2,1,0:T(8,128)S(1)}, f32[2,32,256]{2,1,0:T(8,128)S(1)}, u32[]{:S(2)}, u32[]{:S(2)}) collective-permute-start(f32[2,32,256]{2,1,0:T(8,128)S(1)} %copy-done.27), channel_id=1, source_target_pairs={{0,2},{1,3},{2,0},{3,1},{4,6},{5,7},{6,4},{7,5},{8,10},{9,11},{10,... | collective-permute-start | bytes 196616 | tf_op jit(solution)/shard_map/ppermute | solution.py:47
  76.4 0.7 convolution_bitcast_fusion
  77.1 0.2 copy.19
  77.3 1.1 %collective-permute-start.19 = (f32[2,32,256]{2,1,0:T(8,128)S(1)}, f32[2,32,256]{2,1,0:T(8,128)S(1)}, u32[]{:S(2)}, u32[]{:S(2)}) collective-permute-start(f32[2,32,256]{2,1,0:T(8,128)S(1)} %copy-done.26), channel_id=1, source_target_pairs={{0,4},{1,5},{2,6},{3,7},{4,0},{5,1},{6,2},{7,3},{8,12},{9,13},{10,... | collective-permute-start | bytes 196616 | tf_op jit(solution)/shard_map/ppermute | solution.py:47
  78.4 1.5 %collective-permute-start.20 = (f32[2,32,256]{2,1,0:T(8,128)S(1)}, f32[2,32,256]{2,1,0:T(8,128)S(1)}, u32[]{:S(2)}, u32[]{:S(2)}) collective-permute-start(f32[2,32,256]{2,1,0:T(8,128)S(1)} %copy-done.25), channel_id=1, source_target_pairs={{0,6},{1,7},{2,4},{3,5},{4,2},{5,3},{6,0},{7,1},{8,14},{9,15},{10,... | collective-permute-start | bytes 196616 | tf_op jit(solution)/shard_map/ppermute | solution.py:47
  79.9 0.8 copy-done.8
  80.7 2.0 %shard_map.70 = (f32[256,128]{1,0:T(8,128)}, f32[256,128]{1,0:T(8,128)}, f32[256,128]{1,0:T(8,128)}, f32[256,128]{1,0:T(8,128)}) custom-call(f32[2,2,256,128]{3,2,1,0:T(8,128)} %get-tuple-element.18.keep_ref, f32[2,2,256,128]{3,2,1,0:T(8,128)} %copy-done.8), custom_call_target="tpu_custom_call" | custom-call | flops 262144 | bytes 1048576 | tf_op jit(solution)/shard_map/pallas_call | solution.py:153
  82.7 0.5 collective-permute-start.15
  83.2 1.5 %collective-permute-start.16 = (f32[256,128]{1,0:T(8,128)}, f32[256,128]{1,0:T(8,128)S(1)}, u32[]{:S(2)}, u32[]{:S(2)}) collective-permute-start(f32[256,128]{1,0:T(8,128)} %get-tuple-element.22), channel_id=1, source_target_pairs={{0,16},{1,17},{2,18},{3,19},{4,20},{5,21},{6,22},{7,23},{8,24},{9,... | collective-permute-start | bytes 393224 | tf_op jit(solution)/shard_map/ppermute | solution.py:47
  84.7 0.0 collective-permute-done.18.refs_6_
  84.7 1.5 %collective-permute-start.17 = (f32[256,128]{1,0:T(8,128)}, f32[256,128]{1,0:T(8,128)S(1)}, u32[]{:S(2)}, u32[]{:S(2)}) collective-permute-start(f32[256,128]{1,0:T(8,128)} %get-tuple-element.23), channel_id=1, source_target_pairs={{0,17},{1,16},{2,19},{3,18},{4,21},{5,20},{6,23},{7,22},{8,25},{9,... | collective-permute-start | bytes 393224 | tf_op jit(solution)/shard_map/ppermute | solution.py:47
  86.2 3.7 %fusion.3.refs_4_ = f32[256,128]{1,0:T(8,128)} fusion(f32[1024,128]{1,0:T(8,128)S(1)} %bitcast.76, f32[1024,1024]{1,0:T(8,128)} %maximum_maximum_fusion, s32[]{:T(128)S(6)} %select_n.42), kind=kOutput, calls=%fused_computation.11 | convolution fusion | flops 402653184 | bytes 1703940 | tf_op jit(solution)/shard_map/dot_general | solution.py:21
  89.9 0.0 collective-permute-done.15.refs_1_
  89.9 2.3 %collective-permute-done.17.refs_3_ = f32[256,128]{1,0:T(8,128)S(1)} collective-permute-done((f32[256,128]{1,0:T(8,128)}, f32[256,128]{1,0:T(8,128)S(1)}, u32[]{:S(2)}, u32[]{:S(2)}) %collective-permute-start.17) | collective-permute-done | bytes 131104 | tf_op jit(solution)/shard_map/ppermute | solution.py:47
  92.3 0.6 copy-done.21
  92.9 2.0 %shard_map.71 = (f32[256,128]{1,0:T(8,128)}, f32[4,2,32,256]{3,2,1,0:T(8,128)}) custom-call(s32[5]{0:T(128)} %stack.56.place_ref, f32[256,128]{1,0:T(8,128)} %get-tuple-element.20.refs_0_, f32[256,128]{1,0:T(8,128)} %copy-done.19, f32[256,128]{1,0:T(8,128)} %copy-done.20, f32[256,128]{1,0:T(8,128)} %copy-done.21, f32[256,128]{1,0:T(8,128)} %fusion.3.refs_4_, ...), custom_call_target="tpu_custom_call" | custom-call | flops 262144 | bytes 1048576 | tf_op jit(solution)/shard_map/pallas_call | solution.py:153
  (57 shorter events, 0.1 us)
Async XLA Ops:
  0.6 75.8 %copy-start = (bf16[4,256,256]{2,1,0:T(8,128)(2,1)S(1)}, bf16[4,256,256]{2,1,0:T(8,128)(2,1)}, u32[]{:S(2)}) copy-start(bf16[4,256,256]{2,1,0:T(8,128)(2,1)} %param.9) | copy-start | bytes 1572868
  0.6 13.0 %copy-start.1 = (bf16[6,256,256]{2,1,0:T(8,128)(2,1)S(1)}, bf16[6,256,256]{2,1,0:T(8,128)(2,1)}, u32[]{:S(2)}) copy-start(bf16[6,256,256]{2,1,0:T(8,128)(2,1)} %param.8) | copy-start | bytes 2359300
  0.7 19.3 %collective-permute-start = (bf16[4,2,32,256]{3,2,1,0:T(8,128)(2,1)}, bf16[4,2,32,256]{3,2,1,0:T(8,128)(2,1)}, u32[]{:S(2)}, u32[]{:S(2)}) collective-permute-start(bf16[4,2,32,256]{3,2,1,0:T(8,128)(2,1)} %bitcast.87), channel_id=1, source_target_pairs={{0,2},{1,3},{2,0},{3,1},{4,6},{5,7},{6,4},{7,5},{8,10},{9,11},{10,... | collective-permute-start | bytes 393224 | tf_op jit(solution)/shard_map/ppermute | solution.py:47
  3.7 16.2 %collective-permute-start.1 = (bf16[4,2,32,256]{3,2,1,0:T(8,128)(2,1)}, bf16[4,2,32,256]{3,2,1,0:T(8,128)(2,1)}, u32[]{:S(2)}, u32[]{:S(2)}) collective-permute-start(bf16[4,2,32,256]{3,2,1,0:T(8,128)(2,1)} %bitcast.88), channel_id=1, source_target_pairs={{0,4},{1,5},{2,6},{3,7},{4,0},{5,1},{6,2},{7,3},{8,12},{9,13},{10,... | collective-permute-start | bytes 393224 | tf_op jit(solution)/shard_map/ppermute | solution.py:47
  6.3 13.6 %collective-permute-start.2 = (bf16[4,2,32,256]{3,2,1,0:T(8,128)(2,1)}, bf16[4,2,32,256]{3,2,1,0:T(8,128)(2,1)}, u32[]{:S(2)}, u32[]{:S(2)}) collective-permute-start(bf16[4,2,32,256]{3,2,1,0:T(8,128)(2,1)} %bitcast.89), channel_id=1, source_target_pairs={{0,6},{1,7},{2,4},{3,5},{4,2},{5,3},{6,0},{7,1},{8,14},{9,15},{10,... | collective-permute-start | bytes 393224 | tf_op jit(solution)/shard_map/ppermute | solution.py:47
  8.0 21.0 %collective-permute-start.10 = (bf16[2,4,32,256]{3,2,1,0:T(8,128)(2,1)}, bf16[2,4,32,256]{3,2,1,0:T(8,128)(2,1)}, u32[]{:S(2)}, u32[]{:S(2)}) collective-permute-start(bf16[2,4,32,256]{3,2,1,0:T(8,128)(2,1)} %get-tuple-element.39), channel_id=1, source_target_pairs={{0,1},{1,0},{2,3},{3,2},{4,5},{5,4},{6,7},{7,6},{8,9},{9,8},{10,11... | collective-permute-start | bytes 393224 | tf_op jit(solution)/shard_map/ppermute | solution.py:47
  24.3 37.8 %copy-start.2 = (f32[256,256]{1,0:T(8,128)S(1)}, f32[256,256]{1,0:T(8,128)}, u32[]{:S(2)}) copy-start(f32[256,256]{1,0:T(8,128)} %get-tuple-element.35) | copy-start | bytes 786436
  24.3 37.8 %copy-start.3 = (f32[256,256]{1,0:T(8,128)S(1)}, f32[256,256]{1,0:T(8,128)}, u32[]{:S(2)}) copy-start(f32[256,256]{1,0:T(8,128)} %get-tuple-element.37) | copy-start | bytes 786436
  24.3 37.8 %copy-start.4 = (f32[256,256]{1,0:T(8,128)S(1)}, f32[256,256]{1,0:T(8,128)}, u32[]{:S(2)}) copy-start(f32[256,256]{1,0:T(8,128)} %get-tuple-element.45) | copy-start | bytes 786436
  24.3 37.8 %copy-start.7 = (f32[256,256]{1,0:T(8,128)S(1)}, f32[256,256]{1,0:T(8,128)}, u32[]{:S(2)}) copy-start(f32[256,256]{1,0:T(8,128)} %get-tuple-element.43) | copy-start | bytes 786436
  25.4 29.6 %copy-start.5 = (bf16[2,1,256,256]{3,2,1,0:T(8,128)(2,1)}, bf16[2,1,256,256]{3,2,1,0:T(8,128)(2,1)S(1)}, u32[]{:S(2)}) copy-start(bf16[2,1,256,256]{3,2,1,0:T(8,128)(2,1)S(1)} %fusion.5) | copy-start | bytes 786436
  25.4 8.4 %collective-permute-start.3 = (bf16[2,2,4,32,256]{4,3,2,1,0:T(8,128)(2,1)S(1)}, bf16[2,2,4,32,256]{4,3,2,1,0:T(8,128)(2,1)S(1)}, u32[]{:S(2)}, u32[]{:S(2)}) collective-permute-start(bf16[2,2,4,32,256]{4,3,2,1,0:T(8,128)(2,1)S(1)} %bitcast.79), channel_id=1, source_target_pairs={{0,1},{1,0},{2,3},{3,2},{4,5},{5,4},{6,7},{7,6},{8,9},{9,8},{10,11... | collective-permute-start | bytes 786440 | tf_op jit(solution)/shard_map/ppermute | solution.py:47
  25.7 9.7 %collective-permute-start.4 = (bf16[2,2,4,32,256]{4,3,2,1,0:T(8,128)(2,1)S(1)}, bf16[2,2,4,32,256]{4,3,2,1,0:T(8,128)(2,1)S(1)}, u32[]{:S(2)}, u32[]{:S(2)}) collective-permute-start(bf16[2,2,4,32,256]{4,3,2,1,0:T(8,128)(2,1)S(1)} %bitcast.80), channel_id=1, source_target_pairs={{0,16},{1,17},{2,18},{3,19},{4,20},{5,21},{6,22},{7,23},{8,24},{9,... | collective-permute-start | bytes 786440 | tf_op jit(solution)/shard_map/ppermute | solution.py:47
  27.5 11.8 %collective-permute-start.5 = (bf16[2,2,4,32,256]{4,3,2,1,0:T(8,128)(2,1)S(1)}, bf16[2,2,4,32,256]{4,3,2,1,0:T(8,128)(2,1)S(1)}, u32[]{:S(2)}, u32[]{:S(2)}) collective-permute-start(bf16[2,2,4,32,256]{4,3,2,1,0:T(8,128)(2,1)S(1)} %bitcast.81), channel_id=1, source_target_pairs={{0,17},{1,16},{2,19},{3,18},{4,21},{5,20},{6,23},{7,22},{8,25},{9,... | collective-permute-start | bytes 786440 | tf_op jit(solution)/shard_map/ppermute | solution.py:47
  28.9 10.3 %collective-permute-start.6 = (bf16[2,2,4,32,256]{4,3,2,1,0:T(8,128)(2,1)S(1)}, bf16[2,2,4,32,256]{4,3,2,1,0:T(8,128)(2,1)S(1)}, u32[]{:S(2)}, u32[]{:S(2)}) collective-permute-start(bf16[2,2,4,32,256]{4,3,2,1,0:T(8,128)(2,1)S(1)} %bitcast.82), channel_id=1, source_target_pairs={{0,8},{1,9},{2,10},{3,11},{4,12},{5,13},{6,14},{7,15},{8,0},{9,1},... | collective-permute-start | bytes 786440 | tf_op jit(solution)/shard_map/ppermute | solution.py:47
  29.9 25.1 %copy-start.6 = (bf16[2,256,256]{2,1,0:T(8,128)(2,1)}, bf16[2,256,256]{2,1,0:T(8,128)(2,1)S(1)}, u32[]{:S(2)}) copy-start(bf16[2,256,256]{2,1,0:T(8,128)(2,1)S(1)} %pad_maximum_fusion.refs_8_) | copy-start | bytes 786436
  29.9 12.7 %collective-permute-start.11 = (bf16[2,256,256]{2,1,0:T(8,128)(2,1)S(1)}, bf16[2,256,256]{2,1,0:T(8,128)(2,1)S(1)}, u32[]{:S(2)}, u32[]{:S(2)}) collective-permute-start(bf16[2,256,256]{2,1,0:T(8,128)(2,1)S(1)} %pad_maximum_fusion.refs_8_), channel_id=1, source_target_pairs={{0,2},{1,3},{2,0},{3,1},{4,6},{5,7},{6,4},{7,5},{8,10},{9,11},{10,... | collective-permute-start | bytes 786440 | tf_op jit(solution)/shard_map/ppermute | solution.py:47
  33.8 21.2 %copy-start.9 = (bf16[2,2,4,32,256]{4,3,2,1,0:T(8,128)(2,1)}, bf16[2,2,4,32,256]{4,3,2,1,0:T(8,128)(2,1)S(1)}, u32[]{:S(2)}) copy-start(bf16[2,2,4,32,256]{4,3,2,1,0:T(8,128)(2,1)S(1)} %collective-permute-done.3.refs_1_) | copy-start | bytes 786436
  33.8 21.1 %collective-permute-start.12 = (bf16[2,256,256]{2,1,0:T(8,128)(2,1)S(1)}, bf16[2,256,256]{2,1,0:T(8,128)(2,1)S(1)}, u32[]{:S(2)}, u32[]{:S(2)}) collective-permute-start(bf16[2,256,256]{2,1,0:T(8,128)(2,1)S(1)} %pad_maximum_fusion.refs_8_), channel_id=1, source_target_pairs={{0,4},{1,5},{2,6},{3,7},{4,0},{5,1},{6,2},{7,3},{8,12},{9,13},{10,... | collective-permute-start | bytes 786440 | tf_op jit(solution)/shard_map/ppermute | solution.py:47
  35.5 19.5 %copy-start.10 = (bf16[2,2,4,32,256]{4,3,2,1,0:T(8,128)(2,1)}, bf16[2,2,4,32,256]{4,3,2,1,0:T(8,128)(2,1)S(1)}, u32[]{:S(2)}) copy-start(bf16[2,2,4,32,256]{4,3,2,1,0:T(8,128)(2,1)S(1)} %collective-permute-done.4.refs_2_) | copy-start | bytes 786436
  35.5 19.4 %collective-permute-start.13 = (bf16[2,256,256]{2,1,0:T(8,128)(2,1)S(1)}, bf16[2,256,256]{2,1,0:T(8,128)(2,1)S(1)}, u32[]{:S(2)}, u32[]{:S(2)}) collective-permute-start(bf16[2,256,256]{2,1,0:T(8,128)(2,1)S(1)} %pad_maximum_fusion.refs_8_), channel_id=1, source_target_pairs={{0,6},{1,7},{2,4},{3,5},{4,2},{5,3},{6,0},{7,1},{8,14},{9,15},{10,... | collective-permute-start | bytes 786440 | tf_op jit(solution)/shard_map/ppermute | solution.py:47
  39.2 15.8 %copy-start.11 = (bf16[2,2,4,32,256]{4,3,2,1,0:T(8,128)(2,1)}, bf16[2,2,4,32,256]{4,3,2,1,0:T(8,128)(2,1)S(1)}, u32[]{:S(2)}) copy-start(bf16[2,2,4,32,256]{4,3,2,1,0:T(8,128)(2,1)S(1)} %collective-permute-done.5.refs_3_) | copy-start | bytes 786436
  39.2 15.7 %collective-permute-start.7 = (bf16[2,2,4,32,256]{4,3,2,1,0:T(8,128)(2,1)S(1)}, bf16[2,2,4,32,256]{4,3,2,1,0:T(8,128)(2,1)S(1)}, u32[]{:S(2)}, u32[]{:S(2)}) collective-permute-start(bf16[2,2,4,32,256]{4,3,2,1,0:T(8,128)(2,1)S(1)} %collective-permute-done.3.refs_1_), channel_id=1, source_target_pairs={{0,8},{1,9},{2,10},{3,11},{4,12},{5,13},{6,14},{7,15},{8,0},{9,1},... | collective-permute-start | bytes 786440 | tf_op jit(solution)/shard_map/ppermute | solution.py:47
  39.3 15.8 %copy-start.12 = (bf16[2,2,4,32,256]{4,3,2,1,0:T(8,128)(2,1)}, bf16[2,2,4,32,256]{4,3,2,1,0:T(8,128)(2,1)S(1)}, u32[]{:S(2)}) copy-start(bf16[2,2,4,32,256]{4,3,2,1,0:T(8,128)(2,1)S(1)} %collective-permute-done.6.refs_4_) | copy-start | bytes 786436
  39.3 15.7 %collective-permute-start.8 = (bf16[2,2,4,32,256]{4,3,2,1,0:T(8,128)(2,1)S(1)}, bf16[2,2,4,32,256]{4,3,2,1,0:T(8,128)(2,1)S(1)}, u32[]{:S(2)}, u32[]{:S(2)}) collective-permute-start(bf16[2,2,4,32,256]{4,3,2,1,0:T(8,128)(2,1)S(1)} %collective-permute-done.4.refs_2_), channel_id=1, source_target_pairs={{0,8},{1,9},{2,10},{3,11},{4,12},{5,13},{6,14},{7,15},{8,0},{9,1},... | collective-permute-start | bytes 786440 | tf_op jit(solution)/shard_map/ppermute | solution.py:47
  42.6 12.4 %copy-start.13 = (bf16[2,256,256]{2,1,0:T(8,128)(2,1)}, bf16[2,256,256]{2,1,0:T(8,128)(2,1)S(1)}, u32[]{:S(2)}) copy-start(bf16[2,256,256]{2,1,0:T(8,128)(2,1)S(1)} %collective-permute-done.11.refs_9_) | copy-start | bytes 786436
  42.6 12.3 %collective-permute-start.9 = (bf16[2,2,4,32,256]{4,3,2,1,0:T(8,128)(2,1)S(1)}, bf16[2,2,4,32,256]{4,3,2,1,0:T(8,128)(2,1)S(1)}, u32[]{:S(2)}, u32[]{:S(2)}) collective-permute-start(bf16[2,2,4,32,256]{4,3,2,1,0:T(8,128)(2,1)S(1)} %collective-permute-done.5.refs_3_), channel_id=1, source_target_pairs={{0,8},{1,9},{2,10},{3,11},{4,12},{5,13},{6,14},{7,15},{8,0},{9,1},... | collective-permute-start | bytes 786440 | tf_op jit(solution)/shard_map/ppermute | solution.py:47
  54.9 0.7 copy-start.14
  54.9 0.8 copy-start.15
  54.9 0.9 copy-start.16
  55.0 0.9 copy-start.17
  55.9 0.7 copy-start.18
  62.0 11.1 %copy-start.27 = (f32[2,32,256]{2,1,0:T(8,128)S(1)}, f32[2,32,256]{2,1,0:T(8,128)}, u32[]{:S(2)}) copy-start(f32[2,32,256]{2,1,0:T(8,128)} %get-tuple-element.25) | copy-start | bytes 196612
  62.0 18.0 %collective-permute-start.14 = (f32[2,2,256,128]{3,2,1,0:T(8,128)}, f32[2,2,256,128]{3,2,1,0:T(8,128)S(1)}, u32[]{:S(2)}, u32[]{:S(2)}) collective-permute-start(f32[2,2,256,128]{3,2,1,0:T(8,128)} %get-tuple-element.19), channel_id=1, source_target_pairs={{0,8},{1,9},{2,10},{3,11},{4,12},{5,13},{6,14},{7,15},{8,0},{9,1},... | collective-permute-start | bytes 1572872 | tf_op jit(solution)/shard_map/ppermute | solution.py:47
  62.1 15.2 %copy-start.26 = (f32[2,32,256]{2,1,0:T(8,128)S(1)}, f32[2,32,256]{2,1,0:T(8,128)}, u32[]{:S(2)}) copy-start(f32[2,32,256]{2,1,0:T(8,128)} %get-tuple-element.26) | copy-start | bytes 196612
  62.1 16.3 %copy-start.25 = (f32[2,32,256]{2,1,0:T(8,128)S(1)}, f32[2,32,256]{2,1,0:T(8,128)}, u32[]{:S(2)}) copy-start(f32[2,32,256]{2,1,0:T(8,128)} %get-tuple-element.27) | copy-start | bytes 196612
  73.1 11.7 %collective-permute-start.18 = (f32[2,32,256]{2,1,0:T(8,128)S(1)}, f32[2,32,256]{2,1,0:T(8,128)S(1)}, u32[]{:S(2)}, u32[]{:S(2)}) collective-permute-start(f32[2,32,256]{2,1,0:T(8,128)S(1)} %copy-done.27), channel_id=1, source_target_pairs={{0,2},{1,3},{2,0},{3,1},{4,6},{5,7},{6,4},{7,5},{8,10},{9,11},{10,... | collective-permute-start | bytes 196616 | tf_op jit(solution)/shard_map/ppermute | solution.py:47
  77.3 12.6 %collective-permute-start.19 = (f32[2,32,256]{2,1,0:T(8,128)S(1)}, f32[2,32,256]{2,1,0:T(8,128)S(1)}, u32[]{:S(2)}, u32[]{:S(2)}) collective-permute-start(f32[2,32,256]{2,1,0:T(8,128)S(1)} %copy-done.26), channel_id=1, source_target_pairs={{0,4},{1,5},{2,6},{3,7},{4,0},{5,1},{6,2},{7,3},{8,12},{9,13},{10,... | collective-permute-start | bytes 196616 | tf_op jit(solution)/shard_map/ppermute | solution.py:47
  78.4 11.5 %collective-permute-start.20 = (f32[2,32,256]{2,1,0:T(8,128)S(1)}, f32[2,32,256]{2,1,0:T(8,128)S(1)}, u32[]{:S(2)}, u32[]{:S(2)}) collective-permute-start(f32[2,32,256]{2,1,0:T(8,128)S(1)} %copy-done.25), channel_id=1, source_target_pairs={{0,6},{1,7},{2,4},{3,5},{4,2},{5,3},{6,0},{7,1},{8,14},{9,15},{10,... | collective-permute-start | bytes 196616 | tf_op jit(solution)/shard_map/ppermute | solution.py:47
  79.9 0.8 copy-start.8
  82.7 7.2 %collective-permute-start.15 = (f32[256,128]{1,0:T(8,128)}, f32[256,128]{1,0:T(8,128)S(1)}, u32[]{:S(2)}, u32[]{:S(2)}) collective-permute-start(f32[256,128]{1,0:T(8,128)} %get-tuple-element.21), channel_id=1, source_target_pairs={{0,1},{1,0},{2,3},{3,2},{4,5},{5,4},{6,7},{7,6},{8,9},{9,8},{10,11... | collective-permute-start | bytes 393224 | tf_op jit(solution)/shard_map/ppermute | solution.py:47
  83.2 6.7 %collective-permute-start.16 = (f32[256,128]{1,0:T(8,128)}, f32[256,128]{1,0:T(8,128)S(1)}, u32[]{:S(2)}, u32[]{:S(2)}) collective-permute-start(f32[256,128]{1,0:T(8,128)} %get-tuple-element.22), channel_id=1, source_target_pairs={{0,16},{1,17},{2,18},{3,19},{4,20},{5,21},{6,22},{7,23},{8,24},{9,... | collective-permute-start | bytes 393224 | tf_op jit(solution)/shard_map/ppermute | solution.py:47
  84.7 7.5 %copy-start.22 = (f32[2,32,256]{2,1,0:T(8,128)}, f32[2,32,256]{2,1,0:T(8,128)S(1)}, u32[]{:S(2)}) copy-start(f32[2,32,256]{2,1,0:T(8,128)S(1)} %collective-permute-done.18.refs_6_) | copy-start | bytes 196612
  84.7 7.5 %collective-permute-start.17 = (f32[256,128]{1,0:T(8,128)}, f32[256,128]{1,0:T(8,128)S(1)}, u32[]{:S(2)}, u32[]{:S(2)}) collective-permute-start(f32[256,128]{1,0:T(8,128)} %get-tuple-element.23), channel_id=1, source_target_pairs={{0,17},{1,16},{2,19},{3,18},{4,21},{5,20},{6,23},{7,22},{8,25},{9,... | collective-permute-start | bytes 393224 | tf_op jit(solution)/shard_map/ppermute | solution.py:47
  89.9 2.4 %copy-start.23 = (f32[2,32,256]{2,1,0:T(8,128)}, f32[2,32,256]{2,1,0:T(8,128)S(1)}, u32[]{:S(2)}) copy-start(f32[2,32,256]{2,1,0:T(8,128)S(1)} %collective-permute-done.19.refs_7_) | copy-start | bytes 196612
  89.9 2.4 %copy-start.24 = (f32[2,32,256]{2,1,0:T(8,128)}, f32[2,32,256]{2,1,0:T(8,128)S(1)}, u32[]{:S(2)}) copy-start(f32[2,32,256]{2,1,0:T(8,128)S(1)} %collective-permute-done.20.refs_8_) | copy-start | bytes 196612
  89.9 2.4 %copy-start.19 = (f32[256,128]{1,0:T(8,128)}, f32[256,128]{1,0:T(8,128)S(1)}, u32[]{:S(2)}) copy-start(f32[256,128]{1,0:T(8,128)S(1)} %collective-permute-done.15.refs_1_) | copy-start | bytes 393220
  89.9 2.3 %copy-start.20 = (f32[256,128]{1,0:T(8,128)}, f32[256,128]{1,0:T(8,128)S(1)}, u32[]{:S(2)}) copy-start(f32[256,128]{1,0:T(8,128)S(1)} %collective-permute-done.16.refs_2_) | copy-start | bytes 393220
  92.3 0.7 copy-start.21

commit v2 on v1

--- a/solution.py
+++ b/solution.py
@@ -47,23 +47,59 @@
     return lax.ppermute(value, AXES, pairs)
 
 
-def inverse_blocks(window_factor, supernodes):
-    factor = window_factor.astype(jnp.float32)
-    blocks = {}
+def exact_dot_rows(left, right):
+    return lax.dot_general(
+        left,
+        right,
+        (((0,), (0,)), ((), ())),
+        precision=HIGHEST,
+        preferred_element_type=jnp.float32,
+    )
+
+
+def inverse_kernel(place_ref, factor_ref, diag_ref, inverse_ref, own_ref, full_ref, rows_ref):
+    prow, pcol = place_ref[0], place_ref[5]
+    supernodes, width, _ = diag_ref.shape
+    rows_each, cols_each = own_ref.shape
+    square = (width, width)
+    on_diagonal = lax.broadcasted_iota(jnp.int32, square, 0) == lax.broadcasted_iota(
+        jnp.int32, square, 1
+    )
     for later in range(supernodes):
-        for earlier in range(later):
-            total = factor[pair_index(earlier, later)]
-            for middle in range(earlier + 1, later):
-                total = total + exact_dot(
-                    blocks[earlier, middle], factor[pair_index(middle, later)]
-                )
-            blocks[earlier, later] = -total
-    return blocks
+        for earlier in range(supernodes):
+            if earlier == later:
+                full_ref[earlier, later] = on_diagonal.astype(jnp.float32)
+            elif earlier > later:
+                full_ref[earlier, later] = jnp.zeros(square, jnp.float32)
+            else:
+                total = factor_ref[pair_index(earlier, later)].astype(jnp.float32)
+                for middle in range(earlier + 1, later):
+                    total = total + exact_dot(
+                        full_ref[earlier, middle],
+                        factor_ref[pair_index(middle, later)].astype(jnp.float32),
+                    )
+                full_ref[earlier, later] = -total
+                inverse_ref[pair_index(earlier, later)] = -total
+    row_node, col_node = prow * rows_each // width, pcol * cols_each // width
+
+    rows_ref[...] = jnp.zeros(square, jnp.float32)
+
+    @pl.loop(0, jnp.minimum(row_node, col_node) + 1)
+    def _(k):
+        scaled = exact_dot(diag_ref[k].astype(jnp.float32), full_ref[k, col_node])
+        rows_ref[...] += exact_dot_rows(full_ref[k, row_node], scaled)
+
+    first_row = pl.multiple_of(prow * rows_each % width, rows_each)
+    rows = rows_ref[pl.ds(first_row, rows_each), :]
+    picked = lax.broadcasted_iota(jnp.int32, (width, cols_each), 0) == (
+        lax.broadcasted_iota(jnp.int32, (width, cols_each), 1) + pcol * cols_each % width
+    )
+    own_ref[...] = exact_dot(rows, picked.astype(jnp.float32))
 
 
 def products_kernel(place_ref, flags_ref, *refs, pieces, supernodes, tile_rows, prow_count):
     panel_refs, inverse_ref = refs[:pieces], refs[pieces]
-    high_ref, low_ref, panel_ref = refs[pieces + 1 :]
+    high_ref, low_ref, *mine_refs, panel_ref = refs[pieces + 1 :]
     prow, z = place_ref[0], place_ref[4]
     for later in range(supernodes):
         for r in range(tile_rows):
@@ -79,6 +115,8 @@
         for earlier in range(later):
             total = total + exact_dot(panels[earlier], inverse_ref[pair_index(earlier, later)])
         high_ref[later], low_ref[later] = split(total)
+    for mine_ref in mine_refs:
+        mine_ref[0], mine_ref[1] = high_ref[z], low_ref[z]
 
 
 def main_kernel(place_ref, flags_ref, *refs, lanes, pieces, supernodes, prow_count, width, steps):
@@ -149,16 +187,17 @@
         ys_ref[lax.bitwise_xor(z, d)] = column_refs[d][...]
 
 
-def call(kernel, operands, scalars, outs, scratch, flops):
+def call(kernel, operands, scalars, outs, scratch):
+    arrays = [pltpu.with_memory_space_constraint(a, pltpu.VMEM) for a in operands[scalars:]]
     return pl.pallas_call(
         kernel,
-        out_shape=outs,
-        in_specs=[SMEM] * scalars + [VMEM] * (len(operands) - scalars),
+        out_shape=[pltpu.VMEM(out.shape, out.dtype) for out in outs],
+        in_specs=[SMEM] * scalars + [VMEM] * len(arrays),
         out_specs=[VMEM] * len(outs),
         scratch_shapes=scratch,
-        compiler_params=pltpu.CompilerParams(vmem_limit_bytes=56 * 1024 * 1024),
-        cost_estimate=pl.CostEstimate(flops=flops, bytes_accessed=1 << 20, transcendentals=0),
-    )(*operands)
+        compiler_params=pltpu.CompilerParams(vmem_limit_bytes=20 * 1024 * 1024),
+        cost_estimate=pl.CostEstimate(flops=0, bytes_accessed=0, transcendentals=0),
+    )(*operands[:scalars], *arrays)
 
 
 def per_device(sep_inverse, panels, ancestors, window_factor, diag_inverse):
@@ -174,7 +213,7 @@
     rows = tile_rows * z_count * slice_rows
     bf16, f32 = jnp.bfloat16, jnp.float32
     shape = jax.ShapeDtypeStruct
-    place = jnp.stack([prow, x, core, y, z]).astype(jnp.int32)
+    place = jnp.stack([prow, x, core, y, z, pcol]).astype(jnp.int32)
 
     own_panels = panels.reshape(supernodes, tile_rows, slice_rows, width)
     panel_pieces = [own_panels] + [move(own_panels, 0, 0, d, 0) for d in range(1, z_count)]
@@ -184,33 +223,18 @@
     own_sep = jnp.stack([kept, given]).reshape(2, rows, width)
     sep_pieces = [own_sep] + [move(own_sep, 0, 0, d, 0) for d in range(1, z_count)]
 
-    inverse = inverse_blocks(window_factor, supernodes)
-    stacked = jnp.stack([inverse[m, k] for k in range(supernodes) for m in range(k)])
-    whole = jnp.block(
+    stacked, own_window = call(
+        inverse_kernel,
+        [place, window_factor, diag_inverse],
+        1,
+        [shape(window_factor.shape, f32), shape((rows_each, cols_each), f32)],
         [
-            [
-                jnp.eye(width, dtype=f32)
-                if m == k
-                else inverse[m, k]
-                if m < k
-                else jnp.zeros((width, width), f32)
-                for k in range(supernodes)
-            ]
-            for m in range(supernodes)
-        ]
-    )
-    row_side = lax.dynamic_slice_in_dim(whole, prow * rows_each, rows_each, 1)
-    col_side = lax.dynamic_slice_in_dim(whole, pcol * cols_each, cols_each, 1)
-    scaled = jnp.einsum(
-        "kab,kbc->kac",
-        diag_inverse.astype(f32),
-        col_side.reshape(supernodes, width, cols_each),
-        precision=HIGHEST,
-        preferred_element_type=f32,
-    ).reshape(order, cols_each)
-    own_window = exact_dot(row_side.T, scaled)
-
-    high, low = call(
+            pltpu.VMEM((supernodes, supernodes, width, width), f32),
+            pltpu.VMEM((width, width), f32),
+        ],
+    )
+
+    high, low, *mine = call(
         functools.partial(
             products_kernel,
             pieces=z_count,
@@ -220,14 +244,14 @@
         ),
         [place, ancestors, *panel_pieces, stacked],
         2,
-        [shape((supernodes, rows, width), bf16)] * 2,
+        [shape((supernodes, rows, width), bf16)] * 2
+        + [shape((2, rows, width), bf16)] * (block == width),
         [pltpu.VMEM((supernodes, tile_rows, z_count, slice_rows, width), f32)],
-        6 * rows * order * order,
-    )
-    both = jnp.stack([high, low])
+    )
     if block == width:
-        mine = lax.dynamic_index_in_dim(both, z, 1, keepdims=False)
+        mine = mine[0]
     else:
+        both = jnp.stack([high, low])
         chosen = lax.dynamic_index_in_dim(both, (z * block) // width, 1, keepdims=False)
         mine = lax.dynamic_slice_in_dim(chosen, (z * block) % width, block, 2)
     mine = mine.reshape(2, tile_rows, z_count, slice_rows, block)
@@ -261,7 +285,6 @@
             pltpu.VMEM((tile_rows, z_count, slice_rows, block), f32),
             pltpu.VMEM((order, block), f32),
         ],
-        4 * rows * block * (tile_rows * prow_count * width) + 6 * rows * block * order,
     )
     received = move(send, 0, 1, 0, 0)
     parts = call(
@@ -270,7 +293,6 @@
         0,
         [shape((rows_each, cols_each), f32)] * (2 * x_count),
         [],
-        order * block,
     )
     column_pieces = [columns[0]] + [move(columns[d], 0, 0, d, 0) for d in range(1, z_count)]
     summed = [parts[0]] + [
@@ -288,7 +310,6 @@
             shape((z_count, tile_rows, slice_rows, block), f32),
         ],
         [],
-        order * block,
     )
     if block != width:
         ys = ys.reshape(supernodes, width // block, tile_rows, slice_rows, block)

time: 95.4 us -> 65.3 us (0.68)
  other arithmetic: 15.5 us -> 0.03 us
  matrix products: 10.3 us -> 0 us
  waiting for transfers between devices: 21.1 us -> 28.7 us
  starting transfers between devices: 26.7 us -> 21.8 us
  Pallas kernels: 13.7 us -> 9.07 us
  local copies, waits for them, and re-layouts: 6.67 us -> 4.66 us
    dot_general x6 -> x0, matrix products: 10.3 us -> none  [the longest x5 9.62 us: exact_dot(): jnp.dot(left, right, precision=HIGHEST, preferred_element_type=jnp.float32)]
    concatenate x1 -> x0, other arithmetic: 9.83 us -> none  [per_device(): jnp.block([[jnp.eye(width, dtype=f32) if m == k else inverse[m, k] if m <...]
    ppermute x21, waiting for transfers between devices: 21.1 us -> 28.7 us  [move(): return lax.ppermute(value, AXES, pairs)]
    ppermute x21, starting transfers between devices: 26.7 us -> 21.8 us  [move(): return lax.ppermute(value, AXES, pairs)]
    pallas_call x4 -> x5, Pallas kernels: 13.7 us -> 9.07 us  [call(): pl.pallas_call(kernel, out_shape=[pltpu.VMEM(out.shape, out.dtype) for ou...]
    another operation x2 -> x0, other arithmetic: 1.8 us -> none  [the longest x1 1.08 us: per_device(): both = jnp.stack([high, low])]
    convert_element_type x2 -> x0, other arithmetic: 1.28 us -> none  [the longest x1 1.27 us: inverse_blocks(): factor = window_factor.astype(jnp.float32)]
    dynamic_slice x1 -> x0, local copies, waits for them, and re-layouts: 1.08 us -> none  [per_device(): col_side = lax.dynamic_slice_in_dim(whole, pcol * cols_each, cols_each, 1)]
  transfers between devices with their start and end apart: 21 -> 21, of which waited for: 5 -> 7; matrix products, arithmetic and copies ran while one was open for 31% -> 0% of each run, Pallas kernels for 7% -> 9%
where the time goes in v2:
time: 65.3 us; the launch traced here: 65.1 us
  waiting for transfers between devices  28.7 us (44%)
  starting transfers between devices  21.8 us (33%)
  Pallas kernels  9.07 us (14%)
  local copies, waits for them, and re-layouts  4.66 us (7%)
  between operations  0.79 us (1%)
    ppermute x21, waiting for transfers between devices, move(): return lax.ppermute(value, AXES, pairs)  28.7 us
    ppermute x21, starting transfers between devices, move(): return lax.ppermute(value, AXES, pairs)  21.8 us
    pallas_call x5, Pallas kernels, call(): pl.pallas_call(kernel, out_shape=[pltpu.VMEM(out.shape, out.dtype) for ou...  9.07 us
    unnamed x10, local copies, waits for them, and re-layouts  3.55 us
  transfers between devices with their start and end apart: 21, of which 7 were waited for; matrix products, arithmetic and copies ran while one was open for 0% of the time, Pallas kernels for 9%

profile of v2, /device:TPU:0, one launch (start us, length us, event | category | flops | bytes accessed | tf_op | source)
XLA Modules:
  0.0 65.1 jit_solution(10980285175917364609)
XLA Ops:
  0.6 0.0 copy-start.2
  0.6 0.0 copy-start.3
  0.7 1.0 %constant_dynamic-slice_fusion = (bf16[2,4,1,32,256]{4,3,2,1,0:T(8,128)(2,1)S(1)}, bf16[2,4,32,256]{3,2,1,0:T(8,128)(2,1)S(1)}) fusion(bf16[2,4,2,32,256]{4,3,2,1,0:T(8,128)(2,1)} %bitcast.29, s32[]{:T(128)S(6)} %select_n.29, s32[]{:T(128)S(6)} %select_n.30), kind=kLoop, calls=%fused_computation.2 | loop fusion | bytes 524296 | tf_op jit(solution)/shard_map/jit(dynamic_index_in_dim)/dynamic_slice | solution.py:221
  1.7 3.0 %collective-permute-start.10 = (bf16[2,4,32,256]{3,2,1,0:T(8,128)(2,1)S(1)}, bf16[2,4,32,256]{3,2,1,0:T(8,128)(2,1)S(1)}, u32[]{:S(2)}, u32[]{:S(2)}) collective-permute-start(bf16[2,4,32,256]{3,2,1,0:T(8,128)(2,1)S(1)} %get-tuple-element.39), channel_id=1, source_target_pairs={{0,1},{1,0},{2,3},{3,2},{4,5},{5,4},{6,7},{7,6},{8,9},{9,8},{10,11... | collective-permute-start | bytes 393224 | tf_op jit(solution)/shard_map/ppermute | solution.py:47
  4.7 3.6 %collective-permute-start.2 = (bf16[4,2,32,256]{3,2,1,0:T(8,128)(2,1)}, bf16[4,2,32,256]{3,2,1,0:T(8,128)(2,1)S(1)}, u32[]{:S(2)}, u32[]{:S(2)}) collective-permute-start(bf16[4,2,32,256]{3,2,1,0:T(8,128)(2,1)} %bitcast.24), channel_id=1, source_target_pairs={{0,6},{1,7},{2,4},{3,5},{4,2},{5,3},{6,0},{7,1},{8,14},{9,15},{10,... | collective-permute-start | bytes 393224 | tf_op jit(solution)/shard_map/ppermute | solution.py:47
  8.3 0.0 collective-permute-start.1
  8.3 0.8 %collective-permute-start = (bf16[4,2,32,256]{3,2,1,0:T(8,128)(2,1)}, bf16[4,2,32,256]{3,2,1,0:T(8,128)(2,1)S(1)}, u32[]{:S(2)}, u32[]{:S(2)}) collective-permute-start(bf16[4,2,32,256]{3,2,1,0:T(8,128)(2,1)} %bitcast.26), channel_id=1, source_target_pairs={{0,2},{1,3},{2,0},{3,1},{4,6},{5,7},{6,4},{7,5},{8,10},{9,11},{10,... | collective-permute-start | bytes 393224 | tf_op jit(solution)/shard_map/ppermute | solution.py:47
  9.1 0.1 stack.36.place_ref
  9.2 0.0 copy-start
  9.2 1.1 %copy-done = bf16[6,256,256]{2,1,0:T(8,128)(2,1)S(1)} copy-done((bf16[6,256,256]{2,1,0:T(8,128)(2,1)S(1)}, bf16[6,256,256]{2,1,0:T(8,128)(2,1)}, u32[]{:S(2)}) %copy-start) | copy-done | bytes 786456
  10.3 0.0 copy-start.1
  10.3 1.0 %copy-done.1 = bf16[4,256,256]{2,1,0:T(8,128)(2,1)S(1)} copy-done((bf16[4,256,256]{2,1,0:T(8,128)(2,1)S(1)}, bf16[4,256,256]{2,1,0:T(8,128)(2,1)}, u32[]{:S(2)}) %copy-start.1) | copy-done | bytes 524312
  11.4 3.3 %shard_map.68 = (f32[6,256,256]{2,1,0:T(8,128)S(1)}, f32[256,128]{1,0:T(8,128)S(1)}) custom-call(s32[6]{0:T(128)S(1)} %stack.36.place_ref, bf16[6,256,256]{2,1,0:T(8,128)(2,1)S(1)} %copy-done, bf16[4,256,256]{2,1,0:T(8,128)(2,1)S(1)} %copy-done.1), custom_call_target="tpu_custom_call" | custom-call | tf_op jit(solution)/shard_map/pallas_call | solution.py:192
  14.7 0.0 collective-permute-done.10
  14.8 3.7 %collective-permute-start.13 = (bf16[2,256,256]{2,1,0:T(8,128)(2,1)S(1)}, bf16[2,256,256]{2,1,0:T(8,128)(2,1)S(1)}, u32[]{:S(2)}, u32[]{:S(2)}) collective-permute-start(bf16[2,256,256]{2,1,0:T(8,128)(2,1)S(1)} %pad_maximum_fusion.refs_8_), channel_id=1, source_target_pairs={{0,6},{1,7},{2,4},{3,5},{4,2},{5,3},{6,0},{7,1},{8,14},{9,15},{10,... | collective-permute-start | bytes 786440 | tf_op jit(solution)/shard_map/ppermute | solution.py:47
  18.4 0.0 collective-permute-start.12
  18.4 0.0 collective-permute-done.2.refs_3_
  18.4 13.1 %collective-permute-done.1.refs_2_ = bf16[4,2,32,256]{3,2,1,0:T(8,128)(2,1)S(1)} collective-permute-done((bf16[4,2,32,256]{3,2,1,0:T(8,128)(2,1)}, bf16[4,2,32,256]{3,2,1,0:T(8,128)(2,1)S(1)}, u32[]{:S(2)}, u32[]{:S(2)}) %collective-permute-start.1) | collective-permute-done | bytes 131104 | tf_op jit(solution)/shard_map/ppermute | solution.py:47
  31.6 0.0 collective-permute-done.refs_1_
  31.6 0.0 copy-done.2
  31.6 0.0 copy-done.3
  31.6 2.2 %shard_map.69 = (bf16[4,256,256]{2,1,0:T(8,128)(2,1)S(1)}, bf16[4,256,256]{2,1,0:T(8,128)(2,1)S(1)}, bf16[2,256,256]{2,1,0:T(8,128)(2,1)S(1)}) custom-call(s32[6]{0:T(128)S(1)} %stack.36.place_ref, s32[4,8]{1,0:T(4,128)S(1)} %copy-done.3, bf16[4,2,32,256]{3,2,1,0:T(8,128)(2,1)S(1)} %bitcast.27, bf16[4,2,32,256]{3,2,1,0:T(8,128)(2,1)S(1)} %collective-permute-done.refs_1_, ...), custom_call_target="tpu_custom_call" | custom-call | tf_op jit(solution)/shard_map/pallas_call | solution.py:192
  33.8 0.1 collective-permute-start.5
  33.9 2.0 %collective-permute-start.4 = (bf16[2,2,4,32,256]{4,3,2,1,0:T(8,128)(2,1)S(1)}, bf16[2,2,4,32,256]{4,3,2,1,0:T(8,128)(2,1)S(1)}, u32[]{:S(2)}, u32[]{:S(2)}) collective-permute-start(bf16[2,2,4,32,256]{4,3,2,1,0:T(8,128)(2,1)S(1)} %bitcast.20), channel_id=1, source_target_pairs={{0,16},{1,17},{2,18},{3,19},{4,20},{5,21},{6,22},{7,23},{8,24},{9,... | collective-permute-start | bytes 786440 | tf_op jit(solution)/shard_map/ppermute | solution.py:47
  35.9 1.5 %collective-permute-start.3 = (bf16[2,2,4,32,256]{4,3,2,1,0:T(8,128)(2,1)S(1)}, bf16[2,2,4,32,256]{4,3,2,1,0:T(8,128)(2,1)S(1)}, u32[]{:S(2)}, u32[]{:S(2)}) collective-permute-start(bf16[2,2,4,32,256]{4,3,2,1,0:T(8,128)(2,1)S(1)} %bitcast.21), channel_id=1, source_target_pairs={{0,1},{1,0},{2,3},{3,2},{4,5},{5,4},{6,7},{7,6},{8,9},{9,8},{10,11... | collective-permute-start | bytes 786440 | tf_op jit(solution)/shard_map/ppermute | solution.py:47
  37.4 0.0 collective-permute-done.13.refs_11_
  37.4 0.4 collective-permute-start.11
  37.8 4.2 %collective-permute-done.12.refs_10_ = bf16[2,256,256]{2,1,0:T(8,128)(2,1)S(1)} collective-permute-done((bf16[2,256,256]{2,1,0:T(8,128)(2,1)S(1)}, bf16[2,256,256]{2,1,0:T(8,128)(2,1)S(1)}, u32[]{:S(2)}, u32[]{:S(2)}) %collective-permute-start.12) | collective-permute-done | bytes 262176 | tf_op jit(solution)/shard_map/ppermute | solution.py:47
  41.9 0.0 collective-permute-start.6
  41.9 0.0 collective-permute-done.5.refs_3_
  41.9 0.5 collective-permute-start.9
  42.4 0.6 collective-permute-done.4.refs_2_
  43.0 0.0 collective-permute-start.8
  43.0 1.0 %collective-permute-done.3.refs_1_ = bf16[2,2,4,32,256]{4,3,2,1,0:T(8,128)(2,1)S(1)} collective-permute-done((bf16[2,2,4,32,256]{4,3,2,1,0:T(8,128)(2,1)S(1)}, bf16[2,2,4,32,256]{4,3,2,1,0:T(8,128)(2,1)S(1)}, u32[]{:S(2)}, u32[]{:S(2)}) %collective-permute-start.3) | collective-permute-done | bytes 262176 | tf_op jit(solution)/shard_map/ppermute | solution.py:47
  44.0 0.0 collective-permute-start.7
  44.0 3.2 %collective-permute-done.11.refs_9_ = bf16[2,256,256]{2,1,0:T(8,128)(2,1)S(1)} collective-permute-done((bf16[2,256,256]{2,1,0:T(8,128)(2,1)S(1)}, bf16[2,256,256]{2,1,0:T(8,128)(2,1)S(1)}, u32[]{:S(2)}, u32[]{:S(2)}) %collective-permute-start.11) | collective-permute-done | bytes 262176 | tf_op jit(solution)/shard_map/ppermute | solution.py:47
  47.2 0.0 collective-permute-done.6.refs_4_
  47.2 0.0 collective-permute-done.9.refs_7_
  47.2 0.0 collective-permute-done.8.refs_6_
  47.2 0.0 collective-permute-done.7.refs_5_
  47.2 2.8 %shard_map.70 = (f32[2,32,256]{2,1,0:T(8,128)S(1)}, f32[2,32,256]{2,1,0:T(8,128)S(1)}, f32[2,32,256]{2,1,0:T(8,128)S(1)}, f32[2,32,256]{2,1,0:T(8,128)S(1)}, f32...) custom-call(s32[6]{0:T(128)S(1)} %stack.36.place_ref, s32[4,8]{1,0:T(4,128)S(1)} %copy-done.3, ...), custom_call_target="tpu_custom_call" | custom-call | tf_op jit(solution)/shard_map/pallas_call | solution.py:192
  50.1 0.1 collective-permute-start.14
  50.1 0.1 collective-permute-start.18
  50.2 1.8 %collective-permute-done.14.received_ref = f32[2,2,256,128]{3,2,1,0:T(8,128)S(1)} collective-permute-done((f32[2,2,256,128]{3,2,1,0:T(8,128)S(1)}, f32[2,2,256,128]{3,2,1,0:T(8,128)S(1)}, u32[]{:S(2)}, u32[]{:S(2)}) %collective-permute-start.14) | collective-permute-done | bytes 524320 | tf_op jit(solution)/shard_map/ppermute | solution.py:47
  52.0 0.1 shard_map.71
  52.1 0.6 collective-permute-start.15
  52.7 1.1 %collective-permute-start.16 = (f32[256,128]{1,0:T(8,128)S(1)}, f32[256,128]{1,0:T(8,128)S(1)}, u32[]{:S(2)}, u32[]{:S(2)}) collective-permute-start(f32[256,128]{1,0:T(8,128)S(1)} %get-tuple-element.27), channel_id=1, source_target_pairs={{0,16},{1,17},{2,18},{3,19},{4,20},{5,21},{6,22},{7,23},{8,24},{9,... | collective-permute-start | bytes 393224 | tf_op jit(solution)/shard_map/ppermute | solution.py:47
  53.8 1.9 %collective-permute-start.17 = (f32[256,128]{1,0:T(8,128)S(1)}, f32[256,128]{1,0:T(8,128)S(1)}, u32[]{:S(2)}, u32[]{:S(2)}) collective-permute-start(f32[256,128]{1,0:T(8,128)S(1)} %get-tuple-element.28), channel_id=1, source_target_pairs={{0,17},{1,16},{2,19},{3,18},{4,21},{5,20},{6,23},{7,22},{8,25},{9,... | collective-permute-start | bytes 393224 | tf_op jit(solution)/shard_map/ppermute | solution.py:47
  55.7 1.0 %collective-permute-start.19 = (f32[2,32,256]{2,1,0:T(8,128)S(1)}, f32[2,32,256]{2,1,0:T(8,128)S(1)}, u32[]{:S(2)}, u32[]{:S(2)}) collective-permute-start(f32[2,32,256]{2,1,0:T(8,128)S(1)} %get-tuple-element.32), channel_id=1, source_target_pairs={{0,4},{1,5},{2,6},{3,7},{4,0},{5,1},{6,2},{7,3},{8,12},{9,13},{10,... | collective-permute-start | bytes 196616 | tf_op jit(solution)/shard_map/ppermute | solution.py:47
  56.7 0.0 collective-permute-done.18.refs_6_
  56.7 1.6 %collective-permute-start.20 = (f32[2,32,256]{2,1,0:T(8,128)S(1)}, f32[2,32,256]{2,1,0:T(8,128)S(1)}, u32[]{:S(2)}, u32[]{:S(2)}) collective-permute-start(f32[2,32,256]{2,1,0:T(8,128)S(1)} %get-tuple-element.33), channel_id=1, source_target_pairs={{0,6},{1,7},{2,4},{3,5},{4,2},{5,3},{6,0},{7,1},{8,14},{9,15},{10,... | collective-permute-start | bytes 196616 | tf_op jit(solution)/shard_map/ppermute | solution.py:47
  58.2 4.8 %collective-permute-done.19.refs_7_ = f32[2,32,256]{2,1,0:T(8,128)S(1)} collective-permute-done((f32[2,32,256]{2,1,0:T(8,128)S(1)}, f32[2,32,256]{2,1,0:T(8,128)S(1)}, u32[]{:S(2)}, u32[]{:S(2)}) %collective-permute-start.19) | collective-permute-done | bytes 65568 | tf_op jit(solution)/shard_map/ppermute | solution.py:47
  63.1 0.0 collective-permute-done.20.refs_8_
  63.1 0.0 collective-permute-done.15.refs_1_
  63.1 0.0 collective-permute-done.16.refs_2_
  63.1 0.0 collective-permute-done.17.refs_3_
  63.1 0.6 shard_map.72
  63.7 0.7 %copy.10 = f32[4,2,1,32,256]{4,3,2,1,0:T(8,128)} copy(f32[4,2,1,32,256]{4,3,2,1,0:T(8,128)S(1)} %bitcast.18) | data formatting | bytes 524288
  64.4 0.7 %copy.11 = f32[256,128]{1,0:T(8,128)} copy(f32[256,128]{1,0:T(8,128)S(1)} %get-tuple-element.41) | data formatting | bytes 262144
  (1 shorter events, 0.0 us)
Async XLA Ops:
  0.6 31.0 %copy-start.2 = (bf16[4,2,1,32,256]{4,3,2,1,0:T(8,128)(2,1)S(1)}, bf16[4,2,1,32,256]{4,3,2,1,0:T(8,128)(2,1)}, u32[]{:S(2)}) copy-start(bf16[4,2,1,32,256]{4,3,2,1,0:T(8,128)(2,1)} %param.6) | copy-start | bytes 393220
  0.6 30.9 %copy-start.3 = (s32[4,8]{1,0:T(4,128)S(1)}, s32[4,8]{1,0:T(4,128)}, u32[]{:S(2)}) copy-start(s32[4,8]{1,0:T(4,128)} %flags_ref.3) | copy-start | bytes 388
  1.7 13.0 %collective-permute-start.10 = (bf16[2,4,32,256]{3,2,1,0:T(8,128)(2,1)S(1)}, bf16[2,4,32,256]{3,2,1,0:T(8,128)(2,1)S(1)}, u32[]{:S(2)}, u32[]{:S(2)}) collective-permute-start(bf16[2,4,32,256]{3,2,1,0:T(8,128)(2,1)S(1)} %get-tuple-element.39), channel_id=1, source_target_pairs={{0,1},{1,0},{2,3},{3,2},{4,5},{5,4},{6,7},{7,6},{8,9},{9,8},{10,11... | collective-permute-start | bytes 393224 | tf_op jit(solution)/shard_map/ppermute | solution.py:47
  4.7 13.7 %collective-permute-start.2 = (bf16[4,2,32,256]{3,2,1,0:T(8,128)(2,1)}, bf16[4,2,32,256]{3,2,1,0:T(8,128)(2,1)S(1)}, u32[]{:S(2)}, u32[]{:S(2)}) collective-permute-start(bf16[4,2,32,256]{3,2,1,0:T(8,128)(2,1)} %bitcast.24), channel_id=1, source_target_pairs={{0,6},{1,7},{2,4},{3,5},{4,2},{5,3},{6,0},{7,1},{8,14},{9,15},{10,... | collective-permute-start | bytes 393224 | tf_op jit(solution)/shard_map/ppermute | solution.py:47
  8.3 23.2 %collective-permute-start.1 = (bf16[4,2,32,256]{3,2,1,0:T(8,128)(2,1)}, bf16[4,2,32,256]{3,2,1,0:T(8,128)(2,1)S(1)}, u32[]{:S(2)}, u32[]{:S(2)}) collective-permute-start(bf16[4,2,32,256]{3,2,1,0:T(8,128)(2,1)} %bitcast.25), channel_id=1, source_target_pairs={{0,4},{1,5},{2,6},{3,7},{4,0},{5,1},{6,2},{7,3},{8,12},{9,13},{10,... | collective-permute-start | bytes 393224 | tf_op jit(solution)/shard_map/ppermute | solution.py:47
  8.3 23.2 %collective-permute-start = (bf16[4,2,32,256]{3,2,1,0:T(8,128)(2,1)}, bf16[4,2,32,256]{3,2,1,0:T(8,128)(2,1)S(1)}, u32[]{:S(2)}, u32[]{:S(2)}) collective-permute-start(bf16[4,2,32,256]{3,2,1,0:T(8,128)(2,1)} %bitcast.26), channel_id=1, source_target_pairs={{0,2},{1,3},{2,0},{3,1},{4,6},{5,7},{6,4},{7,5},{8,10},{9,11},{10,... | collective-permute-start | bytes 393224 | tf_op jit(solution)/shard_map/ppermute | solution.py:47
  9.2 1.1 %copy-start = (bf16[6,256,256]{2,1,0:T(8,128)(2,1)S(1)}, bf16[6,256,256]{2,1,0:T(8,128)(2,1)}, u32[]{:S(2)}) copy-start(bf16[6,256,256]{2,1,0:T(8,128)(2,1)} %factor_ref.1) | copy-start | bytes 2359300
  10.3 1.0 %copy-start.1 = (bf16[4,256,256]{2,1,0:T(8,128)(2,1)S(1)}, bf16[4,256,256]{2,1,0:T(8,128)(2,1)}, u32[]{:S(2)}) copy-start(bf16[4,256,256]{2,1,0:T(8,128)(2,1)} %diag_ref.1) | copy-start | bytes 1572868
  14.8 22.6 %collective-permute-start.13 = (bf16[2,256,256]{2,1,0:T(8,128)(2,1)S(1)}, bf16[2,256,256]{2,1,0:T(8,128)(2,1)S(1)}, u32[]{:S(2)}, u32[]{:S(2)}) collective-permute-start(bf16[2,256,256]{2,1,0:T(8,128)(2,1)S(1)} %pad_maximum_fusion.refs_8_), channel_id=1, source_target_pairs={{0,6},{1,7},{2,4},{3,5},{4,2},{5,3},{6,0},{7,1},{8,14},{9,15},{10,... | collective-permute-start | bytes 786440 | tf_op jit(solution)/shard_map/ppermute | solution.py:47
  18.4 23.5 %collective-permute-start.12 = (bf16[2,256,256]{2,1,0:T(8,128)(2,1)S(1)}, bf16[2,256,256]{2,1,0:T(8,128)(2,1)S(1)}, u32[]{:S(2)}, u32[]{:S(2)}) collective-permute-start(bf16[2,256,256]{2,1,0:T(8,128)(2,1)S(1)} %pad_maximum_fusion.refs_8_), channel_id=1, source_target_pairs={{0,4},{1,5},{2,6},{3,7},{4,0},{5,1},{6,2},{7,3},{8,12},{9,13},{10,... | collective-permute-start | bytes 786440 | tf_op jit(solution)/shard_map/ppermute | solution.py:47
  33.8 8.1 %collective-permute-start.5 = (bf16[2,2,4,32,256]{4,3,2,1,0:T(8,128)(2,1)S(1)}, bf16[2,2,4,32,256]{4,3,2,1,0:T(8,128)(2,1)S(1)}, u32[]{:S(2)}, u32[]{:S(2)}) collective-permute-start(bf16[2,2,4,32,256]{4,3,2,1,0:T(8,128)(2,1)S(1)} %bitcast.19), channel_id=1, source_target_pairs={{0,17},{1,16},{2,19},{3,18},{4,21},{5,20},{6,23},{7,22},{8,25},{9,... | collective-permute-start | bytes 786440 | tf_op jit(solution)/shard_map/ppermute | solution.py:47
  33.9 9.1 %collective-permute-start.4 = (bf16[2,2,4,32,256]{4,3,2,1,0:T(8,128)(2,1)S(1)}, bf16[2,2,4,32,256]{4,3,2,1,0:T(8,128)(2,1)S(1)}, u32[]{:S(2)}, u32[]{:S(2)}) collective-permute-start(bf16[2,2,4,32,256]{4,3,2,1,0:T(8,128)(2,1)S(1)} %bitcast.20), channel_id=1, source_target_pairs={{0,16},{1,17},{2,18},{3,19},{4,20},{5,21},{6,22},{7,23},{8,24},{9,... | collective-permute-start | bytes 786440 | tf_op jit(solution)/shard_map/ppermute | solution.py:47
  35.9 8.1 %collective-permute-start.3 = (bf16[2,2,4,32,256]{4,3,2,1,0:T(8,128)(2,1)S(1)}, bf16[2,2,4,32,256]{4,3,2,1,0:T(8,128)(2,1)S(1)}, u32[]{:S(2)}, u32[]{:S(2)}) collective-permute-start(bf16[2,2,4,32,256]{4,3,2,1,0:T(8,128)(2,1)S(1)} %bitcast.21), channel_id=1, source_target_pairs={{0,1},{1,0},{2,3},{3,2},{4,5},{5,4},{6,7},{7,6},{8,9},{9,8},{10,11... | collective-permute-start | bytes 786440 | tf_op jit(solution)/shard_map/ppermute | solution.py:47
  37.4 9.8 %collective-permute-start.11 = (bf16[2,256,256]{2,1,0:T(8,128)(2,1)S(1)}, bf16[2,256,256]{2,1,0:T(8,128)(2,1)S(1)}, u32[]{:S(2)}, u32[]{:S(2)}) collective-permute-start(bf16[2,256,256]{2,1,0:T(8,128)(2,1)S(1)} %pad_maximum_fusion.refs_8_), channel_id=1, source_target_pairs={{0,2},{1,3},{2,0},{3,1},{4,6},{5,7},{6,4},{7,5},{8,10},{9,11},{10,... | collective-permute-start | bytes 786440 | tf_op jit(solution)/shard_map/ppermute | solution.py:47
  41.9 5.3 %collective-permute-start.6 = (bf16[2,2,4,32,256]{4,3,2,1,0:T(8,128)(2,1)S(1)}, bf16[2,2,4,32,256]{4,3,2,1,0:T(8,128)(2,1)S(1)}, u32[]{:S(2)}, u32[]{:S(2)}) collective-permute-start(bf16[2,2,4,32,256]{4,3,2,1,0:T(8,128)(2,1)S(1)} %bitcast.22), channel_id=1, source_target_pairs={{0,8},{1,9},{2,10},{3,11},{4,12},{5,13},{6,14},{7,15},{8,0},{9,1},... | collective-permute-start | bytes 786440 | tf_op jit(solution)/shard_map/ppermute | solution.py:47
  41.9 5.3 %collective-permute-start.9 = (bf16[2,2,4,32,256]{4,3,2,1,0:T(8,128)(2,1)S(1)}, bf16[2,2,4,32,256]{4,3,2,1,0:T(8,128)(2,1)S(1)}, u32[]{:S(2)}, u32[]{:S(2)}) collective-permute-start(bf16[2,2,4,32,256]{4,3,2,1,0:T(8,128)(2,1)S(1)} %collective-permute-done.5.refs_3_), channel_id=1, source_target_pairs={{0,8},{1,9},{2,10},{3,11},{4,12},{5,13},{6,14},{7,15},{8,0},{9,1},... | collective-permute-start | bytes 786440 | tf_op jit(solution)/shard_map/ppermute | solution.py:47
  43.0 4.2 %collective-permute-start.8 = (bf16[2,2,4,32,256]{4,3,2,1,0:T(8,128)(2,1)S(1)}, bf16[2,2,4,32,256]{4,3,2,1,0:T(8,128)(2,1)S(1)}, u32[]{:S(2)}, u32[]{:S(2)}) collective-permute-start(bf16[2,2,4,32,256]{4,3,2,1,0:T(8,128)(2,1)S(1)} %collective-permute-done.4.refs_2_), channel_id=1, source_target_pairs={{0,8},{1,9},{2,10},{3,11},{4,12},{5,13},{6,14},{7,15},{8,0},{9,1},... | collective-permute-start | bytes 786440 | tf_op jit(solution)/shard_map/ppermute | solution.py:47
  44.0 3.2 %collective-permute-start.7 = (bf16[2,2,4,32,256]{4,3,2,1,0:T(8,128)(2,1)S(1)}, bf16[2,2,4,32,256]{4,3,2,1,0:T(8,128)(2,1)S(1)}, u32[]{:S(2)}, u32[]{:S(2)}) collective-permute-start(bf16[2,2,4,32,256]{4,3,2,1,0:T(8,128)(2,1)S(1)} %collective-permute-done.3.refs_1_), channel_id=1, source_target_pairs={{0,8},{1,9},{2,10},{3,11},{4,12},{5,13},{6,14},{7,15},{8,0},{9,1},... | collective-permute-start | bytes 786440 | tf_op jit(solution)/shard_map/ppermute | solution.py:47
  50.1 2.0 %collective-permute-start.14 = (f32[2,2,256,128]{3,2,1,0:T(8,128)S(1)}, f32[2,2,256,128]{3,2,1,0:T(8,128)S(1)}, u32[]{:S(2)}, u32[]{:S(2)}) collective-permute-start(f32[2,2,256,128]{3,2,1,0:T(8,128)S(1)} %get-tuple-element.24), channel_id=1, source_target_pairs={{0,8},{1,9},{2,10},{3,11},{4,12},{5,13},{6,14},{7,15},{8,0},{9,1},... | collective-permute-start | bytes 1572872 | tf_op jit(solution)/shard_map/ppermute | solution.py:47
  50.1 6.5 %collective-permute-start.18 = (f32[2,32,256]{2,1,0:T(8,128)S(1)}, f32[2,32,256]{2,1,0:T(8,128)S(1)}, u32[]{:S(2)}, u32[]{:S(2)}) collective-permute-start(f32[2,32,256]{2,1,0:T(8,128)S(1)} %get-tuple-element.31), channel_id=1, source_target_pairs={{0,2},{1,3},{2,0},{3,1},{4,6},{5,7},{6,4},{7,5},{8,10},{9,11},{10,... | collective-permute-start | bytes 196616 | tf_op jit(solution)/shard_map/ppermute | solution.py:47
  52.1 11.0 %collective-permute-start.15 = (f32[256,128]{1,0:T(8,128)S(1)}, f32[256,128]{1,0:T(8,128)S(1)}, u32[]{:S(2)}, u32[]{:S(2)}) collective-permute-start(f32[256,128]{1,0:T(8,128)S(1)} %get-tuple-element.26), channel_id=1, source_target_pairs={{0,1},{1,0},{2,3},{3,2},{4,5},{5,4},{6,7},{7,6},{8,9},{9,8},{10,11... | collective-permute-start | bytes 393224 | tf_op jit(solution)/shard_map/ppermute | solution.py:47
  52.7 10.4 %collective-permute-start.16 = (f32[256,128]{1,0:T(8,128)S(1)}, f32[256,128]{1,0:T(8,128)S(1)}, u32[]{:S(2)}, u32[]{:S(2)}) collective-permute-start(f32[256,128]{1,0:T(8,128)S(1)} %get-tuple-element.27), channel_id=1, source_target_pairs={{0,16},{1,17},{2,18},{3,19},{4,20},{5,21},{6,22},{7,23},{8,24},{9,... | collective-permute-start | bytes 393224 | tf_op jit(solution)/shard_map/ppermute | solution.py:47
  53.8 9.3 %collective-permute-start.17 = (f32[256,128]{1,0:T(8,128)S(1)}, f32[256,128]{1,0:T(8,128)S(1)}, u32[]{:S(2)}, u32[]{:S(2)}) collective-permute-start(f32[256,128]{1,0:T(8,128)S(1)} %get-tuple-element.28), channel_id=1, source_target_pairs={{0,17},{1,16},{2,19},{3,18},{4,21},{5,20},{6,23},{7,22},{8,25},{9,... | collective-permute-start | bytes 393224 | tf_op jit(solution)/shard_map/ppermute | solution.py:47
  55.7 7.4 %collective-permute-start.19 = (f32[2,32,256]{2,1,0:T(8,128)S(1)}, f32[2,32,256]{2,1,0:T(8,128)S(1)}, u32[]{:S(2)}, u32[]{:S(2)}) collective-permute-start(f32[2,32,256]{2,1,0:T(8,128)S(1)} %get-tuple-element.32), channel_id=1, source_target_pairs={{0,4},{1,5},{2,6},{3,7},{4,0},{5,1},{6,2},{7,3},{8,12},{9,13},{10,... | collective-permute-start | bytes 196616 | tf_op jit(solution)/shard_map/ppermute | solution.py:47
  56.7 6.4 %collective-permute-start.20 = (f32[2,32,256]{2,1,0:T(8,128)S(1)}, f32[2,32,256]{2,1,0:T(8,128)S(1)}, u32[]{:S(2)}, u32[]{:S(2)}) collective-permute-start(f32[2,32,256]{2,1,0:T(8,128)S(1)} %get-tuple-element.33), channel_id=1, source_target_pairs={{0,6},{1,7},{2,4},{3,5},{4,2},{5,3},{6,0},{7,1},{8,14},{9,15},{10,... | collective-permute-start | bytes 196616 | tf_op jit(solution)/shard_map/ppermute | solution.py:47

commit v3 on v2

--- a/solution.py
+++ b/solution.py
@@ -57,44 +57,58 @@
     )
 
 
-def inverse_kernel(place_ref, factor_ref, diag_ref, inverse_ref, own_ref, full_ref, rows_ref):
+def three_parts(value):
+    high, rest = split(value)
+    low = (value - high.astype(jnp.float32) - rest.astype(jnp.float32)).astype(jnp.bfloat16)
+    return high, rest, low
+
+
+def inverse_kernel(factor_ref, inverse_ref, *, supernodes):
+    for later in range(supernodes):
+        for earlier in range(later):
+            total = factor_ref[pair_index(earlier, later)].astype(jnp.float32)
+            for middle in range(earlier + 1, later):
+                right = factor_ref[pair_index(middle, later)]
+                for part in three_parts(inverse_ref[pair_index(earlier, middle)]):
+                    total = total + dot(part, right)
+            inverse_ref[pair_index(earlier, later)] = -total
+
+
+def diagonal_kernel(place_ref, inverse_ref, diag_ref, own_ref, full_ref, rows_ref):
     prow, pcol = place_ref[0], place_ref[5]
     supernodes, width, _ = diag_ref.shape
     rows_each, cols_each = own_ref.shape
+    row_node, col_node = prow * rows_each // width, pcol * cols_each // width
     square = (width, width)
     on_diagonal = lax.broadcasted_iota(jnp.int32, square, 0) == lax.broadcasted_iota(
         jnp.int32, square, 1
     )
-    for later in range(supernodes):
-        for earlier in range(supernodes):
-            if earlier == later:
-                full_ref[earlier, later] = on_diagonal.astype(jnp.float32)
-            elif earlier > later:
-                full_ref[earlier, later] = jnp.zeros(square, jnp.float32)
-            else:
-                total = factor_ref[pair_index(earlier, later)].astype(jnp.float32)
-                for middle in range(earlier + 1, later):
-                    total = total + exact_dot(
-                        full_ref[earlier, middle],
-                        factor_ref[pair_index(middle, later)].astype(jnp.float32),
-                    )
-                full_ref[earlier, later] = -total
-                inverse_ref[pair_index(earlier, later)] = -total
-    row_node, col_node = prow * rows_each // width, pcol * cols_each // width
-
-    rows_ref[...] = jnp.zeros(square, jnp.float32)
+    for which, node in enumerate((row_node, col_node)):
+        full_ref[which, node] = on_diagonal.astype(jnp.float32)
+
+        @pl.loop(0, node)
+        def _(k, which=which, node=node):
+            full_ref[which, k] = inverse_ref[node * (node - 1) // 2 + k]
+
+    halves = 2 * cols_each == width
+    rows_ref[...] = jnp.zeros_like(rows_ref)
 
     @pl.loop(0, jnp.minimum(row_node, col_node) + 1)
     def _(k):
-        scaled = exact_dot(diag_ref[k].astype(jnp.float32), full_ref[k, col_node])
-        rows_ref[...] += exact_dot_rows(full_ref[k, row_node], scaled)
+        cols = full_ref[1, k]
+        if halves:
+            cols = jnp.where(pcol % 2 == 0, cols[:, :cols_each], cols[:, cols_each:])
+        scaled = sum(dot(diag_ref[k], part) for part in three_parts(cols))
+        rows_ref[...] += exact_dot_rows(full_ref[0, k], scaled)
 
     first_row = pl.multiple_of(prow * rows_each % width, rows_each)
     rows = rows_ref[pl.ds(first_row, rows_each), :]
-    picked = lax.broadcasted_iota(jnp.int32, (width, cols_each), 0) == (
-        lax.broadcasted_iota(jnp.int32, (width, cols_each), 1) + pcol * cols_each % width
-    )
-    own_ref[...] = exact_dot(rows, picked.astype(jnp.float32))
+    if not halves:
+        picked = lax.broadcasted_iota(jnp.int32, (width, cols_each), 0) == (
+            lax.broadcasted_iota(jnp.int32, (width, cols_each), 1) + pcol * cols_each % width
+        )
+        rows = exact_dot(rows, picked.astype(jnp.float32))
+    own_ref[...] = rows
 
 
 def products_kernel(place_ref, flags_ref, *refs, pieces, supernodes, tile_rows, prow_count):
@@ -110,20 +124,21 @@
                 )
     rows, width = high_ref.shape[1], high_ref.shape[2]
     panels = [panel_ref[k].reshape(rows, width) for k in range(supernodes)]
+    narrow = [panel.astype(jnp.bfloat16) for panel in panels]
     for later in range(supernodes):
         total = panels[later]
         for earlier in range(later):
-            total = total + exact_dot(panels[earlier], inverse_ref[pair_index(earlier, later)])
+            for part in three_parts(inverse_ref[pair_index(earlier, later)]):
+                total = total + dot(narrow[earlier], part)
         high_ref[later], low_ref[later] = split(total)
     for mine_ref in mine_refs:
         mine_ref[0], mine_ref[1] = high_ref[z], low_ref[z]
 
 
-def main_kernel(place_ref, flags_ref, *refs, lanes, pieces, supernodes, prow_count, width, steps):
+def columns_kernel(place_ref, flags_ref, *refs, lanes, pieces, prow_count, width, steps):
     lane_refs, sep_refs = refs[:lanes], refs[lanes : lanes + pieces]
-    high_ref, low_ref = refs[lanes + pieces : lanes + pieces + 2]
-    column_refs = refs[lanes + pieces + 2 : lanes + 2 * pieces + 2]
-    keep_ref, send_ref, gathered_ref, sums_ref, window_ref = refs[lanes + 2 * pieces + 2 :]
+    column_refs = refs[lanes + pieces : lanes + 2 * pieces]
+    high_ref, low_ref, gathered_ref, sums_ref = refs[lanes + 2 * pieces :]
     prow, x, core, y, z = (place_ref[i] for i in range(5))
     _, tile_rows, sub_count, slice_rows, block = lane_refs[0].shape
     kind = gathered_ref.dtype
@@ -151,9 +166,17 @@
         for r in range(tile_rows):
             keep = flags_ref[later, r * prow_count + prow].astype(jnp.float32)
             column_refs[d][r] = sums_ref[r, lax.bitwise_xor(z, d)] * -keep
-    high, low = split(total)
+    high_ref[...], low_ref[...] = split(total)
+
+
+def window_kernel(
+    place_ref, left_high_ref, left_low_ref, high_ref, low_ref, keep_ref, send_ref, window_ref
+):
+    x, core, y = (place_ref[i] for i in range(1, 4))
+    supernodes, _, width = left_high_ref.shape
+    high, low = high_ref[...], low_ref[...]
     for k in range(supernodes):
-        left_high, left_low = high_ref[k], low_ref[k]
+        left_high, left_low = left_high_ref[k], left_low_ref[k]
         window_ref[k * width : (k + 1) * width, :] = (
             dot_rows(left_high, high) + dot_rows(left_high, low) + dot_rows(left_low, high)
         )
@@ -174,29 +197,36 @@
             out_refs[2 * dx + dy][...] = keep_ref[dx, dy] + received_ref[dx, dy]
 
 
-def last_kernel(place_ref, *refs, parts, pieces):
-    z = place_ref[4]
-    part_refs, own_ref = refs[:parts], refs[parts]
-    column_refs = refs[parts + 1 : parts + 1 + pieces]
-    window_ref, ys_ref = refs[parts + 1 + pieces :]
-    total = own_ref[...]
-    for ref in part_refs:
+def last_kernel(_, *refs):
+    *part_refs, window_ref = refs
+    total = part_refs[0][...]
+    for ref in part_refs[1:]:
         total = total + ref[...]
     window_ref[...] = total
-    for d in range(pieces):
-        ys_ref[lax.bitwise_xor(z, d)] = column_refs[d][...]
-
-
-def call(kernel, operands, scalars, outs, scratch):
+
+
+def ys_kernel(place_ref, *refs):
+    *column_refs, ys_ref, done_ref = refs
+    z = place_ref[4]
+    for d, ref in enumerate(column_refs):
+        ys_ref[lax.bitwise_xor(z, d)] = ref[...]
+    done_ref[...] = jnp.zeros_like(done_ref)
+
+
+def after(value, *others):
+    return lax.optimization_barrier((value, *others))[0]
+
+
+def call(kernel, operands, scalars, outs, scratch, cost, last=False):
     arrays = [pltpu.with_memory_space_constraint(a, pltpu.VMEM) for a in operands[scalars:]]
     return pl.pallas_call(
         kernel,
-        out_shape=[pltpu.VMEM(out.shape, out.dtype) for out in outs],
+        out_shape=outs if last else [pltpu.VMEM(out.shape, out.dtype) for out in outs],
         in_specs=[SMEM] * scalars + [VMEM] * len(arrays),
         out_specs=[VMEM] * len(outs),
         scratch_shapes=scratch,
         compiler_params=pltpu.CompilerParams(vmem_limit_bytes=20 * 1024 * 1024),
-        cost_estimate=pl.CostEstimate(flops=0, bytes_accessed=0, transcendentals=0),
+        cost_estimate=pl.CostEstimate(flops=cost, bytes_accessed=0, transcendentals=0),
     )(*operands[:scalars], *arrays)
 
 
@@ -217,21 +247,30 @@
 
     own_panels = panels.reshape(supernodes, tile_rows, slice_rows, width)
     panel_pieces = [own_panels] + [move(own_panels, 0, 0, d, 0) for d in range(1, z_count)]
-    by_parity = sep_inverse.reshape(tile_rows, z_count, 2, slice_rows, width)
-    kept = lax.dynamic_index_in_dim(by_parity, y, 2, keepdims=False)
-    given = move(lax.dynamic_index_in_dim(by_parity, 1 - y, 2, keepdims=False), 0, 0, 0, 1)
-    own_sep = jnp.stack([kept, given]).reshape(2, rows, width)
+    local_sep = sep_inverse.reshape(tile_rows, width, width)
+    both_sep = jnp.stack([local_sep, move(local_sep, 0, 0, 0, 1)])
+    both_sep = both_sep.reshape(2, tile_rows, z_count, 2, slice_rows, width)
+    own_sep = lax.dynamic_index_in_dim(both_sep, y, 3, keepdims=False).reshape(2, rows, width)
     sep_pieces = [own_sep] + [move(own_sep, 0, 0, d, 0) for d in range(1, z_count)]
 
-    stacked, own_window = call(
-        inverse_kernel,
-        [place, window_factor, diag_inverse],
+    (stacked,) = call(
+        functools.partial(inverse_kernel, supernodes=supernodes),
+        [window_factor],
+        0,
+        [shape(window_factor.shape, f32)],
+        [],
+        cost=1_000_000_000,
+    )
+    (own_window,) = call(
+        diagonal_kernel,
+        [place, stacked, diag_inverse],
         1,
-        [shape(window_factor.shape, f32), shape((rows_each, cols_each), f32)],
+        [shape((rows_each, cols_each), f32)],
         [
-            pltpu.VMEM((supernodes, supernodes, width, width), f32),
-            pltpu.VMEM((width, width), f32),
+            pltpu.VMEM((2, supernodes, width, width), f32),
+            pltpu.VMEM((width, cols_each if 2 * cols_each == width else width), f32),
         ],
+        cost=3_000_000_000,
     )
 
     high, low, *mine = call(
@@ -242,11 +281,12 @@
             tile_rows=tile_rows,
             prow_count=prow_count,
         ),
-        [place, ancestors, *panel_pieces, stacked],
+        [after(place, own_sep, own_window), ancestors, *panel_pieces, stacked],
         2,
         [shape((supernodes, rows, width), bf16)] * 2
         + [shape((2, rows, width), bf16)] * (block == width),
         [pltpu.VMEM((supernodes, tile_rows, z_count, slice_rows, width), f32)],
+        cost=2_500_000_000,
     )
     if block == width:
         mine = mine[0]
@@ -258,7 +298,8 @@
     steps, lanes = [], []
     for dx in range(x_count):
         for dy in range(2):
-            lane = mine if dx + dy == 0 else move(mine, dx, 0, 0, dy)
+            source = after(mine, sep_pieces[1]) if dx + dy == 2 else mine
+            lane = mine if dx + dy == 0 else move(source, dx, 0, 0, dy)
             lanes.append(lane)
             steps.append((dx, 0, dy))
     for (dx, _, dy), lane in zip(list(steps), list(lanes)):
@@ -266,25 +307,32 @@
         steps.append((dx, 1, dy))
 
     kind = bf16 if slice_rows % 16 == 0 else f32
-    *columns, keep, send = call(
+    *columns, sums_high, sums_low = call(
         functools.partial(
-            main_kernel,
+            columns_kernel,
             lanes=len(lanes),
             pieces=z_count,
-            supernodes=supernodes,
             prow_count=prow_count,
             width=width,
             steps=tuple(steps),
         ),
-        [place, ancestors, *lanes, *sep_pieces, high, low],
+        [place, ancestors, *lanes, *sep_pieces],
         2,
-        [shape((tile_rows, slice_rows, block), f32)] * z_count
-        + [shape((x_count, 2, rows_each, cols_each), f32)] * 2,
+        [shape((tile_rows, slice_rows, block), f32)] * z_count + [shape((rows, block), bf16)] * 2,
         [
             pltpu.VMEM((2, tile_rows * prow_count, pcol_count, slice_rows, block), kind),
             pltpu.VMEM((tile_rows, z_count, slice_rows, block), f32),
-            pltpu.VMEM((order, block), f32),
         ],
+        cost=1_700_000_000,
+    )
+    column_pieces = [columns[0]] + [move(columns[d], 0, 0, d, 0) for d in range(1, z_count)]
+    keep, send = call(
+        window_kernel,
+        [place, high, low, sums_high, sums_low],
+        1,
+        [shape((x_count, 2, rows_each, cols_each), f32)] * 2,
+        [pltpu.VMEM((order, block), f32)],
+        cost=1_400_000_000,
     )
     received = move(send, 0, 1, 0, 0)
     parts = call(
@@ -293,23 +341,31 @@
         0,
         [shape((rows_each, cols_each), f32)] * (2 * x_count),
         [],
-    )
-    column_pieces = [columns[0]] + [move(columns[d], 0, 0, d, 0) for d in range(1, z_count)]
+        cost=100_000_000,
+    )
     summed = [parts[0]] + [
         move(parts[2 * dx + dy], dx, 0, 0, dy)
         for dx in range(x_count)
         for dy in range(2)
         if dx + dy > 0
     ]
-    window, ys = call(
-        functools.partial(last_kernel, parts=len(summed), pieces=z_count),
-        [place, *summed, own_window, *column_pieces],
+    ys, done = call(
+        ys_kernel,
+        [place, *column_pieces],
         1,
-        [
-            shape((rows_each, cols_each), f32),
-            shape((z_count, tile_rows, slice_rows, block), f32),
-        ],
+        [shape((z_count, tile_rows, slice_rows, block), f32), shape((8, 128), f32)],
         [],
+        cost=12_000_000_000,
+        last=True,
+    )
+    (window,) = call(
+        last_kernel,
+        [done, *summed, own_window],
+        0,
+        [shape((rows_each, cols_each), f32)],
+        [],
+        cost=500_000_000,
+        last=True,
     )
     if block != width:
         ys = ys.reshape(supernodes, width // block, tile_rows, slice_rows, block)

time: 65.3 us -> 58 us (0.89)
  waiting for transfers between devices: 28.7 us -> 23.4 us
  local copies, waits for them, and re-layouts: 4.66 us -> 1.28 us
  starting transfers between devices: 21.8 us -> 24.4 us
  Pallas kernels: 9.07 us -> 8.08 us
    ppermute x21, waiting for transfers between devices: 28.7 us -> 23.4 us  [move(): return lax.ppermute(value, AXES, pairs)]
    ppermute x21, starting transfers between devices: 21.8 us -> 24.4 us  [move(): return lax.ppermute(value, AXES, pairs)]
    unnamed x10, local copies, waits for them, and re-layouts: 3.55 us -> 1.19 us
    dynamic_slice x1 -> x0, local copies, waits for them, and re-layouts: 1.03 us -> none  [per_device(): kept = lax.dynamic_index_in_dim(by_parity, y, 2, keepdims=False)]
    pallas_call x5 -> x8, Pallas kernels: 9.07 us -> 8.08 us  [call(): pl.pallas_call(kernel, out_shape=outs if last else [pltpu.VMEM(out.shape,...]
  transfers between devices with their start and end apart: 21 -> 21, of which waited for: 7 -> 10; matrix products, arithmetic and copies ran while one was open for 0% -> 0% of each run, Pallas kernels for 9% -> 8%
where the time goes in v3:
time: 58 us; the launch traced here: 57.9 us
  starting transfers between devices  24.4 us (42%)
  waiting for transfers between devices  23.4 us (40%)
  Pallas kernels  8.08 us (14%)
  local copies, waits for them, and re-layouts  1.28 us (2%)
  between operations  0.75 us (1%)
    ppermute x21, starting transfers between devices, move(): return lax.ppermute(value, AXES, pairs)  24.4 us
    ppermute x21, waiting for transfers between devices, move(): return lax.ppermute(value, AXES, pairs)  23.4 us
    pallas_call x8, Pallas kernels, call(): pl.pallas_call(kernel, out_shape=outs if last else [pltpu.VMEM(out.shape,...  8.08 us
    unnamed x10, local copies, waits for them, and re-layouts  1.19 us
  transfers between devices with their start and end apart: 21, of which 10 were waited for; matrix products, arithmetic and copies ran while one was open for 0% of the time, Pallas kernels for 8%

profile of v3, /device:TPU:0, one launch (start us, length us, event | category | flops | bytes accessed | tf_op | source)
XLA Modules:
  0.0 57.9 jit_solution(4193289636691849260)
XLA Ops:
  0.6 3.0 %collective-permute-start = (bf16[2,256,256]{2,1,0:T(8,128)(2,1)}, bf16[2,256,256]{2,1,0:T(8,128)(2,1)S(1)}, u32[]{:S(2)}, u32[]{:S(2)}) collective-permute-start(bf16[2,256,256]{2,1,0:T(8,128)(2,1)} %bitcast.30), channel_id=1, source_target_pairs={{0,1},{1,0},{2,3},{3,2},{4,5},{5,4},{6,7},{7,6},{8,9},{9,8},{10,11... | collective-permute-start | bytes 786440 | tf_op jit(solution)/shard_map/ppermute | solution.py:47
  3.7 3.6 %collective-permute-start.3 = (bf16[4,2,32,256]{3,2,1,0:T(8,128)(2,1)}, bf16[4,2,32,256]{3,2,1,0:T(8,128)(2,1)S(1)}, u32[]{:S(2)}, u32[]{:S(2)}) collective-permute-start(bf16[4,2,32,256]{3,2,1,0:T(8,128)(2,1)} %bitcast.26), channel_id=1, source_target_pairs={{0,6},{1,7},{2,4},{3,5},{4,2},{5,3},{6,0},{7,1},{8,14},{9,15},{10,... | collective-permute-start | bytes 393224 | tf_op jit(solution)/shard_map/ppermute | solution.py:47
  7.3 0.0 collective-permute-start.2
  7.3 0.8 %collective-permute-start.1 = (bf16[4,2,32,256]{3,2,1,0:T(8,128)(2,1)}, bf16[4,2,32,256]{3,2,1,0:T(8,128)(2,1)S(1)}, u32[]{:S(2)}, u32[]{:S(2)}) collective-permute-start(bf16[4,2,32,256]{3,2,1,0:T(8,128)(2,1)} %bitcast.28), channel_id=1, source_target_pairs={{0,2},{1,3},{2,0},{3,1},{4,6},{5,7},{6,4},{7,5},{8,10},{9,11},{10,... | collective-permute-start | bytes 393224 | tf_op jit(solution)/shard_map/ppermute | solution.py:47
  8.1 0.1 stack.35.place_ref
  8.1 0.0 copy-start
  8.1 1.1 %copy-done = bf16[6,256,256]{2,1,0:T(8,128)(2,1)S(1)} copy-done((bf16[6,256,256]{2,1,0:T(8,128)(2,1)S(1)}, bf16[6,256,256]{2,1,0:T(8,128)(2,1)}, u32[]{:S(2)}) %copy-start) | copy-done | bytes 786456
  9.3 0.0 copy-start.4
  9.3 0.0 copy-start.1
  9.3 0.6 %shard_map.68.inverse_ref.refs_4_ = f32[6,256,256]{2,1,0:T(8,128)S(1)} custom-call(bf16[6,256,256]{2,1,0:T(8,128)(2,1)S(1)} %copy-done), custom_call_target="tpu_custom_call" | custom-call | flops 1000000000 | tf_op jit(solution)/shard_map/pallas_call | solution.py:222
  9.9 0.3 collective-permute-done
  10.2 0.0 copy-done.4
  10.2 0.0 copy-start.2
  10.3 0.0 copy-start.3
  10.3 1.8 %collective-permute-start.6 = (bf16[2,256,256]{2,1,0:T(8,128)(2,1)S(1)}, bf16[2,256,256]{2,1,0:T(8,128)(2,1)S(1)}, u32[]{:S(2)}, u32[]{:S(2)}) collective-permute-start(bf16[2,256,256]{2,1,0:T(8,128)(2,1)S(1)} %bitcast.17), channel_id=1, source_target_pairs={{0,2},{1,3},{2,0},{3,1},{4,6},{5,7},{6,4},{7,5},{8,10},{9,11},{10,... | collective-permute-start | bytes 786440 | tf_op jit(solution)/shard_map/ppermute | solution.py:47
  12.1 0.0 copy-done.1
  12.1 1.2 %shard_map.69.refs_4_ = f32[256,128]{1,0:T(8,128)S(1)} custom-call(s32[6]{0:T(128)S(1)} %stack.35.place_ref, f32[6,256,256]{2,1,0:T(8,128)S(1)} %shard_map.68.inverse_ref.refs_4_, bf16[4,256,256]{2,1,0:T(8,128)(2,1)S(1)} %copy-done.1), custom_call_target="tpu_custom_call" | custom-call | flops 3000000000 | tf_op jit(solution)/shard_map/pallas_call | solution.py:222
  13.3 2.6 %collective-permute-start.13 = (bf16[2,256,256]{2,1,0:T(8,128)(2,1)S(1)}, bf16[2,256,256]{2,1,0:T(8,128)(2,1)S(1)}, u32[]{:S(2)}, u32[]{:S(2)}) collective-permute-start(bf16[2,256,256]{2,1,0:T(8,128)(2,1)S(1)} %bitcast.18), channel_id=1, source_target_pairs={{0,6},{1,7},{2,4},{3,5},{4,2},{5,3},{6,0},{7,1},{8,14},{9,15},{10,... | collective-permute-start | bytes 786440 | tf_op jit(solution)/shard_map/ppermute | solution.py:47
  15.9 0.0 collective-permute-done.3.refs_3_
  15.9 3.3 %collective-permute-done.2.refs_2_ = bf16[4,2,32,256]{3,2,1,0:T(8,128)(2,1)S(1)} collective-permute-done((bf16[4,2,32,256]{3,2,1,0:T(8,128)(2,1)}, bf16[4,2,32,256]{3,2,1,0:T(8,128)(2,1)S(1)}, u32[]{:S(2)}, u32[]{:S(2)}) %collective-permute-start.2) | collective-permute-done | bytes 131104 | tf_op jit(solution)/shard_map/ppermute | solution.py:47
  19.3 0.0 collective-permute-done.1.refs_1_
  19.3 0.0 copy-done.2
  19.3 0.0 copy-done.3
  19.3 1.5 %shard_map.70 = (bf16[4,256,256]{2,1,0:T(8,128)(2,1)S(1)}, bf16[4,256,256]{2,1,0:T(8,128)(2,1)S(1)}, bf16[2,256,256]{2,1,0:T(8,128)(2,1)S(1)}) custom-call(s32[6]{0:T(128)S(1)} %stack.35.place_ref, s32[4,8]{1,0:T(4,128)S(1)} %copy-done.3, bf16[4,2,32,256]{3,2,1,0:T(8,128)(2,1)S(1)} %bitcast.29, bf16[4,2,32,256]{3,2,1,0:T(8,128)(2,1)S(1)} %collective-permute-done.1.refs_1_, ...), custom_call_target="tpu_custom_call" | custom-call | flops 2500000000 | tf_op jit(solution)/shard_map/pallas_call | solution.py:222
  20.8 1.6 %collective-permute-start.5 = (bf16[2,2,4,32,256]{4,3,2,1,0:T(8,128)(2,1)S(1)}, bf16[2,2,4,32,256]{4,3,2,1,0:T(8,128)(2,1)S(1)}, u32[]{:S(2)}, u32[]{:S(2)}) collective-permute-start(bf16[2,2,4,32,256]{4,3,2,1,0:T(8,128)(2,1)S(1)} %bitcast.21), channel_id=1, source_target_pairs={{0,16},{1,17},{2,18},{3,19},{4,20},{5,21},{6,22},{7,23},{8,24},{9,... | collective-permute-start | bytes 786440 | tf_op jit(solution)/shard_map/ppermute | solution.py:47
  22.3 0.0 collective-permute-start.4
  22.3 1.0 %collective-permute-done.6.refs_9_ = bf16[2,256,256]{2,1,0:T(8,128)(2,1)S(1)} collective-permute-done((bf16[2,256,256]{2,1,0:T(8,128)(2,1)S(1)}, bf16[2,256,256]{2,1,0:T(8,128)(2,1)S(1)}, u32[]{:S(2)}, u32[]{:S(2)}) %collective-permute-start.6) | collective-permute-done | bytes 262176 | tf_op jit(solution)/shard_map/ppermute | solution.py:47
  23.4 1.2 %collective-permute-start.7 = (bf16[2,2,4,32,256]{4,3,2,1,0:T(8,128)(2,1)S(1)}, bf16[2,2,4,32,256]{4,3,2,1,0:T(8,128)(2,1)S(1)}, u32[]{:S(2)}, u32[]{:S(2)}) collective-permute-start(bf16[2,2,4,32,256]{4,3,2,1,0:T(8,128)(2,1)S(1)} %bitcast.23), channel_id=1, source_target_pairs={{0,17},{1,16},{2,19},{3,18},{4,21},{5,20},{6,23},{7,22},{8,25},{9,... | collective-permute-start | bytes 786440 | tf_op jit(solution)/shard_map/ppermute | solution.py:47
  24.6 1.1 %collective-permute-start.12 = (bf16[2,256,256]{2,1,0:T(8,128)(2,1)S(1)}, bf16[2,256,256]{2,1,0:T(8,128)(2,1)S(1)}, u32[]{:S(2)}, u32[]{:S(2)}) collective-permute-start(bf16[2,256,256]{2,1,0:T(8,128)(2,1)S(1)} %bitcast.19), channel_id=1, source_target_pairs={{0,4},{1,5},{2,6},{3,7},{4,0},{5,1},{6,2},{7,3},{8,12},{9,13},{10,... | collective-permute-start | bytes 786440 | tf_op jit(solution)/shard_map/ppermute | solution.py:47
  25.7 2.7 %collective-permute-done.13.refs_11_ = bf16[2,256,256]{2,1,0:T(8,128)(2,1)S(1)} collective-permute-done((bf16[2,256,256]{2,1,0:T(8,128)(2,1)S(1)}, bf16[2,256,256]{2,1,0:T(8,128)(2,1)S(1)}, u32[]{:S(2)}, u32[]{:S(2)}) %collective-permute-start.13) | collective-permute-done | bytes 262176 | tf_op jit(solution)/shard_map/ppermute | solution.py:47
  28.4 0.0 collective-permute-start.8
  28.4 1.6 %collective-permute-done.5.refs_2_ = bf16[2,2,4,32,256]{4,3,2,1,0:T(8,128)(2,1)S(1)} collective-permute-done((bf16[2,2,4,32,256]{4,3,2,1,0:T(8,128)(2,1)S(1)}, bf16[2,2,4,32,256]{4,3,2,1,0:T(8,128)(2,1)S(1)}, u32[]{:S(2)}, u32[]{:S(2)}) %collective-permute-start.5) | collective-permute-done | bytes 262176 | tf_op jit(solution)/shard_map/ppermute | solution.py:47
  30.0 0.0 collective-permute-start.10
  30.0 4.0 %collective-permute-done.4.refs_1_ = bf16[2,2,4,32,256]{4,3,2,1,0:T(8,128)(2,1)S(1)} collective-permute-done((bf16[2,2,4,32,256]{4,3,2,1,0:T(8,128)(2,1)S(1)}, bf16[2,2,4,32,256]{4,3,2,1,0:T(8,128)(2,1)S(1)}, u32[]{:S(2)}, u32[]{:S(2)}) %collective-permute-start.4) | collective-permute-done | bytes 262176 | tf_op jit(solution)/shard_map/ppermute | solution.py:47
  34.0 0.0 collective-permute-start.9
  34.0 0.0 collective-permute-done.7.refs_3_
  34.0 0.5 collective-permute-start.11
  34.5 6.2 %collective-permute-done.12.refs_10_ = bf16[2,256,256]{2,1,0:T(8,128)(2,1)S(1)} collective-permute-done((bf16[2,256,256]{2,1,0:T(8,128)(2,1)S(1)}, bf16[2,256,256]{2,1,0:T(8,128)(2,1)S(1)}, u32[]{:S(2)}, u32[]{:S(2)}) %collective-permute-start.12) | collective-permute-done | bytes 262176 | tf_op jit(solution)/shard_map/ppermute | solution.py:47
  40.7 0.0 collective-permute-done.8.refs_4_
  40.7 0.0 collective-permute-done.10.refs_6_
  40.7 0.0 collective-permute-done.9.refs_5_
  40.8 0.0 collective-permute-done.11.refs_7_
  40.8 1.5 %shard_map.71 = (f32[2,32,256]{2,1,0:T(8,128)S(1)}, f32[2,32,256]{2,1,0:T(8,128)S(1)}, f32[2,32,256]{2,1,0:T(8,128)S(1)}, f32[2,32,256]{2,1,0:T(8,128)S(1)}, bf1...) custom-call(s32[6]{0:T(128)S(1)} %stack.35.place_ref, s32[4,8]{1,0:T(4,128)S(1)} %copy-done.3, ...), custom_call_target="tpu_custom_call" | custom-call | flops 1700000000 | tf_op jit(solution)/shard_map/pallas_call | solution.py:222
  42.2 1.2 %shard_map.73 = (f32[2,2,256,128]{3,2,1,0:T(8,128)S(1)}, f32[2,2,256,128]{3,2,1,0:T(8,128)S(1)}) custom-call(s32[6]{0:T(128)S(1)} %stack.35.place_ref, bf16[4,256,256]{2,1,0:T(8,128)(2,1)S(1)} %get-tuple-element.30.left_high_ref, bf16[4,256,256]{2,1,0:T(8,128)(2,1)S(1)} %get-tuple-element.31.left_low_ref, bf16[256,256]{1,0:T(8,128)(2,1)S(1)} %get-tuple-element.32.high_ref, ...), custom_call_target="tpu_custom_call" | custom-call | flops 1400000000 | tf_op jit(solution)/shard_map/pallas_call | solution.py:222
  43.5 0.1 collective-permute-start.17
  43.6 0.1 collective-permute-start.14
  43.6 3.0 %collective-permute-start.15 = (f32[2,32,256]{2,1,0:T(8,128)S(1)}, f32[2,32,256]{2,1,0:T(8,128)S(1)}, u32[]{:S(2)}, u32[]{:S(2)}) collective-permute-start(f32[2,32,256]{2,1,0:T(8,128)S(1)} %get-tuple-element.26), channel_id=1, source_target_pairs={{0,4},{1,5},{2,6},{3,7},{4,0},{5,1},{6,2},{7,3},{8,12},{9,13},{10,... | collective-permute-start | bytes 196616 | tf_op jit(solution)/shard_map/ppermute | solution.py:47
  46.7 1.4 %collective-permute-start.16 = (f32[2,32,256]{2,1,0:T(8,128)S(1)}, f32[2,32,256]{2,1,0:T(8,128)S(1)}, u32[]{:S(2)}, u32[]{:S(2)}) collective-permute-start(f32[2,32,256]{2,1,0:T(8,128)S(1)} %get-tuple-element.27), channel_id=1, source_target_pairs={{0,6},{1,7},{2,4},{3,5},{4,2},{5,3},{6,0},{7,1},{8,14},{9,15},{10,... | collective-permute-start | bytes 196616 | tf_op jit(solution)/shard_map/ppermute | solution.py:47
  48.0 0.0 collective-permute-done.17.received_ref
  48.0 0.1 shard_map.74
  48.1 0.6 collective-permute-start.18
  48.6 1.5 %collective-permute-start.19 = (f32[256,128]{1,0:T(8,128)S(1)}, f32[256,128]{1,0:T(8,128)S(1)}, u32[]{:S(2)}, u32[]{:S(2)}) collective-permute-start(f32[256,128]{1,0:T(8,128)S(1)} %get-tuple-element.38), channel_id=1, source_target_pairs={{0,16},{1,17},{2,18},{3,19},{4,20},{5,21},{6,22},{7,23},{8,24},{9,... | collective-permute-start | bytes 393224 | tf_op jit(solution)/shard_map/ppermute | solution.py:47
  50.2 0.0 collective-permute-done.14.refs_1_
  50.2 1.4 %collective-permute-start.20 = (f32[256,128]{1,0:T(8,128)S(1)}, f32[256,128]{1,0:T(8,128)S(1)}, u32[]{:S(2)}, u32[]{:S(2)}) collective-permute-start(f32[256,128]{1,0:T(8,128)S(1)} %get-tuple-element.39), channel_id=1, source_target_pairs={{0,17},{1,16},{2,19},{3,18},{4,21},{5,20},{6,23},{7,22},{8,25},{9,... | collective-permute-start | bytes 393224 | tf_op jit(solution)/shard_map/ppermute | solution.py:47
  51.6 0.0 collective-permute-done.15.refs_2_
  51.6 1.1 %collective-permute-done.16.refs_3_ = f32[2,32,256]{2,1,0:T(8,128)S(1)} collective-permute-done((f32[2,32,256]{2,1,0:T(8,128)S(1)}, f32[2,32,256]{2,1,0:T(8,128)S(1)}, u32[]{:S(2)}, u32[]{:S(2)}) %collective-permute-start.16) | collective-permute-done | bytes 65568 | tf_op jit(solution)/shard_map/ppermute | solution.py:47
  52.8 1.3 %shard_map.72 = (f32[4,2,32,256]{3,2,1,0:T(8,128)}, f32[8,128]{1,0:T(8,128)S(1)}) custom-call(s32[6]{0:T(128)S(1)} %stack.35.place_ref, f32[2,32,256]{2,1,0:T(8,128)S(1)} %get-tuple-element.24.refs_0_, f32[2,32,256]{2,1,0:T(8,128)S(1)} %collective-permute-done.14.refs_1_, f32[2,32,256]{2,1,0:T(8,128)S(1)} %collective-permute-done.15.refs_2_, ...), custom_call_target="tpu_custom_call" | custom-call | flops 12000000000 | tf_op jit(solution)/shard_map/pallas_call | solution.py:222
  54.0 0.0 collective-permute-done.18.refs_1_
  54.0 0.5 collective-permute-done.19.refs_2_
  54.5 2.6 %collective-permute-done.20.refs_3_ = f32[256,128]{1,0:T(8,128)S(1)} collective-permute-done((f32[256,128]{1,0:T(8,128)S(1)}, f32[256,128]{1,0:T(8,128)S(1)}, u32[]{:S(2)}, u32[]{:S(2)}) %collective-permute-start.20) | collective-permute-done | bytes 131104 | tf_op jit(solution)/shard_map/ppermute | solution.py:47
  57.1 0.7 %shard_map.75 = f32[256,128]{1,0:T(8,128)} custom-call(f32[8,128]{1,0:T(8,128)S(1)} %get-tuple-element.29._, f32[256,128]{1,0:T(8,128)S(1)} %get-tuple-element.36.refs_0_, f32[256,128]{1,0:T(8,128)S(1)} %collective-permute-done.18.refs_1_, f32[256,128]{1,0:T(8,128)S(1)} %collective-permute-done.19.refs_2_, f32[256,128]{1,0:T(8,128)S(1)} %collective-permute-done.20.refs_3_, ...), custom_call_target="tpu_custom_call" | custom-call | flops 500000000 | tf_op jit(solution)/shard_map/pallas_call | solution.py:222
  (1 shorter events, 0.0 us)
Async XLA Ops:
  0.6 9.6 %collective-permute-start = (bf16[2,256,256]{2,1,0:T(8,128)(2,1)}, bf16[2,256,256]{2,1,0:T(8,128)(2,1)S(1)}, u32[]{:S(2)}, u32[]{:S(2)}) collective-permute-start(bf16[2,256,256]{2,1,0:T(8,128)(2,1)} %bitcast.30), channel_id=1, source_target_pairs={{0,1},{1,0},{2,3},{3,2},{4,5},{5,4},{6,7},{7,6},{8,9},{9,8},{10,11... | collective-permute-start | bytes 786440 | tf_op jit(solution)/shard_map/ppermute | solution.py:47
  3.7 12.3 %collective-permute-start.3 = (bf16[4,2,32,256]{3,2,1,0:T(8,128)(2,1)}, bf16[4,2,32,256]{3,2,1,0:T(8,128)(2,1)S(1)}, u32[]{:S(2)}, u32[]{:S(2)}) collective-permute-start(bf16[4,2,32,256]{3,2,1,0:T(8,128)(2,1)} %bitcast.26), channel_id=1, source_target_pairs={{0,6},{1,7},{2,4},{3,5},{4,2},{5,3},{6,0},{7,1},{8,14},{9,15},{10,... | collective-permute-start | bytes 393224 | tf_op jit(solution)/shard_map/ppermute | solution.py:47
  7.3 12.0 %collective-permute-start.2 = (bf16[4,2,32,256]{3,2,1,0:T(8,128)(2,1)}, bf16[4,2,32,256]{3,2,1,0:T(8,128)(2,1)S(1)}, u32[]{:S(2)}, u32[]{:S(2)}) collective-permute-start(bf16[4,2,32,256]{3,2,1,0:T(8,128)(2,1)} %bitcast.27), channel_id=1, source_target_pairs={{0,4},{1,5},{2,6},{3,7},{4,0},{5,1},{6,2},{7,3},{8,12},{9,13},{10,... | collective-permute-start | bytes 393224 | tf_op jit(solution)/shard_map/ppermute | solution.py:47
  7.3 12.0 %collective-permute-start.1 = (bf16[4,2,32,256]{3,2,1,0:T(8,128)(2,1)}, bf16[4,2,32,256]{3,2,1,0:T(8,128)(2,1)S(1)}, u32[]{:S(2)}, u32[]{:S(2)}) collective-permute-start(bf16[4,2,32,256]{3,2,1,0:T(8,128)(2,1)} %bitcast.28), channel_id=1, source_target_pairs={{0,2},{1,3},{2,0},{3,1},{4,6},{5,7},{6,4},{7,5},{8,10},{9,11},{10,... | collective-permute-start | bytes 393224 | tf_op jit(solution)/shard_map/ppermute | solution.py:47
  8.1 1.1 %copy-start = (bf16[6,256,256]{2,1,0:T(8,128)(2,1)S(1)}, bf16[6,256,256]{2,1,0:T(8,128)(2,1)}, u32[]{:S(2)}) copy-start(bf16[6,256,256]{2,1,0:T(8,128)(2,1)} %factor_ref.1) | copy-start | bytes 2359300
  9.3 0.9 %copy-start.4 = (bf16[2,1,256,1,1,256]{5,2,4,3,1,0:T(8,128)(2,1)S(1)}, bf16[2,1,256,1,1,256]{5,2,4,3,1,0:T(8,128)(2,1)}, u32[]{:S(2)}) copy-start(bf16[2,1,256,1,1,256]{5,2,4,3,1,0:T(8,128)(2,1)} %param.5) | copy-start | bytes 786436
  9.3 2.8 %copy-start.1 = (bf16[4,256,256]{2,1,0:T(8,128)(2,1)S(1)}, bf16[4,256,256]{2,1,0:T(8,128)(2,1)}, u32[]{:S(2)}) copy-start(bf16[4,256,256]{2,1,0:T(8,128)(2,1)} %diag_ref.1) | copy-start | bytes 1572868
  10.2 9.0 %copy-start.2 = (bf16[4,2,1,32,256]{4,3,2,1,0:T(8,128)(2,1)S(1)}, bf16[4,2,1,32,256]{4,3,2,1,0:T(8,128)(2,1)}, u32[]{:S(2)}) copy-start(bf16[4,2,1,32,256]{4,3,2,1,0:T(8,128)(2,1)} %param.6) | copy-start | bytes 393220
  10.3 9.0 %copy-start.3 = (s32[4,8]{1,0:T(4,128)S(1)}, s32[4,8]{1,0:T(4,128)}, u32[]{:S(2)}) copy-start(s32[4,8]{1,0:T(4,128)} %flags_ref.3) | copy-start | bytes 388
  10.3 13.1 %collective-permute-start.6 = (bf16[2,256,256]{2,1,0:T(8,128)(2,1)S(1)}, bf16[2,256,256]{2,1,0:T(8,128)(2,1)S(1)}, u32[]{:S(2)}, u32[]{:S(2)}) collective-permute-start(bf16[2,256,256]{2,1,0:T(8,128)(2,1)S(1)} %bitcast.17), channel_id=1, source_target_pairs={{0,2},{1,3},{2,0},{3,1},{4,6},{5,7},{6,4},{7,5},{8,10},{9,11},{10,... | collective-permute-start | bytes 786440 | tf_op jit(solution)/shard_map/ppermute | solution.py:47
  13.3 15.1 %collective-permute-start.13 = (bf16[2,256,256]{2,1,0:T(8,128)(2,1)S(1)}, bf16[2,256,256]{2,1,0:T(8,128)(2,1)S(1)}, u32[]{:S(2)}, u32[]{:S(2)}) collective-permute-start(bf16[2,256,256]{2,1,0:T(8,128)(2,1)S(1)} %bitcast.18), channel_id=1, source_target_pairs={{0,6},{1,7},{2,4},{3,5},{4,2},{5,3},{6,0},{7,1},{8,14},{9,15},{10,... | collective-permute-start | bytes 786440 | tf_op jit(solution)/shard_map/ppermute | solution.py:47
  20.8 9.2 %collective-permute-start.5 = (bf16[2,2,4,32,256]{4,3,2,1,0:T(8,128)(2,1)S(1)}, bf16[2,2,4,32,256]{4,3,2,1,0:T(8,128)(2,1)S(1)}, u32[]{:S(2)}, u32[]{:S(2)}) collective-permute-start(bf16[2,2,4,32,256]{4,3,2,1,0:T(8,128)(2,1)S(1)} %bitcast.21), channel_id=1, source_target_pairs={{0,16},{1,17},{2,18},{3,19},{4,20},{5,21},{6,22},{7,23},{8,24},{9,... | collective-permute-start | bytes 786440 | tf_op jit(solution)/shard_map/ppermute | solution.py:47
  22.3 11.7 %collective-permute-start.4 = (bf16[2,2,4,32,256]{4,3,2,1,0:T(8,128)(2,1)S(1)}, bf16[2,2,4,32,256]{4,3,2,1,0:T(8,128)(2,1)S(1)}, u32[]{:S(2)}, u32[]{:S(2)}) collective-permute-start(bf16[2,2,4,32,256]{4,3,2,1,0:T(8,128)(2,1)S(1)} %bitcast.22), channel_id=1, source_target_pairs={{0,1},{1,0},{2,3},{3,2},{4,5},{5,4},{6,7},{7,6},{8,9},{9,8},{10,11... | collective-permute-start | bytes 786440 | tf_op jit(solution)/shard_map/ppermute | solution.py:47
  23.4 10.6 %collective-permute-start.7 = (bf16[2,2,4,32,256]{4,3,2,1,0:T(8,128)(2,1)S(1)}, bf16[2,2,4,32,256]{4,3,2,1,0:T(8,128)(2,1)S(1)}, u32[]{:S(2)}, u32[]{:S(2)}) collective-permute-start(bf16[2,2,4,32,256]{4,3,2,1,0:T(8,128)(2,1)S(1)} %bitcast.23), channel_id=1, source_target_pairs={{0,17},{1,16},{2,19},{3,18},{4,21},{5,20},{6,23},{7,22},{8,25},{9,... | collective-permute-start | bytes 786440 | tf_op jit(solution)/shard_map/ppermute | solution.py:47
  24.6 16.1 %collective-permute-start.12 = (bf16[2,256,256]{2,1,0:T(8,128)(2,1)S(1)}, bf16[2,256,256]{2,1,0:T(8,128)(2,1)S(1)}, u32[]{:S(2)}, u32[]{:S(2)}) collective-permute-start(bf16[2,256,256]{2,1,0:T(8,128)(2,1)S(1)} %bitcast.19), channel_id=1, source_target_pairs={{0,4},{1,5},{2,6},{3,7},{4,0},{5,1},{6,2},{7,3},{8,12},{9,13},{10,... | collective-permute-start | bytes 786440 | tf_op jit(solution)/shard_map/ppermute | solution.py:47
  28.4 12.3 %collective-permute-start.8 = (bf16[2,2,4,32,256]{4,3,2,1,0:T(8,128)(2,1)S(1)}, bf16[2,2,4,32,256]{4,3,2,1,0:T(8,128)(2,1)S(1)}, u32[]{:S(2)}, u32[]{:S(2)}) collective-permute-start(bf16[2,2,4,32,256]{4,3,2,1,0:T(8,128)(2,1)S(1)} %bitcast.24), channel_id=1, source_target_pairs={{0,8},{1,9},{2,10},{3,11},{4,12},{5,13},{6,14},{7,15},{8,0},{9,1},... | collective-permute-start | bytes 786440 | tf_op jit(solution)/shard_map/ppermute | solution.py:47
  30.0 10.8 %collective-permute-start.10 = (bf16[2,2,4,32,256]{4,3,2,1,0:T(8,128)(2,1)S(1)}, bf16[2,2,4,32,256]{4,3,2,1,0:T(8,128)(2,1)S(1)}, u32[]{:S(2)}, u32[]{:S(2)}) collective-permute-start(bf16[2,2,4,32,256]{4,3,2,1,0:T(8,128)(2,1)S(1)} %collective-permute-done.5.refs_2_), channel_id=1, source_target_pairs={{0,8},{1,9},{2,10},{3,11},{4,12},{5,13},{6,14},{7,15},{8,0},{9,1},... | collective-permute-start | bytes 786440 | tf_op jit(solution)/shard_map/ppermute | solution.py:47
  34.0 6.7 %collective-permute-start.9 = (bf16[2,2,4,32,256]{4,3,2,1,0:T(8,128)(2,1)S(1)}, bf16[2,2,4,32,256]{4,3,2,1,0:T(8,128)(2,1)S(1)}, u32[]{:S(2)}, u32[]{:S(2)}) collective-permute-start(bf16[2,2,4,32,256]{4,3,2,1,0:T(8,128)(2,1)S(1)} %collective-permute-done.4.refs_1_), channel_id=1, source_target_pairs={{0,8},{1,9},{2,10},{3,11},{4,12},{5,13},{6,14},{7,15},{8,0},{9,1},... | collective-permute-start | bytes 786440 | tf_op jit(solution)/shard_map/ppermute | solution.py:47
  34.0 6.7 %collective-permute-start.11 = (bf16[2,2,4,32,256]{4,3,2,1,0:T(8,128)(2,1)S(1)}, bf16[2,2,4,32,256]{4,3,2,1,0:T(8,128)(2,1)S(1)}, u32[]{:S(2)}, u32[]{:S(2)}) collective-permute-start(bf16[2,2,4,32,256]{4,3,2,1,0:T(8,128)(2,1)S(1)} %collective-permute-done.7.refs_3_), channel_id=1, source_target_pairs={{0,8},{1,9},{2,10},{3,11},{4,12},{5,13},{6,14},{7,15},{8,0},{9,1},... | collective-permute-start | bytes 786440 | tf_op jit(solution)/shard_map/ppermute | solution.py:47
  43.5 4.5 %collective-permute-start.17 = (f32[2,2,256,128]{3,2,1,0:T(8,128)S(1)}, f32[2,2,256,128]{3,2,1,0:T(8,128)S(1)}, u32[]{:S(2)}, u32[]{:S(2)}) collective-permute-start(f32[2,2,256,128]{3,2,1,0:T(8,128)S(1)} %get-tuple-element.35), channel_id=1, source_target_pairs={{0,8},{1,9},{2,10},{3,11},{4,12},{5,13},{6,14},{7,15},{8,0},{9,1},... | collective-permute-start | bytes 1572872 | tf_op jit(solution)/shard_map/ppermute | solution.py:47
  43.6 6.6 %collective-permute-start.14 = (f32[2,32,256]{2,1,0:T(8,128)S(1)}, f32[2,32,256]{2,1,0:T(8,128)S(1)}, u32[]{:S(2)}, u32[]{:S(2)}) collective-permute-start(f32[2,32,256]{2,1,0:T(8,128)S(1)} %get-tuple-element.25), channel_id=1, source_target_pairs={{0,2},{1,3},{2,0},{3,1},{4,6},{5,7},{6,4},{7,5},{8,10},{9,11},{10,... | collective-permute-start | bytes 196616 | tf_op jit(solution)/shard_map/ppermute | solution.py:47
  43.6 8.0 %collective-permute-start.15 = (f32[2,32,256]{2,1,0:T(8,128)S(1)}, f32[2,32,256]{2,1,0:T(8,128)S(1)}, u32[]{:S(2)}, u32[]{:S(2)}) collective-permute-start(f32[2,32,256]{2,1,0:T(8,128)S(1)} %get-tuple-element.26), channel_id=1, source_target_pairs={{0,4},{1,5},{2,6},{3,7},{4,0},{5,1},{6,2},{7,3},{8,12},{9,13},{10,... | collective-permute-start | bytes 196616 | tf_op jit(solution)/shard_map/ppermute | solution.py:47
  46.7 6.1 %collective-permute-start.16 = (f32[2,32,256]{2,1,0:T(8,128)S(1)}, f32[2,32,256]{2,1,0:T(8,128)S(1)}, u32[]{:S(2)}, u32[]{:S(2)}) collective-permute-start(f32[2,32,256]{2,1,0:T(8,128)S(1)} %get-tuple-element.27), channel_id=1, source_target_pairs={{0,6},{1,7},{2,4},{3,5},{4,2},{5,3},{6,0},{7,1},{8,14},{9,15},{10,... | collective-permute-start | bytes 196616 | tf_op jit(solution)/shard_map/ppermute | solution.py:47
  48.1 6.0 %collective-permute-start.18 = (f32[256,128]{1,0:T(8,128)S(1)}, f32[256,128]{1,0:T(8,128)S(1)}, u32[]{:S(2)}, u32[]{:S(2)}) collective-permute-start(f32[256,128]{1,0:T(8,128)S(1)} %get-tuple-element.37), channel_id=1, source_target_pairs={{0,1},{1,0},{2,3},{3,2},{4,5},{5,4},{6,7},{7,6},{8,9},{9,8},{10,11... | collective-permute-start | bytes 393224 | tf_op jit(solution)/shard_map/ppermute | solution.py:47
  48.6 5.9 %collective-permute-start.19 = (f32[256,128]{1,0:T(8,128)S(1)}, f32[256,128]{1,0:T(8,128)S(1)}, u32[]{:S(2)}, u32[]{:S(2)}) collective-permute-start(f32[256,128]{1,0:T(8,128)S(1)} %get-tuple-element.38), channel_id=1, source_target_pairs={{0,16},{1,17},{2,18},{3,19},{4,20},{5,21},{6,22},{7,23},{8,24},{9,... | collective-permute-start | bytes 393224 | tf_op jit(solution)/shard_map/ppermute | solution.py:47
  50.2 7.0 %collective-permute-start.20 = (f32[256,128]{1,0:T(8,128)S(1)}, f32[256,128]{1,0:T(8,128)S(1)}, u32[]{:S(2)}, u32[]{:S(2)}) collective-permute-start(f32[256,128]{1,0:T(8,128)S(1)} %get-tuple-element.39), channel_id=1, source_target_pairs={{0,17},{1,16},{2,19},{3,18},{4,21},{5,20},{6,23},{7,22},{8,25},{9,... | collective-permute-start | bytes 393224 | tf_op jit(solution)/shard_map/ppermute | solution.py:47

commit v4 on v3

--- a/solution.py
+++ b/solution.py
@@ -36,9 +36,13 @@
     return high, (value - high.astype(jnp.float32)).astype(jnp.bfloat16)
 
 
-def move(value, dx, dc, dz, dy):
+def column_of(line, half):
+    return 4 * (line // 2) + 2 * half + line % 2
+
+
+def move(value, dx, dc, dl, dh):
     prow_count, pcol_count = (lax.axis_size(a) for a in AXES)
-    flip_row, flip_col = 2 * dx + dc, 2 * dz + dy
+    flip_row, flip_col = 2 * dx + dc, column_of(dl, dh)
     pairs = [
         (p * pcol_count + q, (p ^ flip_row) * pcol_count + (q ^ flip_col))
         for p in range(prow_count)
@@ -114,12 +118,12 @@
 def products_kernel(place_ref, flags_ref, *refs, pieces, supernodes, tile_rows, prow_count):
     panel_refs, inverse_ref = refs[:pieces], refs[pieces]
     high_ref, low_ref, *mine_refs, panel_ref = refs[pieces + 1 :]
-    prow, z = place_ref[0], place_ref[4]
+    prow, line = place_ref[0], place_ref[4]
     for later in range(supernodes):
         for r in range(tile_rows):
             keep = flags_ref[later, r * prow_count + prow].astype(jnp.float32)
             for d in range(pieces):
-                panel_ref[later, r, lax.bitwise_xor(z, d)] = (
+                panel_ref[later, r, lax.bitwise_xor(line, d)] = (
                     panel_refs[d][later, r].astype(jnp.float32) * keep
                 )
     rows, width = high_ref.shape[1], high_ref.shape[2]
@@ -132,47 +136,58 @@
                 total = total + dot(narrow[earlier], part)
         high_ref[later], low_ref[later] = split(total)
     for mine_ref in mine_refs:
-        mine_ref[0], mine_ref[1] = high_ref[z], low_ref[z]
-
-
-def columns_kernel(place_ref, flags_ref, *refs, lanes, pieces, prow_count, width, steps):
+        cols_each = width // 2
+        first = line % 2 == 0
+        for which, ref in enumerate((high_ref, low_ref)):
+            for half in range(2):
+                node = ref[column_of(line, half) // 2]
+                mine_ref[which, :, half * cols_each : (half + 1) * cols_each] = jnp.where(
+                    first, node[:, :cols_each], node[:, cols_each:]
+                )
+
+
+def columns_kernel(
+    place_ref, flags_ref, *refs, lanes, pieces, lines, prow_count, width, steps, flips
+):
     lane_refs, sep_refs = refs[:lanes], refs[lanes : lanes + pieces]
-    column_refs = refs[lanes + pieces : lanes + 2 * pieces]
-    high_ref, low_ref, gathered_ref, sums_ref = refs[lanes + 2 * pieces :]
-    prow, x, core, y, z = (place_ref[i] for i in range(5))
-    _, tile_rows, sub_count, slice_rows, block = lane_refs[0].shape
+    column_refs = refs[lanes + pieces : lanes + pieces + lines]
+    high_ref, low_ref, gathered_ref, sums_ref = refs[lanes + pieces + lines :]
+    prow, x, core, half, line, pcol = (place_ref[i] for i in range(6))
+    _, tile_rows, _, slice_rows, block = lane_refs[0].shape
     kind = gathered_ref.dtype
-    for lane, (dx, dc, dy) in enumerate(steps):
+    for lane, (dx, dc, dh) in enumerate(steps):
         lane_prow = 2 * lax.bitwise_xor(x, dx) + lax.bitwise_xor(core, dc)
-        parity = lax.bitwise_xor(y, dy)
-        for half in range(2):
+        lane_half = lax.bitwise_xor(half, dh)
+        for which in range(2):
             for r in range(tile_rows):
-                for sub in range(sub_count):
-                    gathered_ref[half, r * prow_count + lane_prow, 2 * sub + parity] = lane_refs[
-                        lane
-                    ][half, r, sub].astype(kind)
+                for sub in range(lines):
+                    gathered_ref[
+                        which, r * prow_count + lane_prow, column_of(sub, 0) + 2 * lane_half
+                    ] = lane_refs[lane][which, r, sub].astype(kind)
     total = None
-    for d in range(pieces):
-        for dy in range(2):
-            tile = 2 * lax.bitwise_xor(z, d) + lax.bitwise_xor(y, dy)
-            sep = sep_refs[d][dy]
-            for half in range(2):
-                part = gathered_ref[half, tile].reshape(width, block).astype(jnp.bfloat16)
-                term = dot(sep, part)
-                total = term if total is None else total + term
-    later = (z * block) // width
+    for piece, flip in enumerate(flips):
+        tile = lax.bitwise_xor(pcol, flip)
+        sep = sep_refs[piece][...]
+        for which in range(2):
+            part = gathered_ref[which, tile].reshape(width, block).astype(jnp.bfloat16)
+            term = dot(sep, part)
+            total = term if total is None else total + term
+    cols_each = block // 2
+    nodes = [column_of(line, h) * cols_each // width for h in range(2)]
     sums_ref[...] = total.reshape(sums_ref.shape)
-    for d in range(pieces):
-        for r in range(tile_rows):
-            keep = flags_ref[later, r * prow_count + prow].astype(jnp.float32)
-            column_refs[d][r] = sums_ref[r, lax.bitwise_xor(z, d)] * -keep
+    first = lax.broadcasted_iota(jnp.int32, (slice_rows, block), 1) < cols_each
+    for r in range(tile_rows):
+        keeps = [flags_ref[k, r * prow_count + prow].astype(jnp.float32) for k in nodes]
+        keep = jnp.where(first, -keeps[0], -keeps[1])
+        for d in range(lines):
+            column_refs[d][r] = sums_ref[r, lax.bitwise_xor(line, d)] * keep
     high_ref[...], low_ref[...] = split(total)
 
 
 def window_kernel(
     place_ref, left_high_ref, left_low_ref, high_ref, low_ref, keep_ref, send_ref, window_ref
 ):
-    x, core, y = (place_ref[i] for i in range(1, 4))
+    x, core, half = (place_ref[i] for i in range(1, 4))
     supernodes, _, width = left_high_ref.shape
     high, low = high_ref[...], low_ref[...]
     for k in range(supernodes):
@@ -186,8 +201,8 @@
             row_block = 2 * lax.bitwise_xor(x, dx) + lax.bitwise_xor(core, dc)
             rows = window_ref[pl.ds(pl.multiple_of(row_block * rows_each, rows_each), rows_each), :]
             first, second = rows[:, :cols_each], rows[:, cols_each:]
-            target[dx, 0] = jnp.where(y == 0, first, second)
-            target[dx, 1] = jnp.where(y == 0, second, first)
+            target[dx, 0] = jnp.where(half == 0, first, second)
+            target[dx, 1] = jnp.where(half == 0, second, first)
 
 
 def add_kernel(keep_ref, received_ref, *out_refs):
@@ -207,10 +222,25 @@
 
 def ys_kernel(place_ref, *refs):
     *column_refs, ys_ref, done_ref = refs
-    z = place_ref[4]
-    for d, ref in enumerate(column_refs):
-        ys_ref[lax.bitwise_xor(z, d)] = ref[...]
     done_ref[...] = jnp.zeros_like(done_ref)
+    line = place_ref[4]
+    block = column_refs[0].shape[2]
+    cols_each = block // 2
+    if ys_ref.ndim == 4 and ys_ref.shape[0] == len(column_refs) and ys_ref.shape[3] == block:
+        first = line % 2 == 0
+        for d in range(0, len(column_refs), 2):
+            for half in range(2):
+                node = column_of(lax.bitwise_xor(line, d), half) // 2
+                cols = slice(half * cols_each, (half + 1) * cols_each)
+                even, odd = column_refs[d][:, :, cols], column_refs[d + 1][:, :, cols]
+                ys_ref[node, :, :, :cols_each] = jnp.where(first, even, odd)
+                ys_ref[node, :, :, cols_each:] = jnp.where(first, odd, even)
+    else:
+        for d, ref in enumerate(column_refs):
+            for half in range(2):
+                ys_ref[lax.bitwise_xor(line, d), half] = ref[
+                    :, :, half * cols_each : (half + 1) * cols_each
+                ]
 
 
 def after(value, *others):
@@ -233,25 +263,33 @@
 def per_device(sep_inverse, panels, ancestors, window_factor, diag_inverse):
     prow_count, pcol_count = (lax.axis_size(a) for a in AXES)
     prow, pcol = (lax.axis_index(a) for a in AXES)
-    x_count, z_count = prow_count // 2, pcol_count // 2
-    x, core, z, y = prow // 2, prow % 2, pcol // 2, pcol % 2
+    x_count, lines = prow_count // 2, pcol_count // 2
+    x, core, half = prow // 2, prow % 2, pcol // 2 % 2
+    line = 2 * (pcol // 4) + pcol % 2
     tile_rows, width = sep_inverse.shape[0], sep_inverse.shape[2]
     supernodes, slice_rows = panels.shape[0], panels.shape[3]
     order = supernodes * width
-    block = order // z_count
     rows_each, cols_each = order // prow_count, order // pcol_count
-    rows = tile_rows * z_count * slice_rows
+    block = 2 * cols_each
+    rows = tile_rows * lines * slice_rows
     bf16, f32 = jnp.bfloat16, jnp.float32
     shape = jax.ShapeDtypeStruct
-    place = jnp.stack([prow, x, core, y, z, pcol]).astype(jnp.int32)
+    place = jnp.stack([prow, x, core, half, line, pcol]).astype(jnp.int32)
 
     own_panels = panels.reshape(supernodes, tile_rows, slice_rows, width)
-    panel_pieces = [own_panels] + [move(own_panels, 0, 0, d, 0) for d in range(1, z_count)]
-    local_sep = sep_inverse.reshape(tile_rows, width, width)
-    both_sep = jnp.stack([local_sep, move(local_sep, 0, 0, 0, 1)])
-    both_sep = both_sep.reshape(2, tile_rows, z_count, 2, slice_rows, width)
-    own_sep = lax.dynamic_index_in_dim(both_sep, y, 3, keepdims=False).reshape(2, rows, width)
-    sep_pieces = [own_sep] + [move(own_sep, 0, 0, d, 0) for d in range(1, z_count)]
+    panel_pieces = []
+    for dl in range(0, lines, 2):
+        piece = own_panels if dl == 0 else move(own_panels, 0, 0, dl, 0)
+        panel_pieces += [piece, move(piece, 0, 0, 1, 0)]
+    by_half = sep_inverse.reshape(tile_rows, lines // 2, 2, 2, slice_rows, width)
+    kept = lax.dynamic_index_in_dim(by_half, half, 2, keepdims=False).reshape(rows, width)
+    given = lax.dynamic_index_in_dim(by_half, 1 - half, 2, keepdims=False).reshape(rows, width)
+    sep_pieces, flips = [], []
+    for dl in range(0, lines, 2):
+        for dh in range(2):
+            piece = kept if dl + dh == 0 else move((kept, given)[dh], 0, 0, dl, dh)
+            sep_pieces += [piece, move(piece, 0, 0, 1, 0)]
+            flips += [column_of(dl, dh), column_of(dl + 1, dh)]
 
     (stacked,) = call(
         functools.partial(inverse_kernel, supernodes=supernodes),
@@ -276,56 +314,62 @@
     high, low, *mine = call(
         functools.partial(
             products_kernel,
-            pieces=z_count,
+            pieces=lines,
             supernodes=supernodes,
             tile_rows=tile_rows,
             prow_count=prow_count,
         ),
-        [after(place, own_sep, own_window), ancestors, *panel_pieces, stacked],
+        [after(place, own_window, sep_pieces[1], sep_pieces[3]), ancestors, *panel_pieces, stacked],
         2,
         [shape((supernodes, rows, width), bf16)] * 2
-        + [shape((2, rows, width), bf16)] * (block == width),
-        [pltpu.VMEM((supernodes, tile_rows, z_count, slice_rows, width), f32)],
+        + [shape((2, rows, block), bf16)] * (block == width),
+        [pltpu.VMEM((supernodes, tile_rows, lines, slice_rows, width), f32)],
         cost=2_500_000_000,
     )
     if block == width:
         mine = mine[0]
     else:
         both = jnp.stack([high, low])
-        chosen = lax.dynamic_index_in_dim(both, (z * block) // width, 1, keepdims=False)
-        mine = lax.dynamic_slice_in_dim(chosen, (z * block) % width, block, 2)
-    mine = mine.reshape(2, tile_rows, z_count, slice_rows, block)
+        slices = []
+        for h in range(2):
+            start = column_of(line, h) * cols_each
+            chosen = lax.dynamic_index_in_dim(both, start // width, 1, keepdims=False)
+            slices.append(lax.dynamic_slice_in_dim(chosen, start % width, cols_each, 2))
+        mine = jnp.concatenate(slices, 2)
+    mine = mine.reshape(2, tile_rows, lines, slice_rows, block)
     steps, lanes = [], []
     for dx in range(x_count):
-        for dy in range(2):
-            source = after(mine, sep_pieces[1]) if dx + dy == 2 else mine
-            lane = mine if dx + dy == 0 else move(source, dx, 0, 0, dy)
+        for dh in range(2):
+            lane = mine if dx + dh == 0 else move(mine, dx, 0, 0, dh)
             lanes.append(lane)
-            steps.append((dx, 0, dy))
-    for (dx, _, dy), lane in zip(list(steps), list(lanes)):
+            steps.append((dx, 0, dh))
+    lanes[1:] = [after(lane, *sep_pieces[1:]) for lane in lanes[1:]]
+    for (dx, _, dh), lane in zip(list(steps), list(lanes)):
         lanes.append(move(lane, 0, 1, 0, 0))
-        steps.append((dx, 1, dy))
+        steps.append((dx, 1, dh))
 
     kind = bf16 if slice_rows % 16 == 0 else f32
     *columns, sums_high, sums_low = call(
         functools.partial(
             columns_kernel,
             lanes=len(lanes),
-            pieces=z_count,
+            pieces=len(sep_pieces),
+            lines=lines,
             prow_count=prow_count,
             width=width,
             steps=tuple(steps),
+            flips=tuple(flips),
         ),
         [place, ancestors, *lanes, *sep_pieces],
         2,
-        [shape((tile_rows, slice_rows, block), f32)] * z_count + [shape((rows, block), bf16)] * 2,
+        [shape((tile_rows, slice_rows, block), f32)] * lines + [shape((rows, block), bf16)] * 2,
         [
             pltpu.VMEM((2, tile_rows * prow_count, pcol_count, slice_rows, block), kind),
-            pltpu.VMEM((tile_rows, z_count, slice_rows, block), f32),
+            pltpu.VMEM((tile_rows, lines, slice_rows, block), f32),
         ],
         cost=1_700_000_000,
     )
-    column_pieces = [columns[0]] + [move(columns[d], 0, 0, d, 0) for d in range(1, z_count)]
+    column_pieces = [columns[0]] + [move(columns[d], 0, 0, d, 0) for d in range(1, lines)]
     keep, send = call(
         window_kernel,
         [place, high, low, sums_high, sums_low],
@@ -343,21 +387,32 @@
         [],
         cost=100_000_000,
     )
-    summed = [parts[0]] + [
-        move(parts[2 * dx + dy], dx, 0, 0, dy)
-        for dx in range(x_count)
-        for dy in range(2)
-        if dx + dy > 0
-    ]
+    by_node = block == width and lines == supernodes
     ys, done = call(
         ys_kernel,
         [place, *column_pieces],
         1,
-        [shape((z_count, tile_rows, slice_rows, block), f32), shape((8, 128), f32)],
+        [
+            shape((supernodes, tile_rows, slice_rows, width), f32)
+            if by_node
+            else shape((lines, 2, tile_rows, slice_rows, cols_each), f32),
+            shape((8, 128), f32),
+        ],
         [],
         cost=12_000_000_000,
-        last=True,
-    )
+        last=by_node,
+    )
+    if not by_node:
+        ys = ys.reshape(lines // 2, 2, 2, tile_rows, slice_rows, cols_each)
+        ys = jnp.transpose(ys, (3, 4, 0, 2, 1, 5))
+        ys = ys.reshape(tile_rows, slice_rows, supernodes, width)
+        ys = jnp.transpose(ys, (2, 0, 1, 3))
+    summed = [parts[0]] + [
+        move(parts[2 * dx + dh], dx, 0, 0, dh)
+        for dx in range(x_count)
+        for dh in range(2)
+        if dx + dh > 0
+    ]
     (window,) = call(
         last_kernel,
         [done, *summed, own_window],
@@ -367,9 +422,6 @@
         cost=500_000_000,
         last=True,
     )
-    if block != width:
-        ys = ys.reshape(supernodes, width // block, tile_rows, slice_rows, block)
-        ys = jnp.transpose(ys, (0, 2, 3, 1, 4))
     return ys.reshape(supernodes, tile_rows, 1, slice_rows, width), window
 
 

time: 58 us -> 56.5 us (0.974)
  waiting for transfers between devices: 23.4 us -> 19.8 us
  starting transfers between devices: 24.4 us -> 25.5 us
  local copies, waits for them, and re-layouts: 1.28 us -> 2.22 us
    ppermute x21 -> x24, waiting for transfers between devices: 23.4 us -> 19.8 us  [move(): return lax.ppermute(value, AXES, pairs)]
    ppermute x21 -> x24, starting transfers between devices: 24.4 us -> 25.5 us  [move(): return lax.ppermute(value, AXES, pairs)]
    dynamic_slice x0 -> x1, local copies, waits for them, and re-layouts: none -> 0.99 us  [per_device(): lax.dynamic_index_in_dim(by_half, 1 - half, 2, keepdims=False)]
    unnamed x10 -> x8, local copies, waits for them, and re-layouts: 1.19 us -> 1.15 us
  transfers between devices with their start and end apart: 21 -> 24, of which waited for: 10 -> 13; matrix products, arithmetic and copies ran while one was open for 0% -> 2% of each run, Pallas kernels for 8% -> 8%
where the time goes in v4:
time: 56.5 us; the launch traced here: 56.3 us
  starting transfers between devices  25.5 us (45%)
  waiting for transfers between devices  19.8 us (35%)
  Pallas kernels  8.12 us (14%)
  local copies, waits for them, and re-layouts  2.22 us (4%)
  between operations  0.73 us (1%)
    ppermute x24, starting transfers between devices, move(): return lax.ppermute(value, AXES, pairs)  25.5 us
    ppermute x24, waiting for transfers between devices, move(): return lax.ppermute(value, AXES, pairs)  19.8 us
    pallas_call x8, Pallas kernels, call(): pl.pallas_call(kernel, out_shape=outs if last else [pltpu.VMEM(out.shape,...  8.12 us
    unnamed x8, local copies, waits for them, and re-layouts  1.15 us
  transfers between devices with their start and end apart: 24, of which 13 were waited for; matrix products, arithmetic and copies ran while one was open for 2% of the time, Pallas kernels for 8%

profile of v4, /device:TPU:0, one launch (start us, length us, event | category | flops | bytes accessed | tf_op | source)
XLA Modules:
  0.0 56.3 jit_solution(17591859296305187397)
XLA Ops:
  0.6 4.1 %collective-permute-start.4 = (bf16[4,2,32,256]{3,2,1,0:T(8,128)(2,1)}, bf16[4,2,32,256]{3,2,1,0:T(8,128)(2,1)S(1)}, u32[]{:S(2)}, u32[]{:S(2)}) collective-permute-start(bf16[4,2,32,256]{3,2,1,0:T(8,128)(2,1)} %bitcast.26), channel_id=1, source_target_pairs={{0,4},{1,5},{2,6},{3,7},{4,0},{5,1},{6,2},{7,3},{8,12},{9,13},{10,... | collective-permute-start | bytes 393224 | tf_op jit(solution)/shard_map/ppermute | solution.py:51
  4.7 1.0 %constant_dynamic-slice_fusion = (bf16[2,2,1,2,32,256]{5,4,3,2,1,0:T(8,128)(2,1)S(1)}, bf16[2,2,1,2,32,256]{5,4,3,2,1,0:T(8,128)(2,1)S(1)}) fusion(bf16[2,2,2,2,32,256]{5,4,3,2,1,0:T(8,128)(2,1)} %bitcast.29, s32[]{:T(128)S(6)} %select_n.39, s32[]{:T(128)S(6)} %select_n.38), kind=kLoop, calls=%fused_computation | loop fusion | bytes 524296 | tf_op jit(solution)/shard_map/jit(dynamic_index_in_dim)/dynamic_slice | solution.py:286
  5.7 1.6 %collective-permute-start.1 = (bf16[256,256]{1,0:T(8,128)(2,1)S(1)}, bf16[256,256]{1,0:T(8,128)(2,1)S(1)}, u32[]{:S(2)}, u32[]{:S(2)}) collective-permute-start(bf16[256,256]{1,0:T(8,128)(2,1)S(1)} %bitcast.30), channel_id=1, source_target_pairs={{0,2},{1,3},{2,0},{3,1},{4,6},{5,7},{6,4},{7,5},{8,10},{9,11},{10,... | collective-permute-start | bytes 393224 | tf_op jit(solution)/shard_map/ppermute | solution.py:51
  7.4 1.5 %collective-permute-start.3 = (bf16[4,2,32,256]{3,2,1,0:T(8,128)(2,1)}, bf16[4,2,32,256]{3,2,1,0:T(8,128)(2,1)S(1)}, u32[]{:S(2)}, u32[]{:S(2)}) collective-permute-start(bf16[4,2,32,256]{3,2,1,0:T(8,128)(2,1)} %bitcast.27), channel_id=1, source_target_pairs={{0,1},{1,0},{2,3},{3,2},{4,5},{5,4},{6,7},{7,6},{8,9},{9,8},{10,11... | collective-permute-start | bytes 393224 | tf_op jit(solution)/shard_map/ppermute | solution.py:51
  8.9 0.2 collective-permute-start.9
  9.1 0.3 collective-permute-start
  9.4 0.1 stack.27.place_ref
  9.5 1.1 %copy-done = bf16[6,256,256]{2,1,0:T(8,128)(2,1)S(1)} copy-done((bf16[6,256,256]{2,1,0:T(8,128)(2,1)S(1)}, bf16[6,256,256]{2,1,0:T(8,128)(2,1)}, u32[]{:S(2)}) %copy-start) | copy-done | bytes 786456
  10.6 0.6 %shard_map.68.inverse_ref.refs_4_ = f32[6,256,256]{2,1,0:T(8,128)S(1)} custom-call(bf16[6,256,256]{2,1,0:T(8,128)(2,1)S(1)} %copy-done), custom_call_target="tpu_custom_call" | custom-call | flops 1000000000 | tf_op jit(solution)/shard_map/pallas_call | solution.py:252
  11.2 0.0 copy-start.2
  11.3 0.0 copy-start.3
  11.3 0.7 %collective-permute-done.4.refs_2_ = bf16[4,2,32,256]{3,2,1,0:T(8,128)(2,1)S(1)} collective-permute-done((bf16[4,2,32,256]{3,2,1,0:T(8,128)(2,1)}, bf16[4,2,32,256]{3,2,1,0:T(8,128)(2,1)S(1)}, u32[]{:S(2)}, u32[]{:S(2)}) %collective-permute-start.4) | collective-permute-done | bytes 131104 | tf_op jit(solution)/shard_map/ppermute | solution.py:51
  11.9 3.1 %collective-permute-start.5 = (bf16[4,2,32,256]{3,2,1,0:T(8,128)(2,1)S(1)}, bf16[4,2,32,256]{3,2,1,0:T(8,128)(2,1)S(1)}, u32[]{:S(2)}, u32[]{:S(2)}) collective-permute-start(bf16[4,2,32,256]{3,2,1,0:T(8,128)(2,1)S(1)} %collective-permute-done.4.refs_2_), channel_id=1, source_target_pairs={{0,1},{1,0},{2,3},{3,2},{4,5},{5,4},{6,7},{7,6},{8,9},{9,8},{10,11... | collective-permute-start | bytes 393224 | tf_op jit(solution)/shard_map/ppermute | solution.py:51
  15.0 0.0 collective-permute-done.1.refs_10_
  15.0 0.0 collective-permute-start.2
  15.0 0.0 copy-done.1
  15.0 1.2 %shard_map.69.refs_4_ = f32[256,128]{1,0:T(8,128)S(1)} custom-call(s32[6]{0:T(128)S(1)} %stack.27.place_ref, f32[6,256,256]{2,1,0:T(8,128)S(1)} %shard_map.68.inverse_ref.refs_4_, bf16[4,256,256]{2,1,0:T(8,128)(2,1)S(1)} %copy-done.1), custom_call_target="tpu_custom_call" | custom-call | flops 3000000000 | tf_op jit(solution)/shard_map/pallas_call | solution.py:252
  16.2 0.6 %collective-permute-done.refs_9_ = bf16[256,256]{1,0:T(8,128)(2,1)S(1)} collective-permute-done((bf16[256,256]{1,0:T(8,128)(2,1)S(1)}, bf16[256,256]{1,0:T(8,128)(2,1)S(1)}, u32[]{:S(2)}, u32[]{:S(2)}) %collective-permute-start) | collective-permute-done | bytes 131104 | tf_op jit(solution)/shard_map/ppermute | solution.py:51
  16.8 0.3 collective-permute-start.7
  17.2 3.5 %collective-permute-done.2.refs_11_ = bf16[256,256]{1,0:T(8,128)(2,1)S(1)} collective-permute-done((bf16[256,256]{1,0:T(8,128)(2,1)S(1)}, bf16[256,256]{1,0:T(8,128)(2,1)S(1)}, u32[]{:S(2)}, u32[]{:S(2)}) %collective-permute-start.2) | collective-permute-done | bytes 131104 | tf_op jit(solution)/shard_map/ppermute | solution.py:51
  20.7 0.0 collective-permute-done.3.refs_1_
  20.7 0.0 collective-permute-done.5.refs_3_
  20.7 0.0 copy-done.2
  20.7 0.0 copy-done.3
  20.7 1.5 %shard_map.70 = (bf16[4,256,256]{2,1,0:T(8,128)(2,1)S(1)}, bf16[4,256,256]{2,1,0:T(8,128)(2,1)S(1)}, bf16[2,256,256]{2,1,0:T(8,128)(2,1)S(1)}) custom-call(s32[6]{0:T(128)S(1)} %stack.27.place_ref, s32[4,8]{1,0:T(4,128)S(1)} %copy-done.3, bf16[4,2,32,256]{3,2,1,0:T(8,128)(2,1)S(1)} %bitcast.28, bf16[4,2,32,256]{3,2,1,0:T(8,128)(2,1)S(1)} %collective-permute-done.3.refs_1_, ...), custom_call_target="tpu_custom_call" | custom-call | flops 2500000000 | tf_op jit(solution)/shard_map/pallas_call | solution.py:252
  22.3 1.4 %collective-permute-start.12 = (bf16[2,2,4,32,256]{4,3,2,1,0:T(8,128)(2,1)S(1)}, bf16[2,2,4,32,256]{4,3,2,1,0:T(8,128)(2,1)S(1)}, u32[]{:S(2)}, u32[]{:S(2)}) collective-permute-start(bf16[2,2,4,32,256]{4,3,2,1,0:T(8,128)(2,1)S(1)} %bitcast.21), channel_id=1, source_target_pairs={{0,18},{1,19},{2,16},{3,17},{4,22},{5,23},{6,20},{7,21},{8,26},{9,... | collective-permute-start | bytes 786440 | tf_op jit(solution)/shard_map/ppermute | solution.py:51
  23.7 0.5 collective-permute-start.11
  24.2 1.6 %collective-permute-start.6 = (bf16[2,2,4,32,256]{4,3,2,1,0:T(8,128)(2,1)S(1)}, bf16[2,2,4,32,256]{4,3,2,1,0:T(8,128)(2,1)S(1)}, u32[]{:S(2)}, u32[]{:S(2)}) collective-permute-start(bf16[2,2,4,32,256]{4,3,2,1,0:T(8,128)(2,1)S(1)} %bitcast.23), channel_id=1, source_target_pairs={{0,2},{1,3},{2,0},{3,1},{4,6},{5,7},{6,4},{7,5},{8,10},{9,11},{10,... | collective-permute-start | bytes 786440 | tf_op jit(solution)/shard_map/ppermute | solution.py:51
  25.8 0.0 collective-permute-done.9.refs_14_
  25.8 1.5 %collective-permute-start.10 = (bf16[256,256]{1,0:T(8,128)(2,1)S(1)}, bf16[256,256]{1,0:T(8,128)(2,1)S(1)}, u32[]{:S(2)}, u32[]{:S(2)}) collective-permute-start(bf16[256,256]{1,0:T(8,128)(2,1)S(1)} %collective-permute-done.9.refs_14_), channel_id=1, source_target_pairs={{0,1},{1,0},{2,3},{3,2},{4,5},{5,4},{6,7},{7,6},{8,9},{9,8},{10,11... | collective-permute-start | bytes 393224 | tf_op jit(solution)/shard_map/ppermute | solution.py:51
  27.3 0.0 collective-permute-done.7.refs_12_
  27.3 0.5 collective-permute-start.8
  27.8 2.9 %collective-permute-done.10.refs_15_ = bf16[256,256]{1,0:T(8,128)(2,1)S(1)} collective-permute-done((bf16[256,256]{1,0:T(8,128)(2,1)S(1)}, bf16[256,256]{1,0:T(8,128)(2,1)S(1)}, u32[]{:S(2)}, u32[]{:S(2)}) %collective-permute-start.10) | collective-permute-done | bytes 131104 | tf_op jit(solution)/shard_map/ppermute | solution.py:51
  30.8 0.0 collective-permute-start.13
  30.8 1.5 %collective-permute-done.8.refs_13_ = bf16[256,256]{1,0:T(8,128)(2,1)S(1)} collective-permute-done((bf16[256,256]{1,0:T(8,128)(2,1)S(1)}, bf16[256,256]{1,0:T(8,128)(2,1)S(1)}, u32[]{:S(2)}, u32[]{:S(2)}) %collective-permute-start.8) | collective-permute-done | bytes 131104 | tf_op jit(solution)/shard_map/ppermute | solution.py:51
  32.3 0.2 collective-permute-done.12.refs_3_
  32.5 0.0 collective-permute-start.16
  32.5 3.3 %collective-permute-done.11.refs_2_ = bf16[2,2,4,32,256]{4,3,2,1,0:T(8,128)(2,1)S(1)} collective-permute-done((bf16[2,2,4,32,256]{4,3,2,1,0:T(8,128)(2,1)S(1)}, bf16[2,2,4,32,256]{4,3,2,1,0:T(8,128)(2,1)S(1)}, u32[]{:S(2)}, u32[]{:S(2)}) %collective-permute-start.11) | collective-permute-done | bytes 262176 | tf_op jit(solution)/shard_map/ppermute | solution.py:51
  35.8 0.0 collective-permute-start.15
  35.8 0.0 collective-permute-done.6.refs_1_
  35.8 0.5 collective-permute-start.14
  36.3 0.0 collective-permute-done.13.refs_4_
  36.3 0.0 collective-permute-done.16.refs_7_
  36.3 1.0 %collective-permute-done.15.refs_6_ = bf16[2,2,4,32,256]{4,3,2,1,0:T(8,128)(2,1)S(1)} collective-permute-done((bf16[2,2,4,32,256]{4,3,2,1,0:T(8,128)(2,1)S(1)}, bf16[2,2,4,32,256]{4,3,2,1,0:T(8,128)(2,1)S(1)}, u32[]{:S(2)}, u32[]{:S(2)}) %collective-permute-start.15) | collective-permute-done | bytes 262176 | tf_op jit(solution)/shard_map/ppermute | solution.py:51
  37.3 0.4 collective-permute-done.14.refs_5_
  37.7 1.4 %shard_map.71 = (f32[2,32,256]{2,1,0:T(8,128)S(1)}, f32[2,32,256]{2,1,0:T(8,128)S(1)}, f32[2,32,256]{2,1,0:T(8,128)S(1)}, f32[2,32,256]{2,1,0:T(8,128)S(1)}, bf1...) custom-call(s32[6]{0:T(128)S(1)} %stack.27.place_ref, s32[4,8]{1,0:T(4,128)S(1)} %copy-done.3, ...), custom_call_target="tpu_custom_call" | custom-call | flops 1700000000 | tf_op jit(solution)/shard_map/pallas_call | solution.py:252
  39.1 1.2 %shard_map.73 = (f32[2,2,256,128]{3,2,1,0:T(8,128)S(1)}, f32[2,2,256,128]{3,2,1,0:T(8,128)S(1)}) custom-call(s32[6]{0:T(128)S(1)} %stack.27.place_ref, bf16[4,256,256]{2,1,0:T(8,128)(2,1)S(1)} %get-tuple-element.34.left_high_ref, bf16[4,256,256]{2,1,0:T(8,128)(2,1)S(1)} %get-tuple-element.35.left_low_ref, bf16[256,256]{1,0:T(8,128)(2,1)S(1)} %get-tuple-element.36.high_ref, ...), custom_call_target="tpu_custom_call" | custom-call | flops 1400000000 | tf_op jit(solution)/shard_map/pallas_call | solution.py:252
  40.4 0.2 collective-permute-start.20
  40.6 1.3 %collective-permute-start.17 = (f32[2,32,256]{2,1,0:T(8,128)S(1)}, f32[2,32,256]{2,1,0:T(8,128)S(1)}, u32[]{:S(2)}, u32[]{:S(2)}) collective-permute-start(f32[2,32,256]{2,1,0:T(8,128)S(1)} %get-tuple-element.29), channel_id=1, source_target_pairs={{0,1},{1,0},{2,3},{3,2},{4,5},{5,4},{6,7},{7,6},{8,9},{9,8},{10,11... | collective-permute-start | bytes 196616 | tf_op jit(solution)/shard_map/ppermute | solution.py:51
  41.9 2.2 %collective-permute-start.18 = (f32[2,32,256]{2,1,0:T(8,128)S(1)}, f32[2,32,256]{2,1,0:T(8,128)S(1)}, u32[]{:S(2)}, u32[]{:S(2)}) collective-permute-start(f32[2,32,256]{2,1,0:T(8,128)S(1)} %get-tuple-element.30), channel_id=1, source_target_pairs={{0,4},{1,5},{2,6},{3,7},{4,0},{5,1},{6,2},{7,3},{8,12},{9,13},{10,... | collective-permute-start | bytes 196616 | tf_op jit(solution)/shard_map/ppermute | solution.py:51
  44.2 0.8 %collective-permute-start.19 = (f32[2,32,256]{2,1,0:T(8,128)S(1)}, f32[2,32,256]{2,1,0:T(8,128)S(1)}, u32[]{:S(2)}, u32[]{:S(2)}) collective-permute-start(f32[2,32,256]{2,1,0:T(8,128)S(1)} %get-tuple-element.31), channel_id=1, source_target_pairs={{0,5},{1,4},{2,7},{3,6},{4,1},{5,0},{6,3},{7,2},{8,13},{9,12},{10,... | collective-permute-start | bytes 196616 | tf_op jit(solution)/shard_map/ppermute | solution.py:51
  45.0 0.0 collective-permute-done.20.received_ref
  45.0 0.1 shard_map.74
  45.0 1.1 %collective-permute-start.21 = (f32[256,128]{1,0:T(8,128)S(1)}, f32[256,128]{1,0:T(8,128)S(1)}, u32[]{:S(2)}, u32[]{:S(2)}) collective-permute-start(f32[256,128]{1,0:T(8,128)S(1)} %get-tuple-element.41), channel_id=1, source_target_pairs={{0,2},{1,3},{2,0},{3,1},{4,6},{5,7},{6,4},{7,5},{8,10},{9,11},{10,... | collective-permute-start | bytes 393224 | tf_op jit(solution)/shard_map/ppermute | solution.py:51
  46.2 0.9 %collective-permute-start.22 = (f32[256,128]{1,0:T(8,128)S(1)}, f32[256,128]{1,0:T(8,128)S(1)}, u32[]{:S(2)}, u32[]{:S(2)}) collective-permute-start(f32[256,128]{1,0:T(8,128)S(1)} %get-tuple-element.42), channel_id=1, source_target_pairs={{0,16},{1,17},{2,18},{3,19},{4,20},{5,21},{6,22},{7,23},{8,24},{9,... | collective-permute-start | bytes 393224 | tf_op jit(solution)/shard_map/ppermute | solution.py:51
  47.0 0.0 collective-permute-done.17.refs_1_
  47.1 1.6 %collective-permute-start.23 = (f32[256,128]{1,0:T(8,128)S(1)}, f32[256,128]{1,0:T(8,128)S(1)}, u32[]{:S(2)}, u32[]{:S(2)}) collective-permute-start(f32[256,128]{1,0:T(8,128)S(1)} %get-tuple-element.43), channel_id=1, source_target_pairs={{0,18},{1,19},{2,16},{3,17},{4,22},{5,23},{6,20},{7,21},{8,26},{9,... | collective-permute-start | bytes 393224 | tf_op jit(solution)/shard_map/ppermute | solution.py:51
  48.6 1.0 %collective-permute-done.18.refs_2_ = f32[2,32,256]{2,1,0:T(8,128)S(1)} collective-permute-done((f32[2,32,256]{2,1,0:T(8,128)S(1)}, f32[2,32,256]{2,1,0:T(8,128)S(1)}, u32[]{:S(2)}, u32[]{:S(2)}) %collective-permute-start.18) | collective-permute-done | bytes 65568 | tf_op jit(solution)/shard_map/ppermute | solution.py:51
  49.6 1.2 %collective-permute-done.19.refs_3_ = f32[2,32,256]{2,1,0:T(8,128)S(1)} collective-permute-done((f32[2,32,256]{2,1,0:T(8,128)S(1)}, f32[2,32,256]{2,1,0:T(8,128)S(1)}, u32[]{:S(2)}, u32[]{:S(2)}) %collective-permute-start.19) | collective-permute-done | bytes 65568 | tf_op jit(solution)/shard_map/ppermute | solution.py:51
  50.8 1.3 %shard_map.72 = (f32[4,2,32,256]{3,2,1,0:T(8,128)}, f32[8,128]{1,0:T(8,128)S(1)}) custom-call(s32[6]{0:T(128)S(1)} %stack.27.place_ref, f32[2,32,256]{2,1,0:T(8,128)S(1)} %get-tuple-element.28.refs_0_, f32[2,32,256]{2,1,0:T(8,128)S(1)} %collective-permute-done.17.refs_1_, f32[2,32,256]{2,1,0:T(8,128)S(1)} %collective-permute-done.18.refs_2_, ...), custom_call_target="tpu_custom_call" | custom-call | flops 12000000000 | tf_op jit(solution)/shard_map/pallas_call | solution.py:252
  52.1 0.8 %collective-permute-done.21.refs_1_ = f32[256,128]{1,0:T(8,128)S(1)} collective-permute-done((f32[256,128]{1,0:T(8,128)S(1)}, f32[256,128]{1,0:T(8,128)S(1)}, u32[]{:S(2)}, u32[]{:S(2)}) %collective-permute-start.21) | collective-permute-done | bytes 131104 | tf_op jit(solution)/shard_map/ppermute | solution.py:51
  52.9 0.0 collective-permute-done.22.refs_2_
  52.9 2.7 %collective-permute-done.23.refs_3_ = f32[256,128]{1,0:T(8,128)S(1)} collective-permute-done((f32[256,128]{1,0:T(8,128)S(1)}, f32[256,128]{1,0:T(8,128)S(1)}, u32[]{:S(2)}, u32[]{:S(2)}) %collective-permute-start.23) | collective-permute-done | bytes 131104 | tf_op jit(solution)/shard_map/ppermute | solution.py:51
  55.6 0.7 %shard_map.75 = f32[256,128]{1,0:T(8,128)} custom-call(f32[8,128]{1,0:T(8,128)S(1)} %get-tuple-element.33._, f32[256,128]{1,0:T(8,128)S(1)} %get-tuple-element.40.refs_0_, f32[256,128]{1,0:T(8,128)S(1)} %collective-permute-done.21.refs_1_, f32[256,128]{1,0:T(8,128)S(1)} %collective-permute-done.22.refs_2_, f32[256,128]{1,0:T(8,128)S(1)} %collective-permute-done.23.refs_3_, ...), custom_call_target="tpu_custom_call" | custom-call | flops 500000000 | tf_op jit(solution)/shard_map/pallas_call | solution.py:252
  (2 shorter events, 0.0 us)
Async XLA Ops:
  0.6 11.3 %collective-permute-start.4 = (bf16[4,2,32,256]{3,2,1,0:T(8,128)(2,1)}, bf16[4,2,32,256]{3,2,1,0:T(8,128)(2,1)S(1)}, u32[]{:S(2)}, u32[]{:S(2)}) collective-permute-start(bf16[4,2,32,256]{3,2,1,0:T(8,128)(2,1)} %bitcast.26), channel_id=1, source_target_pairs={{0,4},{1,5},{2,6},{3,7},{4,0},{5,1},{6,2},{7,3},{8,12},{9,13},{10,... | collective-permute-start | bytes 393224 | tf_op jit(solution)/shard_map/ppermute | solution.py:51
  5.7 9.3 %collective-permute-start.1 = (bf16[256,256]{1,0:T(8,128)(2,1)S(1)}, bf16[256,256]{1,0:T(8,128)(2,1)S(1)}, u32[]{:S(2)}, u32[]{:S(2)}) collective-permute-start(bf16[256,256]{1,0:T(8,128)(2,1)S(1)} %bitcast.30), channel_id=1, source_target_pairs={{0,2},{1,3},{2,0},{3,1},{4,6},{5,7},{6,4},{7,5},{8,10},{9,11},{10,... | collective-permute-start | bytes 393224 | tf_op jit(solution)/shard_map/ppermute | solution.py:51
  7.4 13.3 %collective-permute-start.3 = (bf16[4,2,32,256]{3,2,1,0:T(8,128)(2,1)}, bf16[4,2,32,256]{3,2,1,0:T(8,128)(2,1)S(1)}, u32[]{:S(2)}, u32[]{:S(2)}) collective-permute-start(bf16[4,2,32,256]{3,2,1,0:T(8,128)(2,1)} %bitcast.27), channel_id=1, source_target_pairs={{0,1},{1,0},{2,3},{3,2},{4,5},{5,4},{6,7},{7,6},{8,9},{9,8},{10,11... | collective-permute-start | bytes 393224 | tf_op jit(solution)/shard_map/ppermute | solution.py:51
  8.9 16.9 %collective-permute-start.9 = (bf16[256,256]{1,0:T(8,128)(2,1)S(1)}, bf16[256,256]{1,0:T(8,128)(2,1)S(1)}, u32[]{:S(2)}, u32[]{:S(2)}) collective-permute-start(bf16[256,256]{1,0:T(8,128)(2,1)S(1)} %bitcast.31), channel_id=1, source_target_pairs={{0,6},{1,7},{2,4},{3,5},{4,2},{5,3},{6,0},{7,1},{8,14},{9,15},{10,... | collective-permute-start | bytes 393224 | tf_op jit(solution)/shard_map/ppermute | solution.py:51
  9.1 7.7 %collective-permute-start = (bf16[256,256]{1,0:T(8,128)(2,1)S(1)}, bf16[256,256]{1,0:T(8,128)(2,1)S(1)}, u32[]{:S(2)}, u32[]{:S(2)}) collective-permute-start(bf16[256,256]{1,0:T(8,128)(2,1)S(1)} %bitcast.18), channel_id=1, source_target_pairs={{0,1},{1,0},{2,3},{3,2},{4,5},{5,4},{6,7},{7,6},{8,9},{9,8},{10,11... | collective-permute-start | bytes 393224 | tf_op jit(solution)/shard_map/ppermute | solution.py:51
  9.5 1.1 %copy-start = (bf16[6,256,256]{2,1,0:T(8,128)(2,1)S(1)}, bf16[6,256,256]{2,1,0:T(8,128)(2,1)}, u32[]{:S(2)}) copy-start(bf16[6,256,256]{2,1,0:T(8,128)(2,1)} %factor_ref.1) | copy-start | bytes 2359300
  10.6 4.4 %copy-start.1 = (bf16[4,256,256]{2,1,0:T(8,128)(2,1)S(1)}, bf16[4,256,256]{2,1,0:T(8,128)(2,1)}, u32[]{:S(2)}) copy-start(bf16[4,256,256]{2,1,0:T(8,128)(2,1)} %diag_ref.1) | copy-start | bytes 1572868
  11.2 9.4 %copy-start.2 = (bf16[4,2,1,32,256]{4,3,2,1,0:T(8,128)(2,1)S(1)}, bf16[4,2,1,32,256]{4,3,2,1,0:T(8,128)(2,1)}, u32[]{:S(2)}) copy-start(bf16[4,2,1,32,256]{4,3,2,1,0:T(8,128)(2,1)} %param.6) | copy-start | bytes 393220
  11.3 9.4 %copy-start.3 = (s32[4,8]{1,0:T(4,128)S(1)}, s32[4,8]{1,0:T(4,128)}, u32[]{:S(2)}) copy-start(s32[4,8]{1,0:T(4,128)} %flags_ref.3) | copy-start | bytes 388
  11.9 8.8 %collective-permute-start.5 = (bf16[4,2,32,256]{3,2,1,0:T(8,128)(2,1)S(1)}, bf16[4,2,32,256]{3,2,1,0:T(8,128)(2,1)S(1)}, u32[]{:S(2)}, u32[]{:S(2)}) collective-permute-start(bf16[4,2,32,256]{3,2,1,0:T(8,128)(2,1)S(1)} %collective-permute-done.4.refs_2_), channel_id=1, source_target_pairs={{0,1},{1,0},{2,3},{3,2},{4,5},{5,4},{6,7},{7,6},{8,9},{9,8},{10,11... | collective-permute-start | bytes 393224 | tf_op jit(solution)/shard_map/ppermute | solution.py:51
  15.0 5.7 %collective-permute-start.2 = (bf16[256,256]{1,0:T(8,128)(2,1)S(1)}, bf16[256,256]{1,0:T(8,128)(2,1)S(1)}, u32[]{:S(2)}, u32[]{:S(2)}) collective-permute-start(bf16[256,256]{1,0:T(8,128)(2,1)S(1)} %collective-permute-done.1.refs_10_), channel_id=1, source_target_pairs={{0,1},{1,0},{2,3},{3,2},{4,5},{5,4},{6,7},{7,6},{8,9},{9,8},{10,11... | collective-permute-start | bytes 393224 | tf_op jit(solution)/shard_map/ppermute | solution.py:51
  16.8 10.5 %collective-permute-start.7 = (bf16[256,256]{1,0:T(8,128)(2,1)S(1)}, bf16[256,256]{1,0:T(8,128)(2,1)S(1)}, u32[]{:S(2)}, u32[]{:S(2)}) collective-permute-start(bf16[256,256]{1,0:T(8,128)(2,1)S(1)} %bitcast.19), channel_id=1, source_target_pairs={{0,4},{1,5},{2,6},{3,7},{4,0},{5,1},{6,2},{7,3},{8,12},{9,13},{10,... | collective-permute-start | bytes 393224 | tf_op jit(solution)/shard_map/ppermute | solution.py:51
  22.3 10.3 %collective-permute-start.12 = (bf16[2,2,4,32,256]{4,3,2,1,0:T(8,128)(2,1)S(1)}, bf16[2,2,4,32,256]{4,3,2,1,0:T(8,128)(2,1)S(1)}, u32[]{:S(2)}, u32[]{:S(2)}) collective-permute-start(bf16[2,2,4,32,256]{4,3,2,1,0:T(8,128)(2,1)S(1)} %bitcast.21), channel_id=1, source_target_pairs={{0,18},{1,19},{2,16},{3,17},{4,22},{5,23},{6,20},{7,21},{8,26},{9,... | collective-permute-start | bytes 786440 | tf_op jit(solution)/shard_map/ppermute | solution.py:51
  23.7 12.1 %collective-permute-start.11 = (bf16[2,2,4,32,256]{4,3,2,1,0:T(8,128)(2,1)S(1)}, bf16[2,2,4,32,256]{4,3,2,1,0:T(8,128)(2,1)S(1)}, u32[]{:S(2)}, u32[]{:S(2)}) collective-permute-start(bf16[2,2,4,32,256]{4,3,2,1,0:T(8,128)(2,1)S(1)} %bitcast.22), channel_id=1, source_target_pairs={{0,16},{1,17},{2,18},{3,19},{4,20},{5,21},{6,22},{7,23},{8,24},{9,... | collective-permute-start | bytes 786440 | tf_op jit(solution)/shard_map/ppermute | solution.py:51
  24.2 11.6 %collective-permute-start.6 = (bf16[2,2,4,32,256]{4,3,2,1,0:T(8,128)(2,1)S(1)}, bf16[2,2,4,32,256]{4,3,2,1,0:T(8,128)(2,1)S(1)}, u32[]{:S(2)}, u32[]{:S(2)}) collective-permute-start(bf16[2,2,4,32,256]{4,3,2,1,0:T(8,128)(2,1)S(1)} %bitcast.23), channel_id=1, source_target_pairs={{0,2},{1,3},{2,0},{3,1},{4,6},{5,7},{6,4},{7,5},{8,10},{9,11},{10,... | collective-permute-start | bytes 786440 | tf_op jit(solution)/shard_map/ppermute | solution.py:51
  25.8 5.0 %collective-permute-start.10 = (bf16[256,256]{1,0:T(8,128)(2,1)S(1)}, bf16[256,256]{1,0:T(8,128)(2,1)S(1)}, u32[]{:S(2)}, u32[]{:S(2)}) collective-permute-start(bf16[256,256]{1,0:T(8,128)(2,1)S(1)} %collective-permute-done.9.refs_14_), channel_id=1, source_target_pairs={{0,1},{1,0},{2,3},{3,2},{4,5},{5,4},{6,7},{7,6},{8,9},{9,8},{10,11... | collective-permute-start | bytes 393224 | tf_op jit(solution)/shard_map/ppermute | solution.py:51
  27.3 5.0 %collective-permute-start.8 = (bf16[256,256]{1,0:T(8,128)(2,1)S(1)}, bf16[256,256]{1,0:T(8,128)(2,1)S(1)}, u32[]{:S(2)}, u32[]{:S(2)}) collective-permute-start(bf16[256,256]{1,0:T(8,128)(2,1)S(1)} %collective-permute-done.7.refs_12_), channel_id=1, source_target_pairs={{0,1},{1,0},{2,3},{3,2},{4,5},{5,4},{6,7},{7,6},{8,9},{9,8},{10,11... | collective-permute-start | bytes 393224 | tf_op jit(solution)/shard_map/ppermute | solution.py:51
  30.8 5.5 %collective-permute-start.13 = (bf16[2,2,4,32,256]{4,3,2,1,0:T(8,128)(2,1)S(1)}, bf16[2,2,4,32,256]{4,3,2,1,0:T(8,128)(2,1)S(1)}, u32[]{:S(2)}, u32[]{:S(2)}) collective-permute-start(bf16[2,2,4,32,256]{4,3,2,1,0:T(8,128)(2,1)S(1)} %bitcast.24), channel_id=1, source_target_pairs={{0,8},{1,9},{2,10},{3,11},{4,12},{5,13},{6,14},{7,15},{8,0},{9,1},... | collective-permute-start | bytes 786440 | tf_op jit(solution)/shard_map/ppermute | solution.py:51
  32.5 3.8 %collective-permute-start.16 = (bf16[2,2,4,32,256]{4,3,2,1,0:T(8,128)(2,1)S(1)}, bf16[2,2,4,32,256]{4,3,2,1,0:T(8,128)(2,1)S(1)}, u32[]{:S(2)}, u32[]{:S(2)}) collective-permute-start(bf16[2,2,4,32,256]{4,3,2,1,0:T(8,128)(2,1)S(1)} %collective-permute-done.12.refs_3_), channel_id=1, source_target_pairs={{0,8},{1,9},{2,10},{3,11},{4,12},{5,13},{6,14},{7,15},{8,0},{9,1},... | collective-permute-start | bytes 786440 | tf_op jit(solution)/shard_map/ppermute | solution.py:51
  35.8 1.5 %collective-permute-start.15 = (bf16[2,2,4,32,256]{4,3,2,1,0:T(8,128)(2,1)S(1)}, bf16[2,2,4,32,256]{4,3,2,1,0:T(8,128)(2,1)S(1)}, u32[]{:S(2)}, u32[]{:S(2)}) collective-permute-start(bf16[2,2,4,32,256]{4,3,2,1,0:T(8,128)(2,1)S(1)} %collective-permute-done.11.refs_2_), channel_id=1, source_target_pairs={{0,8},{1,9},{2,10},{3,11},{4,12},{5,13},{6,14},{7,15},{8,0},{9,1},... | collective-permute-start | bytes 786440 | tf_op jit(solution)/shard_map/ppermute | solution.py:51
  35.8 1.9 %collective-permute-start.14 = (bf16[2,2,4,32,256]{4,3,2,1,0:T(8,128)(2,1)S(1)}, bf16[2,2,4,32,256]{4,3,2,1,0:T(8,128)(2,1)S(1)}, u32[]{:S(2)}, u32[]{:S(2)}) collective-permute-start(bf16[2,2,4,32,256]{4,3,2,1,0:T(8,128)(2,1)S(1)} %collective-permute-done.6.refs_1_), channel_id=1, source_target_pairs={{0,8},{1,9},{2,10},{3,11},{4,12},{5,13},{6,14},{7,15},{8,0},{9,1},... | collective-permute-start | bytes 786440 | tf_op jit(solution)/shard_map/ppermute | solution.py:51
  40.4 4.6 %collective-permute-start.20 = (f32[2,2,256,128]{3,2,1,0:T(8,128)S(1)}, f32[2,2,256,128]{3,2,1,0:T(8,128)S(1)}, u32[]{:S(2)}, u32[]{:S(2)}) collective-permute-start(f32[2,2,256,128]{3,2,1,0:T(8,128)S(1)} %get-tuple-element.39), channel_id=1, source_target_pairs={{0,8},{1,9},{2,10},{3,11},{4,12},{5,13},{6,14},{7,15},{8,0},{9,1},... | collective-permute-start | bytes 1572872 | tf_op jit(solution)/shard_map/ppermute | solution.py:51
  40.6 6.5 %collective-permute-start.17 = (f32[2,32,256]{2,1,0:T(8,128)S(1)}, f32[2,32,256]{2,1,0:T(8,128)S(1)}, u32[]{:S(2)}, u32[]{:S(2)}) collective-permute-start(f32[2,32,256]{2,1,0:T(8,128)S(1)} %get-tuple-element.29), channel_id=1, source_target_pairs={{0,1},{1,0},{2,3},{3,2},{4,5},{5,4},{6,7},{7,6},{8,9},{9,8},{10,11... | collective-permute-start | bytes 196616 | tf_op jit(solution)/shard_map/ppermute | solution.py:51
  41.9 7.7 %collective-permute-start.18 = (f32[2,32,256]{2,1,0:T(8,128)S(1)}, f32[2,32,256]{2,1,0:T(8,128)S(1)}, u32[]{:S(2)}, u32[]{:S(2)}) collective-permute-start(f32[2,32,256]{2,1,0:T(8,128)S(1)} %get-tuple-element.30), channel_id=1, source_target_pairs={{0,4},{1,5},{2,6},{3,7},{4,0},{5,1},{6,2},{7,3},{8,12},{9,13},{10,... | collective-permute-start | bytes 196616 | tf_op jit(solution)/shard_map/ppermute | solution.py:51
  44.2 6.6 %collective-permute-start.19 = (f32[2,32,256]{2,1,0:T(8,128)S(1)}, f32[2,32,256]{2,1,0:T(8,128)S(1)}, u32[]{:S(2)}, u32[]{:S(2)}) collective-permute-start(f32[2,32,256]{2,1,0:T(8,128)S(1)} %get-tuple-element.31), channel_id=1, source_target_pairs={{0,5},{1,4},{2,7},{3,6},{4,1},{5,0},{6,3},{7,2},{8,13},{9,12},{10,... | collective-permute-start | bytes 196616 | tf_op jit(solution)/shard_map/ppermute | solution.py:51
  45.0 7.8 %collective-permute-start.21 = (f32[256,128]{1,0:T(8,128)S(1)}, f32[256,128]{1,0:T(8,128)S(1)}, u32[]{:S(2)}, u32[]{:S(2)}) collective-permute-start(f32[256,128]{1,0:T(8,128)S(1)} %get-tuple-element.41), channel_id=1, source_target_pairs={{0,2},{1,3},{2,0},{3,1},{4,6},{5,7},{6,4},{7,5},{8,10},{9,11},{10,... | collective-permute-start | bytes 393224 | tf_op jit(solution)/shard_map/ppermute | solution.py:51
  46.2 6.7 %collective-permute-start.22 = (f32[256,128]{1,0:T(8,128)S(1)}, f32[256,128]{1,0:T(8,128)S(1)}, u32[]{:S(2)}, u32[]{:S(2)}) collective-permute-start(f32[256,128]{1,0:T(8,128)S(1)} %get-tuple-element.42), channel_id=1, source_target_pairs={{0,16},{1,17},{2,18},{3,19},{4,20},{5,21},{6,22},{7,23},{8,24},{9,... | collective-permute-start | bytes 393224 | tf_op jit(solution)/shard_map/ppermute | solution.py:51
  47.1 8.6 %collective-permute-start.23 = (f32[256,128]{1,0:T(8,128)S(1)}, f32[256,128]{1,0:T(8,128)S(1)}, u32[]{:S(2)}, u32[]{:S(2)}) collective-permute-start(f32[256,128]{1,0:T(8,128)S(1)} %get-tuple-element.43), channel_id=1, source_target_pairs={{0,18},{1,19},{2,16},{3,17},{4,22},{5,23},{6,20},{7,21},{8,26},{9,... | collective-permute-start | bytes 393224 | tf_op jit(solution)/shard_map/ppermute | solution.py:51

commit v5 on v4

--- a/solution.py
+++ b/solution.py
@@ -132,7 +132,7 @@
     for later in range(supernodes):
         total = panels[later]
         for earlier in range(later):
-            for part in three_parts(inverse_ref[pair_index(earlier, later)]):
+            for part in split(inverse_ref[pair_index(earlier, later)]):
                 total = total + dot(narrow[earlier], part)
         high_ref[later], low_ref[later] = split(total)
     for mine_ref in mine_refs:
@@ -338,11 +338,9 @@
         mine = jnp.concatenate(slices, 2)
     mine = mine.reshape(2, tile_rows, lines, slice_rows, block)
     steps, lanes = [], []
-    for dx in range(x_count):
-        for dh in range(2):
-            lane = mine if dx + dh == 0 else move(mine, dx, 0, 0, dh)
-            lanes.append(lane)
-            steps.append((dx, 0, dh))
+    for dx, dh in sorted(((dx, dh) for dx in range(x_count) for dh in range(2)), key=lambda f: (f != (0, 0), -f[0] - f[1], f)):
+        lanes.append(mine if dx + dh == 0 else move(mine, dx, 0, 0, dh))
+        steps.append((dx, 0, dh))
     lanes[1:] = [after(lane, *sep_pieces[1:]) for lane in lanes[1:]]
     for (dx, _, dh), lane in zip(list(steps), list(lanes)):
         lanes.append(move(lane, 0, 1, 0, 0))

time: 56.5 us -> 55.7 us (0.986)
  starting transfers between devices: 25.5 us -> 24.9 us
  transfers between devices with their start and end apart: 24 -> 24, of which waited for: 13 -> 12; matrix products, arithmetic and copies ran while one was open for 2% -> 2% of each run, Pallas kernels for 8% -> 8%
where the time goes in v5:
time: 55.7 us; the launch traced here: 55.5 us
  starting transfers between devices  24.9 us (45%)
  waiting for transfers between devices  19.7 us (35%)
  Pallas kernels  7.9 us (14%)
  local copies, waits for them, and re-layouts  2.22 us (4%)
  between operations  0.74 us (1%)
    ppermute x24, starting transfers between devices, move(): return lax.ppermute(value, AXES, pairs)  24.9 us
    ppermute x24, waiting for transfers between devices, move(): return lax.ppermute(value, AXES, pairs)  19.7 us
    pallas_call x8, Pallas kernels, call(): pl.pallas_call(kernel, out_shape=outs if last else [pltpu.VMEM(out.shape,...  7.9 us
    unnamed x8, local copies, waits for them, and re-layouts  1.15 us
  transfers between devices with their start and end apart: 24, of which 12 were waited for; matrix products, arithmetic and copies ran while one was open for 2% of the time, Pallas kernels for 8%

profile of v5, /device:TPU:0, one launch (start us, length us, event | category | flops | bytes accessed | tf_op | source)
XLA Modules:
  0.0 55.5 jit_solution(14275018888622716698)
XLA Ops:
  0.6 4.1 %collective-permute-start.4 = (bf16[4,2,32,256]{3,2,1,0:T(8,128)(2,1)}, bf16[4,2,32,256]{3,2,1,0:T(8,128)(2,1)S(1)}, u32[]{:S(2)}, u32[]{:S(2)}) collective-permute-start(bf16[4,2,32,256]{3,2,1,0:T(8,128)(2,1)} %bitcast.26), channel_id=1, source_target_pairs={{0,4},{1,5},{2,6},{3,7},{4,0},{5,1},{6,2},{7,3},{8,12},{9,13},{10,... | collective-permute-start | bytes 393224 | tf_op jit(solution)/shard_map/ppermute | solution.py:51
  4.7 1.0 %constant_dynamic-slice_fusion = (bf16[2,2,1,2,32,256]{5,4,3,2,1,0:T(8,128)(2,1)S(1)}, bf16[2,2,1,2,32,256]{5,4,3,2,1,0:T(8,128)(2,1)S(1)}) fusion(bf16[2,2,2,2,32,256]{5,4,3,2,1,0:T(8,128)(2,1)} %bitcast.29, s32[]{:T(128)S(6)} %select_n.39, s32[]{:T(128)S(6)} %select_n.38), kind=kLoop, calls=%fused_computation | loop fusion | bytes 524296 | tf_op jit(solution)/shard_map/jit(dynamic_index_in_dim)/dynamic_slice | solution.py:286
  5.7 1.6 %collective-permute-start.1 = (bf16[256,256]{1,0:T(8,128)(2,1)S(1)}, bf16[256,256]{1,0:T(8,128)(2,1)S(1)}, u32[]{:S(2)}, u32[]{:S(2)}) collective-permute-start(bf16[256,256]{1,0:T(8,128)(2,1)S(1)} %bitcast.30), channel_id=1, source_target_pairs={{0,2},{1,3},{2,0},{3,1},{4,6},{5,7},{6,4},{7,5},{8,10},{9,11},{10,... | collective-permute-start | bytes 393224 | tf_op jit(solution)/shard_map/ppermute | solution.py:51
  7.4 1.5 %collective-permute-start.3 = (bf16[4,2,32,256]{3,2,1,0:T(8,128)(2,1)}, bf16[4,2,32,256]{3,2,1,0:T(8,128)(2,1)S(1)}, u32[]{:S(2)}, u32[]{:S(2)}) collective-permute-start(bf16[4,2,32,256]{3,2,1,0:T(8,128)(2,1)} %bitcast.27), channel_id=1, source_target_pairs={{0,1},{1,0},{2,3},{3,2},{4,5},{5,4},{6,7},{7,6},{8,9},{9,8},{10,11... | collective-permute-start | bytes 393224 | tf_op jit(solution)/shard_map/ppermute | solution.py:51
  8.9 0.2 collective-permute-start.9
  9.1 0.3 collective-permute-start
  9.4 0.1 stack.27.place_ref
  9.5 1.1 %copy-done = bf16[6,256,256]{2,1,0:T(8,128)(2,1)S(1)} copy-done((bf16[6,256,256]{2,1,0:T(8,128)(2,1)S(1)}, bf16[6,256,256]{2,1,0:T(8,128)(2,1)}, u32[]{:S(2)}) %copy-start) | copy-done | bytes 786456
  10.6 0.6 %shard_map.68.inverse_ref.refs_4_ = f32[6,256,256]{2,1,0:T(8,128)S(1)} custom-call(bf16[6,256,256]{2,1,0:T(8,128)(2,1)S(1)} %copy-done), custom_call_target="tpu_custom_call" | custom-call | flops 1000000000 | tf_op jit(solution)/shard_map/pallas_call | solution.py:252
  11.2 0.0 copy-start.2
  11.3 0.0 copy-start.3
  11.3 0.7 %collective-permute-done.4.refs_2_ = bf16[4,2,32,256]{3,2,1,0:T(8,128)(2,1)S(1)} collective-permute-done((bf16[4,2,32,256]{3,2,1,0:T(8,128)(2,1)}, bf16[4,2,32,256]{3,2,1,0:T(8,128)(2,1)S(1)}, u32[]{:S(2)}, u32[]{:S(2)}) %collective-permute-start.4) | collective-permute-done | bytes 131104 | tf_op jit(solution)/shard_map/ppermute | solution.py:51
  11.9 3.1 %collective-permute-start.5 = (bf16[4,2,32,256]{3,2,1,0:T(8,128)(2,1)S(1)}, bf16[4,2,32,256]{3,2,1,0:T(8,128)(2,1)S(1)}, u32[]{:S(2)}, u32[]{:S(2)}) collective-permute-start(bf16[4,2,32,256]{3,2,1,0:T(8,128)(2,1)S(1)} %collective-permute-done.4.refs_2_), channel_id=1, source_target_pairs={{0,1},{1,0},{2,3},{3,2},{4,5},{5,4},{6,7},{7,6},{8,9},{9,8},{10,11... | collective-permute-start | bytes 393224 | tf_op jit(solution)/shard_map/ppermute | solution.py:51
  15.0 0.0 collective-permute-done.1.refs_10_
  15.0 0.0 collective-permute-start.2
  15.0 0.0 copy-done.1
  15.0 1.2 %shard_map.69.refs_4_ = f32[256,128]{1,0:T(8,128)S(1)} custom-call(s32[6]{0:T(128)S(1)} %stack.27.place_ref, f32[6,256,256]{2,1,0:T(8,128)S(1)} %shard_map.68.inverse_ref.refs_4_, bf16[4,256,256]{2,1,0:T(8,128)(2,1)S(1)} %copy-done.1), custom_call_target="tpu_custom_call" | custom-call | flops 3000000000 | tf_op jit(solution)/shard_map/pallas_call | solution.py:252
  16.2 0.6 %collective-permute-done.refs_9_ = bf16[256,256]{1,0:T(8,128)(2,1)S(1)} collective-permute-done((bf16[256,256]{1,0:T(8,128)(2,1)S(1)}, bf16[256,256]{1,0:T(8,128)(2,1)S(1)}, u32[]{:S(2)}, u32[]{:S(2)}) %collective-permute-start) | collective-permute-done | bytes 131104 | tf_op jit(solution)/shard_map/ppermute | solution.py:51
  16.8 0.3 collective-permute-start.7
  17.2 3.5 %collective-permute-done.2.refs_11_ = bf16[256,256]{1,0:T(8,128)(2,1)S(1)} collective-permute-done((bf16[256,256]{1,0:T(8,128)(2,1)S(1)}, bf16[256,256]{1,0:T(8,128)(2,1)S(1)}, u32[]{:S(2)}, u32[]{:S(2)}) %collective-permute-start.2) | collective-permute-done | bytes 131104 | tf_op jit(solution)/shard_map/ppermute | solution.py:51
  20.7 0.0 collective-permute-done.3.refs_1_
  20.7 0.0 collective-permute-done.5.refs_3_
  20.7 0.0 copy-done.2
  20.7 0.0 copy-done.3
  20.7 1.3 %shard_map.70 = (bf16[4,256,256]{2,1,0:T(8,128)(2,1)S(1)}, bf16[4,256,256]{2,1,0:T(8,128)(2,1)S(1)}, bf16[2,256,256]{2,1,0:T(8,128)(2,1)S(1)}) custom-call(s32[6]{0:T(128)S(1)} %stack.27.place_ref, s32[4,8]{1,0:T(4,128)S(1)} %copy-done.3, bf16[4,2,32,256]{3,2,1,0:T(8,128)(2,1)S(1)} %bitcast.28, bf16[4,2,32,256]{3,2,1,0:T(8,128)(2,1)S(1)} %collective-permute-done.3.refs_1_, ...), custom_call_target="tpu_custom_call" | custom-call | flops 2500000000 | tf_op jit(solution)/shard_map/pallas_call | solution.py:252
  22.0 1.6 %collective-permute-start.12 = (bf16[2,2,4,32,256]{4,3,2,1,0:T(8,128)(2,1)S(1)}, bf16[2,2,4,32,256]{4,3,2,1,0:T(8,128)(2,1)S(1)}, u32[]{:S(2)}, u32[]{:S(2)}) collective-permute-start(bf16[2,2,4,32,256]{4,3,2,1,0:T(8,128)(2,1)S(1)} %bitcast.21), channel_id=1, source_target_pairs={{0,16},{1,17},{2,18},{3,19},{4,20},{5,21},{6,22},{7,23},{8,24},{9,... | collective-permute-start | bytes 786440 | tf_op jit(solution)/shard_map/ppermute | solution.py:51
  23.6 0.4 collective-permute-start.11
  24.0 1.5 %collective-permute-start.6 = (bf16[2,2,4,32,256]{4,3,2,1,0:T(8,128)(2,1)S(1)}, bf16[2,2,4,32,256]{4,3,2,1,0:T(8,128)(2,1)S(1)}, u32[]{:S(2)}, u32[]{:S(2)}) collective-permute-start(bf16[2,2,4,32,256]{4,3,2,1,0:T(8,128)(2,1)S(1)} %bitcast.23), channel_id=1, source_target_pairs={{0,18},{1,19},{2,16},{3,17},{4,22},{5,23},{6,20},{7,21},{8,26},{9,... | collective-permute-start | bytes 786440 | tf_op jit(solution)/shard_map/ppermute | solution.py:51
  25.6 0.0 collective-permute-done.9.refs_14_
  25.6 1.5 %collective-permute-start.10 = (bf16[256,256]{1,0:T(8,128)(2,1)S(1)}, bf16[256,256]{1,0:T(8,128)(2,1)S(1)}, u32[]{:S(2)}, u32[]{:S(2)}) collective-permute-start(bf16[256,256]{1,0:T(8,128)(2,1)S(1)} %collective-permute-done.9.refs_14_), channel_id=1, source_target_pairs={{0,1},{1,0},{2,3},{3,2},{4,5},{5,4},{6,7},{7,6},{8,9},{9,8},{10,11... | collective-permute-start | bytes 393224 | tf_op jit(solution)/shard_map/ppermute | solution.py:51
  27.1 0.0 collective-permute-done.7.refs_12_
  27.1 0.5 collective-permute-start.8
  27.6 2.9 %collective-permute-done.10.refs_15_ = bf16[256,256]{1,0:T(8,128)(2,1)S(1)} collective-permute-done((bf16[256,256]{1,0:T(8,128)(2,1)S(1)}, bf16[256,256]{1,0:T(8,128)(2,1)S(1)}, u32[]{:S(2)}, u32[]{:S(2)}) %collective-permute-start.10) | collective-permute-done | bytes 131104 | tf_op jit(solution)/shard_map/ppermute | solution.py:51
  30.6 0.0 collective-permute-start.13
  30.6 1.5 %collective-permute-done.8.refs_13_ = bf16[256,256]{1,0:T(8,128)(2,1)S(1)} collective-permute-done((bf16[256,256]{1,0:T(8,128)(2,1)S(1)}, bf16[256,256]{1,0:T(8,128)(2,1)S(1)}, u32[]{:S(2)}, u32[]{:S(2)}) %collective-permute-start.8) | collective-permute-done | bytes 131104 | tf_op jit(solution)/shard_map/ppermute | solution.py:51
  32.1 0.0 collective-permute-done.12.refs_3_
  32.1 0.0 collective-permute-start.16
  32.1 0.6 %collective-permute-done.11.refs_2_ = bf16[2,2,4,32,256]{4,3,2,1,0:T(8,128)(2,1)S(1)} collective-permute-done((bf16[2,2,4,32,256]{4,3,2,1,0:T(8,128)(2,1)S(1)}, bf16[2,2,4,32,256]{4,3,2,1,0:T(8,128)(2,1)S(1)}, u32[]{:S(2)}, u32[]{:S(2)}) %collective-permute-start.11) | collective-permute-done | bytes 262176 | tf_op jit(solution)/shard_map/ppermute | solution.py:51
  32.7 0.0 collective-permute-start.15
  32.7 4.1 %collective-permute-done.6.refs_1_ = bf16[2,2,4,32,256]{4,3,2,1,0:T(8,128)(2,1)S(1)} collective-permute-done((bf16[2,2,4,32,256]{4,3,2,1,0:T(8,128)(2,1)S(1)}, bf16[2,2,4,32,256]{4,3,2,1,0:T(8,128)(2,1)S(1)}, u32[]{:S(2)}, u32[]{:S(2)}) %collective-permute-start.6) | collective-permute-done | bytes 262176 | tf_op jit(solution)/shard_map/ppermute | solution.py:51
  36.8 0.0 collective-permute-start.14
  36.8 0.0 collective-permute-done.13.refs_4_
  36.8 0.0 collective-permute-done.16.refs_7_
  36.8 0.0 collective-permute-done.15.refs_6_
  36.8 1.5 %collective-permute-done.14.refs_5_ = bf16[2,2,4,32,256]{4,3,2,1,0:T(8,128)(2,1)S(1)} collective-permute-done((bf16[2,2,4,32,256]{4,3,2,1,0:T(8,128)(2,1)S(1)}, bf16[2,2,4,32,256]{4,3,2,1,0:T(8,128)(2,1)S(1)}, u32[]{:S(2)}, u32[]{:S(2)}) %collective-permute-start.14) | collective-permute-done | bytes 262176 | tf_op jit(solution)/shard_map/ppermute | solution.py:51
  38.3 1.4 %shard_map.71 = (f32[2,32,256]{2,1,0:T(8,128)S(1)}, f32[2,32,256]{2,1,0:T(8,128)S(1)}, f32[2,32,256]{2,1,0:T(8,128)S(1)}, f32[2,32,256]{2,1,0:T(8,128)S(1)}, bf1...) custom-call(s32[6]{0:T(128)S(1)} %stack.27.place_ref, s32[4,8]{1,0:T(4,128)S(1)} %copy-done.3, ...), custom_call_target="tpu_custom_call" | custom-call | flops 1700000000 | tf_op jit(solution)/shard_map/pallas_call | solution.py:252
  39.8 1.2 %shard_map.73 = (f32[2,2,256,128]{3,2,1,0:T(8,128)S(1)}, f32[2,2,256,128]{3,2,1,0:T(8,128)S(1)}) custom-call(s32[6]{0:T(128)S(1)} %stack.27.place_ref, bf16[4,256,256]{2,1,0:T(8,128)(2,1)S(1)} %get-tuple-element.34.left_high_ref, bf16[4,256,256]{2,1,0:T(8,128)(2,1)S(1)} %get-tuple-element.35.left_low_ref, bf16[256,256]{1,0:T(8,128)(2,1)S(1)} %get-tuple-element.36.high_ref, ...), custom_call_target="tpu_custom_call" | custom-call | flops 1400000000 | tf_op jit(solution)/shard_map/pallas_call | solution.py:252
  41.0 0.2 collective-permute-start.20
  41.2 1.3 %collective-permute-start.17 = (f32[2,32,256]{2,1,0:T(8,128)S(1)}, f32[2,32,256]{2,1,0:T(8,128)S(1)}, u32[]{:S(2)}, u32[]{:S(2)}) collective-permute-start(f32[2,32,256]{2,1,0:T(8,128)S(1)} %get-tuple-element.29), channel_id=1, source_target_pairs={{0,1},{1,0},{2,3},{3,2},{4,5},{5,4},{6,7},{7,6},{8,9},{9,8},{10,11... | collective-permute-start | bytes 196616 | tf_op jit(solution)/shard_map/ppermute | solution.py:51
  42.5 1.4 %collective-permute-start.18 = (f32[2,32,256]{2,1,0:T(8,128)S(1)}, f32[2,32,256]{2,1,0:T(8,128)S(1)}, u32[]{:S(2)}, u32[]{:S(2)}) collective-permute-start(f32[2,32,256]{2,1,0:T(8,128)S(1)} %get-tuple-element.30), channel_id=1, source_target_pairs={{0,4},{1,5},{2,6},{3,7},{4,0},{5,1},{6,2},{7,3},{8,12},{9,13},{10,... | collective-permute-start | bytes 196616 | tf_op jit(solution)/shard_map/ppermute | solution.py:51
  43.8 1.8 %collective-permute-start.19 = (f32[2,32,256]{2,1,0:T(8,128)S(1)}, f32[2,32,256]{2,1,0:T(8,128)S(1)}, u32[]{:S(2)}, u32[]{:S(2)}) collective-permute-start(f32[2,32,256]{2,1,0:T(8,128)S(1)} %get-tuple-element.31), channel_id=1, source_target_pairs={{0,5},{1,4},{2,7},{3,6},{4,1},{5,0},{6,3},{7,2},{8,13},{9,12},{10,... | collective-permute-start | bytes 196616 | tf_op jit(solution)/shard_map/ppermute | solution.py:51
  45.6 0.0 collective-permute-done.20.received_ref
  45.6 0.1 shard_map.74
  45.7 0.8 %collective-permute-start.21 = (f32[256,128]{1,0:T(8,128)S(1)}, f32[256,128]{1,0:T(8,128)S(1)}, u32[]{:S(2)}, u32[]{:S(2)}) collective-permute-start(f32[256,128]{1,0:T(8,128)S(1)} %get-tuple-element.41), channel_id=1, source_target_pairs={{0,2},{1,3},{2,0},{3,1},{4,6},{5,7},{6,4},{7,5},{8,10},{9,11},{10,... | collective-permute-start | bytes 393224 | tf_op jit(solution)/shard_map/ppermute | solution.py:51
  46.4 1.0 %collective-permute-start.22 = (f32[256,128]{1,0:T(8,128)S(1)}, f32[256,128]{1,0:T(8,128)S(1)}, u32[]{:S(2)}, u32[]{:S(2)}) collective-permute-start(f32[256,128]{1,0:T(8,128)S(1)} %get-tuple-element.42), channel_id=1, source_target_pairs={{0,16},{1,17},{2,18},{3,19},{4,20},{5,21},{6,22},{7,23},{8,24},{9,... | collective-permute-start | bytes 393224 | tf_op jit(solution)/shard_map/ppermute | solution.py:51
  47.4 0.0 collective-permute-done.17.refs_1_
  47.4 1.8 %collective-permute-start.23 = (f32[256,128]{1,0:T(8,128)S(1)}, f32[256,128]{1,0:T(8,128)S(1)}, u32[]{:S(2)}, u32[]{:S(2)}) collective-permute-start(f32[256,128]{1,0:T(8,128)S(1)} %get-tuple-element.43), channel_id=1, source_target_pairs={{0,18},{1,19},{2,16},{3,17},{4,22},{5,23},{6,20},{7,21},{8,26},{9,... | collective-permute-start | bytes 393224 | tf_op jit(solution)/shard_map/ppermute | solution.py:51
  49.2 1.0 %collective-permute-done.18.refs_2_ = f32[2,32,256]{2,1,0:T(8,128)S(1)} collective-permute-done((f32[2,32,256]{2,1,0:T(8,128)S(1)}, f32[2,32,256]{2,1,0:T(8,128)S(1)}, u32[]{:S(2)}, u32[]{:S(2)}) %collective-permute-start.18) | collective-permute-done | bytes 65568 | tf_op jit(solution)/shard_map/ppermute | solution.py:51
  50.3 1.0 %collective-permute-done.19.refs_3_ = f32[2,32,256]{2,1,0:T(8,128)S(1)} collective-permute-done((f32[2,32,256]{2,1,0:T(8,128)S(1)}, f32[2,32,256]{2,1,0:T(8,128)S(1)}, u32[]{:S(2)}, u32[]{:S(2)}) %collective-permute-start.19) | collective-permute-done | bytes 65568 | tf_op jit(solution)/shard_map/ppermute | solution.py:51
  51.3 1.3 %shard_map.72 = (f32[4,2,32,256]{3,2,1,0:T(8,128)}, f32[8,128]{1,0:T(8,128)S(1)}) custom-call(s32[6]{0:T(128)S(1)} %stack.27.place_ref, f32[2,32,256]{2,1,0:T(8,128)S(1)} %get-tuple-element.28.refs_0_, f32[2,32,256]{2,1,0:T(8,128)S(1)} %collective-permute-done.17.refs_1_, f32[2,32,256]{2,1,0:T(8,128)S(1)} %collective-permute-done.18.refs_2_, ...), custom_call_target="tpu_custom_call" | custom-call | flops 12000000000 | tf_op jit(solution)/shard_map/pallas_call | solution.py:252
  52.6 0.7 %collective-permute-done.21.refs_1_ = f32[256,128]{1,0:T(8,128)S(1)} collective-permute-done((f32[256,128]{1,0:T(8,128)S(1)}, f32[256,128]{1,0:T(8,128)S(1)}, u32[]{:S(2)}, u32[]{:S(2)}) %collective-permute-start.21) | collective-permute-done | bytes 131104 | tf_op jit(solution)/shard_map/ppermute | solution.py:51
  53.3 0.0 collective-permute-done.22.refs_2_
  53.3 1.5 %collective-permute-done.23.refs_3_ = f32[256,128]{1,0:T(8,128)S(1)} collective-permute-done((f32[256,128]{1,0:T(8,128)S(1)}, f32[256,128]{1,0:T(8,128)S(1)}, u32[]{:S(2)}, u32[]{:S(2)}) %collective-permute-start.23) | collective-permute-done | bytes 131104 | tf_op jit(solution)/shard_map/ppermute | solution.py:51
  54.8 0.7 %shard_map.75 = f32[256,128]{1,0:T(8,128)} custom-call(f32[8,128]{1,0:T(8,128)S(1)} %get-tuple-element.33._, f32[256,128]{1,0:T(8,128)S(1)} %get-tuple-element.40.refs_0_, f32[256,128]{1,0:T(8,128)S(1)} %collective-permute-done.21.refs_1_, f32[256,128]{1,0:T(8,128)S(1)} %collective-permute-done.22.refs_2_, f32[256,128]{1,0:T(8,128)S(1)} %collective-permute-done.23.refs_3_, ...), custom_call_target="tpu_custom_call" | custom-call | flops 500000000 | tf_op jit(solution)/shard_map/pallas_call | solution.py:252
  (2 shorter events, 0.0 us)
Async XLA Ops:
  0.6 11.3 %collective-permute-start.4 = (bf16[4,2,32,256]{3,2,1,0:T(8,128)(2,1)}, bf16[4,2,32,256]{3,2,1,0:T(8,128)(2,1)S(1)}, u32[]{:S(2)}, u32[]{:S(2)}) collective-permute-start(bf16[4,2,32,256]{3,2,1,0:T(8,128)(2,1)} %bitcast.26), channel_id=1, source_target_pairs={{0,4},{1,5},{2,6},{3,7},{4,0},{5,1},{6,2},{7,3},{8,12},{9,13},{10,... | collective-permute-start | bytes 393224 | tf_op jit(solution)/shard_map/ppermute | solution.py:51
  5.7 9.3 %collective-permute-start.1 = (bf16[256,256]{1,0:T(8,128)(2,1)S(1)}, bf16[256,256]{1,0:T(8,128)(2,1)S(1)}, u32[]{:S(2)}, u32[]{:S(2)}) collective-permute-start(bf16[256,256]{1,0:T(8,128)(2,1)S(1)} %bitcast.30), channel_id=1, source_target_pairs={{0,2},{1,3},{2,0},{3,1},{4,6},{5,7},{6,4},{7,5},{8,10},{9,11},{10,... | collective-permute-start | bytes 393224 | tf_op jit(solution)/shard_map/ppermute | solution.py:51
  7.4 13.3 %collective-permute-start.3 = (bf16[4,2,32,256]{3,2,1,0:T(8,128)(2,1)}, bf16[4,2,32,256]{3,2,1,0:T(8,128)(2,1)S(1)}, u32[]{:S(2)}, u32[]{:S(2)}) collective-permute-start(bf16[4,2,32,256]{3,2,1,0:T(8,128)(2,1)} %bitcast.27), channel_id=1, source_target_pairs={{0,1},{1,0},{2,3},{3,2},{4,5},{5,4},{6,7},{7,6},{8,9},{9,8},{10,11... | collective-permute-start | bytes 393224 | tf_op jit(solution)/shard_map/ppermute | solution.py:51
  8.9 16.7 %collective-permute-start.9 = (bf16[256,256]{1,0:T(8,128)(2,1)S(1)}, bf16[256,256]{1,0:T(8,128)(2,1)S(1)}, u32[]{:S(2)}, u32[]{:S(2)}) collective-permute-start(bf16[256,256]{1,0:T(8,128)(2,1)S(1)} %bitcast.31), channel_id=1, source_target_pairs={{0,6},{1,7},{2,4},{3,5},{4,2},{5,3},{6,0},{7,1},{8,14},{9,15},{10,... | collective-permute-start | bytes 393224 | tf_op jit(solution)/shard_map/ppermute | solution.py:51
  9.1 7.7 %collective-permute-start = (bf16[256,256]{1,0:T(8,128)(2,1)S(1)}, bf16[256,256]{1,0:T(8,128)(2,1)S(1)}, u32[]{:S(2)}, u32[]{:S(2)}) collective-permute-start(bf16[256,256]{1,0:T(8,128)(2,1)S(1)} %bitcast.18), channel_id=1, source_target_pairs={{0,1},{1,0},{2,3},{3,2},{4,5},{5,4},{6,7},{7,6},{8,9},{9,8},{10,11... | collective-permute-start | bytes 393224 | tf_op jit(solution)/shard_map/ppermute | solution.py:51
  9.5 1.1 %copy-start = (bf16[6,256,256]{2,1,0:T(8,128)(2,1)S(1)}, bf16[6,256,256]{2,1,0:T(8,128)(2,1)}, u32[]{:S(2)}) copy-start(bf16[6,256,256]{2,1,0:T(8,128)(2,1)} %factor_ref.1) | copy-start | bytes 2359300
  10.6 4.4 %copy-start.1 = (bf16[4,256,256]{2,1,0:T(8,128)(2,1)S(1)}, bf16[4,256,256]{2,1,0:T(8,128)(2,1)}, u32[]{:S(2)}) copy-start(bf16[4,256,256]{2,1,0:T(8,128)(2,1)} %diag_ref.1) | copy-start | bytes 1572868
  11.2 9.4 %copy-start.2 = (bf16[4,2,1,32,256]{4,3,2,1,0:T(8,128)(2,1)S(1)}, bf16[4,2,1,32,256]{4,3,2,1,0:T(8,128)(2,1)}, u32[]{:S(2)}) copy-start(bf16[4,2,1,32,256]{4,3,2,1,0:T(8,128)(2,1)} %param.6) | copy-start | bytes 393220
  11.3 9.4 %copy-start.3 = (s32[4,8]{1,0:T(4,128)S(1)}, s32[4,8]{1,0:T(4,128)}, u32[]{:S(2)}) copy-start(s32[4,8]{1,0:T(4,128)} %flags_ref.3) | copy-start | bytes 388
  11.9 8.8 %collective-permute-start.5 = (bf16[4,2,32,256]{3,2,1,0:T(8,128)(2,1)S(1)}, bf16[4,2,32,256]{3,2,1,0:T(8,128)(2,1)S(1)}, u32[]{:S(2)}, u32[]{:S(2)}) collective-permute-start(bf16[4,2,32,256]{3,2,1,0:T(8,128)(2,1)S(1)} %collective-permute-done.4.refs_2_), channel_id=1, source_target_pairs={{0,1},{1,0},{2,3},{3,2},{4,5},{5,4},{6,7},{7,6},{8,9},{9,8},{10,11... | collective-permute-start | bytes 393224 | tf_op jit(solution)/shard_map/ppermute | solution.py:51
  15.0 5.7 %collective-permute-start.2 = (bf16[256,256]{1,0:T(8,128)(2,1)S(1)}, bf16[256,256]{1,0:T(8,128)(2,1)S(1)}, u32[]{:S(2)}, u32[]{:S(2)}) collective-permute-start(bf16[256,256]{1,0:T(8,128)(2,1)S(1)} %collective-permute-done.1.refs_10_), channel_id=1, source_target_pairs={{0,1},{1,0},{2,3},{3,2},{4,5},{5,4},{6,7},{7,6},{8,9},{9,8},{10,11... | collective-permute-start | bytes 393224 | tf_op jit(solution)/shard_map/ppermute | solution.py:51
  16.8 10.3 %collective-permute-start.7 = (bf16[256,256]{1,0:T(8,128)(2,1)S(1)}, bf16[256,256]{1,0:T(8,128)(2,1)S(1)}, u32[]{:S(2)}, u32[]{:S(2)}) collective-permute-start(bf16[256,256]{1,0:T(8,128)(2,1)S(1)} %bitcast.19), channel_id=1, source_target_pairs={{0,4},{1,5},{2,6},{3,7},{4,0},{5,1},{6,2},{7,3},{8,12},{9,13},{10,... | collective-permute-start | bytes 393224 | tf_op jit(solution)/shard_map/ppermute | solution.py:51
  22.0 10.1 %collective-permute-start.12 = (bf16[2,2,4,32,256]{4,3,2,1,0:T(8,128)(2,1)S(1)}, bf16[2,2,4,32,256]{4,3,2,1,0:T(8,128)(2,1)S(1)}, u32[]{:S(2)}, u32[]{:S(2)}) collective-permute-start(bf16[2,2,4,32,256]{4,3,2,1,0:T(8,128)(2,1)S(1)} %bitcast.21), channel_id=1, source_target_pairs={{0,16},{1,17},{2,18},{3,19},{4,20},{5,21},{6,22},{7,23},{8,24},{9,... | collective-permute-start | bytes 786440 | tf_op jit(solution)/shard_map/ppermute | solution.py:51
  23.6 9.1 %collective-permute-start.11 = (bf16[2,2,4,32,256]{4,3,2,1,0:T(8,128)(2,1)S(1)}, bf16[2,2,4,32,256]{4,3,2,1,0:T(8,128)(2,1)S(1)}, u32[]{:S(2)}, u32[]{:S(2)}) collective-permute-start(bf16[2,2,4,32,256]{4,3,2,1,0:T(8,128)(2,1)S(1)} %bitcast.22), channel_id=1, source_target_pairs={{0,2},{1,3},{2,0},{3,1},{4,6},{5,7},{6,4},{7,5},{8,10},{9,11},{10,... | collective-permute-start | bytes 786440 | tf_op jit(solution)/shard_map/ppermute | solution.py:51
  24.0 12.7 %collective-permute-start.6 = (bf16[2,2,4,32,256]{4,3,2,1,0:T(8,128)(2,1)S(1)}, bf16[2,2,4,32,256]{4,3,2,1,0:T(8,128)(2,1)S(1)}, u32[]{:S(2)}, u32[]{:S(2)}) collective-permute-start(bf16[2,2,4,32,256]{4,3,2,1,0:T(8,128)(2,1)S(1)} %bitcast.23), channel_id=1, source_target_pairs={{0,18},{1,19},{2,16},{3,17},{4,22},{5,23},{6,20},{7,21},{8,26},{9,... | collective-permute-start | bytes 786440 | tf_op jit(solution)/shard_map/ppermute | solution.py:51
  25.6 5.0 %collective-permute-start.10 = (bf16[256,256]{1,0:T(8,128)(2,1)S(1)}, bf16[256,256]{1,0:T(8,128)(2,1)S(1)}, u32[]{:S(2)}, u32[]{:S(2)}) collective-permute-start(bf16[256,256]{1,0:T(8,128)(2,1)S(1)} %collective-permute-done.9.refs_14_), channel_id=1, source_target_pairs={{0,1},{1,0},{2,3},{3,2},{4,5},{5,4},{6,7},{7,6},{8,9},{9,8},{10,11... | collective-permute-start | bytes 393224 | tf_op jit(solution)/shard_map/ppermute | solution.py:51
  27.1 5.0 %collective-permute-start.8 = (bf16[256,256]{1,0:T(8,128)(2,1)S(1)}, bf16[256,256]{1,0:T(8,128)(2,1)S(1)}, u32[]{:S(2)}, u32[]{:S(2)}) collective-permute-start(bf16[256,256]{1,0:T(8,128)(2,1)S(1)} %collective-permute-done.7.refs_12_), channel_id=1, source_target_pairs={{0,1},{1,0},{2,3},{3,2},{4,5},{5,4},{6,7},{7,6},{8,9},{9,8},{10,11... | collective-permute-start | bytes 393224 | tf_op jit(solution)/shard_map/ppermute | solution.py:51
  30.6 6.2 %collective-permute-start.13 = (bf16[2,2,4,32,256]{4,3,2,1,0:T(8,128)(2,1)S(1)}, bf16[2,2,4,32,256]{4,3,2,1,0:T(8,128)(2,1)S(1)}, u32[]{:S(2)}, u32[]{:S(2)}) collective-permute-start(bf16[2,2,4,32,256]{4,3,2,1,0:T(8,128)(2,1)S(1)} %bitcast.24), channel_id=1, source_target_pairs={{0,8},{1,9},{2,10},{3,11},{4,12},{5,13},{6,14},{7,15},{8,0},{9,1},... | collective-permute-start | bytes 786440 | tf_op jit(solution)/shard_map/ppermute | solution.py:51
  32.1 4.7 %collective-permute-start.16 = (bf16[2,2,4,32,256]{4,3,2,1,0:T(8,128)(2,1)S(1)}, bf16[2,2,4,32,256]{4,3,2,1,0:T(8,128)(2,1)S(1)}, u32[]{:S(2)}, u32[]{:S(2)}) collective-permute-start(bf16[2,2,4,32,256]{4,3,2,1,0:T(8,128)(2,1)S(1)} %collective-permute-done.12.refs_3_), channel_id=1, source_target_pairs={{0,8},{1,9},{2,10},{3,11},{4,12},{5,13},{6,14},{7,15},{8,0},{9,1},... | collective-permute-start | bytes 786440 | tf_op jit(solution)/shard_map/ppermute | solution.py:51
  32.7 4.1 %collective-permute-start.15 = (bf16[2,2,4,32,256]{4,3,2,1,0:T(8,128)(2,1)S(1)}, bf16[2,2,4,32,256]{4,3,2,1,0:T(8,128)(2,1)S(1)}, u32[]{:S(2)}, u32[]{:S(2)}) collective-permute-start(bf16[2,2,4,32,256]{4,3,2,1,0:T(8,128)(2,1)S(1)} %collective-permute-done.11.refs_2_), channel_id=1, source_target_pairs={{0,8},{1,9},{2,10},{3,11},{4,12},{5,13},{6,14},{7,15},{8,0},{9,1},... | collective-permute-start | bytes 786440 | tf_op jit(solution)/shard_map/ppermute | solution.py:51
  36.8 1.5 %collective-permute-start.14 = (bf16[2,2,4,32,256]{4,3,2,1,0:T(8,128)(2,1)S(1)}, bf16[2,2,4,32,256]{4,3,2,1,0:T(8,128)(2,1)S(1)}, u32[]{:S(2)}, u32[]{:S(2)}) collective-permute-start(bf16[2,2,4,32,256]{4,3,2,1,0:T(8,128)(2,1)S(1)} %collective-permute-done.6.refs_1_), channel_id=1, source_target_pairs={{0,8},{1,9},{2,10},{3,11},{4,12},{5,13},{6,14},{7,15},{8,0},{9,1},... | collective-permute-start | bytes 786440 | tf_op jit(solution)/shard_map/ppermute | solution.py:51
  41.0 4.6 %collective-permute-start.20 = (f32[2,2,256,128]{3,2,1,0:T(8,128)S(1)}, f32[2,2,256,128]{3,2,1,0:T(8,128)S(1)}, u32[]{:S(2)}, u32[]{:S(2)}) collective-permute-start(f32[2,2,256,128]{3,2,1,0:T(8,128)S(1)} %get-tuple-element.39), channel_id=1, source_target_pairs={{0,8},{1,9},{2,10},{3,11},{4,12},{5,13},{6,14},{7,15},{8,0},{9,1},... | collective-permute-start | bytes 1572872 | tf_op jit(solution)/shard_map/ppermute | solution.py:51
  41.2 6.2 %collective-permute-start.17 = (f32[2,32,256]{2,1,0:T(8,128)S(1)}, f32[2,32,256]{2,1,0:T(8,128)S(1)}, u32[]{:S(2)}, u32[]{:S(2)}) collective-permute-start(f32[2,32,256]{2,1,0:T(8,128)S(1)} %get-tuple-element.29), channel_id=1, source_target_pairs={{0,1},{1,0},{2,3},{3,2},{4,5},{5,4},{6,7},{7,6},{8,9},{9,8},{10,11... | collective-permute-start | bytes 196616 | tf_op jit(solution)/shard_map/ppermute | solution.py:51
  42.5 7.8 %collective-permute-start.18 = (f32[2,32,256]{2,1,0:T(8,128)S(1)}, f32[2,32,256]{2,1,0:T(8,128)S(1)}, u32[]{:S(2)}, u32[]{:S(2)}) collective-permute-start(f32[2,32,256]{2,1,0:T(8,128)S(1)} %get-tuple-element.30), channel_id=1, source_target_pairs={{0,4},{1,5},{2,6},{3,7},{4,0},{5,1},{6,2},{7,3},{8,12},{9,13},{10,... | collective-permute-start | bytes 196616 | tf_op jit(solution)/shard_map/ppermute | solution.py:51
  43.8 7.5 %collective-permute-start.19 = (f32[2,32,256]{2,1,0:T(8,128)S(1)}, f32[2,32,256]{2,1,0:T(8,128)S(1)}, u32[]{:S(2)}, u32[]{:S(2)}) collective-permute-start(f32[2,32,256]{2,1,0:T(8,128)S(1)} %get-tuple-element.31), channel_id=1, source_target_pairs={{0,5},{1,4},{2,7},{3,6},{4,1},{5,0},{6,3},{7,2},{8,13},{9,12},{10,... | collective-permute-start | bytes 196616 | tf_op jit(solution)/shard_map/ppermute | solution.py:51
  45.7 7.6 %collective-permute-start.21 = (f32[256,128]{1,0:T(8,128)S(1)}, f32[256,128]{1,0:T(8,128)S(1)}, u32[]{:S(2)}, u32[]{:S(2)}) collective-permute-start(f32[256,128]{1,0:T(8,128)S(1)} %get-tuple-element.41), channel_id=1, source_target_pairs={{0,2},{1,3},{2,0},{3,1},{4,6},{5,7},{6,4},{7,5},{8,10},{9,11},{10,... | collective-permute-start | bytes 393224 | tf_op jit(solution)/shard_map/ppermute | solution.py:51
  46.4 6.8 %collective-permute-start.22 = (f32[256,128]{1,0:T(8,128)S(1)}, f32[256,128]{1,0:T(8,128)S(1)}, u32[]{:S(2)}, u32[]{:S(2)}) collective-permute-start(f32[256,128]{1,0:T(8,128)S(1)} %get-tuple-element.42), channel_id=1, source_target_pairs={{0,16},{1,17},{2,18},{3,19},{4,20},{5,21},{6,22},{7,23},{8,24},{9,... | collective-permute-start | bytes 393224 | tf_op jit(solution)/shard_map/ppermute | solution.py:51
  47.4 7.4 %collective-permute-start.23 = (f32[256,128]{1,0:T(8,128)S(1)}, f32[256,128]{1,0:T(8,128)S(1)}, u32[]{:S(2)}, u32[]{:S(2)}) collective-permute-start(f32[256,128]{1,0:T(8,128)S(1)} %get-tuple-element.43), channel_id=1, source_target_pairs={{0,18},{1,19},{2,16},{3,17},{4,22},{5,23},{6,20},{7,21},{8,26},{9,... | collective-permute-start | bytes 393224 | tf_op jit(solution)/shard_map/ppermute | solution.py:51

commit v6 on v5

--- a/solution.py
+++ b/solution.py
@@ -190,10 +190,12 @@
     x, core, half = (place_ref[i] for i in range(1, 4))
     supernodes, _, width = left_high_ref.shape
     high, low = high_ref[...], low_ref[...]
+    block = high.shape[1]
+    pair = jnp.concatenate([high, low], 1)
     for k in range(supernodes):
-        left_high, left_low = left_high_ref[k], left_low_ref[k]
+        both = dot_rows(left_high_ref[k], pair)
         window_ref[k * width : (k + 1) * width, :] = (
-            dot_rows(left_high, high) + dot_rows(left_high, low) + dot_rows(left_low, high)
+            both[:, :block] + both[:, block:] + dot_rows(left_low_ref[k], high)
         )
     x_count, _, rows_each, cols_each = keep_ref.shape
     for dx in range(x_count):

time: 55.7 us -> 55.7 us (level)
  no operation moved by 1% of the time
where the time goes in v6:
time: 55.7 us; the launch traced here: 55.5 us
  starting transfers between devices  24.9 us (45%)
  waiting for transfers between devices  19.7 us (35%)
  Pallas kernels  7.9 us (14%)
  local copies, waits for them, and re-layouts  2.22 us (4%)
  between operations  0.74 us (1%)
    ppermute x24, starting transfers between devices, move(): return lax.ppermute(value, AXES, pairs)  24.9 us
    ppermute x24, waiting for transfers between devices, move(): return lax.ppermute(value, AXES, pairs)  19.7 us
    pallas_call x8, Pallas kernels, call(): pl.pallas_call(kernel, out_shape=outs if last else [pltpu.VMEM(out.shape,...  7.9 us
    unnamed x8, local copies, waits for them, and re-layouts  1.15 us
  transfers between devices with their start and end apart: 24, of which 12 were waited for; matrix products, arithmetic and copies ran while one was open for 2% of the time, Pallas kernels for 8%

profile of v6, /device:TPU:0, one launch (start us, length us, event | category | flops | bytes accessed | tf_op | source)
XLA Modules:
  0.0 55.5 jit_solution(6183288106701623144)
XLA Ops:
  0.6 4.1 %collective-permute-start.4 = (bf16[4,2,32,256]{3,2,1,0:T(8,128)(2,1)}, bf16[4,2,32,256]{3,2,1,0:T(8,128)(2,1)S(1)}, u32[]{:S(2)}, u32[]{:S(2)}) collective-permute-start(bf16[4,2,32,256]{3,2,1,0:T(8,128)(2,1)} %bitcast.26), channel_id=1, source_target_pairs={{0,4},{1,5},{2,6},{3,7},{4,0},{5,1},{6,2},{7,3},{8,12},{9,13},{10,... | collective-permute-start | bytes 393224 | tf_op jit(solution)/shard_map/ppermute | solution.py:51
  4.7 1.0 %constant_dynamic-slice_fusion = (bf16[2,2,1,2,32,256]{5,4,3,2,1,0:T(8,128)(2,1)S(1)}, bf16[2,2,1,2,32,256]{5,4,3,2,1,0:T(8,128)(2,1)S(1)}) fusion(bf16[2,2,2,2,32,256]{5,4,3,2,1,0:T(8,128)(2,1)} %bitcast.29, s32[]{:T(128)S(6)} %select_n.39, s32[]{:T(128)S(6)} %select_n.38), kind=kLoop, calls=%fused_computation | loop fusion | bytes 524296 | tf_op jit(solution)/shard_map/jit(dynamic_index_in_dim)/dynamic_slice | solution.py:288
  5.7 1.6 %collective-permute-start.1 = (bf16[256,256]{1,0:T(8,128)(2,1)S(1)}, bf16[256,256]{1,0:T(8,128)(2,1)S(1)}, u32[]{:S(2)}, u32[]{:S(2)}) collective-permute-start(bf16[256,256]{1,0:T(8,128)(2,1)S(1)} %bitcast.30), channel_id=1, source_target_pairs={{0,2},{1,3},{2,0},{3,1},{4,6},{5,7},{6,4},{7,5},{8,10},{9,11},{10,... | collective-permute-start | bytes 393224 | tf_op jit(solution)/shard_map/ppermute | solution.py:51
  7.4 1.5 %collective-permute-start.3 = (bf16[4,2,32,256]{3,2,1,0:T(8,128)(2,1)}, bf16[4,2,32,256]{3,2,1,0:T(8,128)(2,1)S(1)}, u32[]{:S(2)}, u32[]{:S(2)}) collective-permute-start(bf16[4,2,32,256]{3,2,1,0:T(8,128)(2,1)} %bitcast.27), channel_id=1, source_target_pairs={{0,1},{1,0},{2,3},{3,2},{4,5},{5,4},{6,7},{7,6},{8,9},{9,8},{10,11... | collective-permute-start | bytes 393224 | tf_op jit(solution)/shard_map/ppermute | solution.py:51
  8.9 0.2 collective-permute-start.9
  9.1 0.3 collective-permute-start
  9.4 0.1 stack.27.place_ref
  9.5 1.1 %copy-done = bf16[6,256,256]{2,1,0:T(8,128)(2,1)S(1)} copy-done((bf16[6,256,256]{2,1,0:T(8,128)(2,1)S(1)}, bf16[6,256,256]{2,1,0:T(8,128)(2,1)}, u32[]{:S(2)}) %copy-start) | copy-done | bytes 786456
  10.6 0.6 %shard_map.68.inverse_ref.refs_4_ = f32[6,256,256]{2,1,0:T(8,128)S(1)} custom-call(bf16[6,256,256]{2,1,0:T(8,128)(2,1)S(1)} %copy-done), custom_call_target="tpu_custom_call" | custom-call | flops 1000000000 | tf_op jit(solution)/shard_map/pallas_call | solution.py:254
  11.2 0.0 copy-start.2
  11.3 0.0 copy-start.3
  11.3 0.7 %collective-permute-done.4.refs_2_ = bf16[4,2,32,256]{3,2,1,0:T(8,128)(2,1)S(1)} collective-permute-done((bf16[4,2,32,256]{3,2,1,0:T(8,128)(2,1)}, bf16[4,2,32,256]{3,2,1,0:T(8,128)(2,1)S(1)}, u32[]{:S(2)}, u32[]{:S(2)}) %collective-permute-start.4) | collective-permute-done | bytes 131104 | tf_op jit(solution)/shard_map/ppermute | solution.py:51
  11.9 3.1 %collective-permute-start.5 = (bf16[4,2,32,256]{3,2,1,0:T(8,128)(2,1)S(1)}, bf16[4,2,32,256]{3,2,1,0:T(8,128)(2,1)S(1)}, u32[]{:S(2)}, u32[]{:S(2)}) collective-permute-start(bf16[4,2,32,256]{3,2,1,0:T(8,128)(2,1)S(1)} %collective-permute-done.4.refs_2_), channel_id=1, source_target_pairs={{0,1},{1,0},{2,3},{3,2},{4,5},{5,4},{6,7},{7,6},{8,9},{9,8},{10,11... | collective-permute-start | bytes 393224 | tf_op jit(solution)/shard_map/ppermute | solution.py:51
  15.0 0.0 collective-permute-done.1.refs_10_
  15.0 0.0 collective-permute-start.2
  15.0 0.0 copy-done.1
  15.0 1.2 %shard_map.69.refs_4_ = f32[256,128]{1,0:T(8,128)S(1)} custom-call(s32[6]{0:T(128)S(1)} %stack.27.place_ref, f32[6,256,256]{2,1,0:T(8,128)S(1)} %shard_map.68.inverse_ref.refs_4_, bf16[4,256,256]{2,1,0:T(8,128)(2,1)S(1)} %copy-done.1), custom_call_target="tpu_custom_call" | custom-call | flops 3000000000 | tf_op jit(solution)/shard_map/pallas_call | solution.py:254
  16.2 0.6 %collective-permute-done.refs_9_ = bf16[256,256]{1,0:T(8,128)(2,1)S(1)} collective-permute-done((bf16[256,256]{1,0:T(8,128)(2,1)S(1)}, bf16[256,256]{1,0:T(8,128)(2,1)S(1)}, u32[]{:S(2)}, u32[]{:S(2)}) %collective-permute-start) | collective-permute-done | bytes 131104 | tf_op jit(solution)/shard_map/ppermute | solution.py:51
  16.8 0.3 collective-permute-start.7
  17.2 3.5 %collective-permute-done.2.refs_11_ = bf16[256,256]{1,0:T(8,128)(2,1)S(1)} collective-permute-done((bf16[256,256]{1,0:T(8,128)(2,1)S(1)}, bf16[256,256]{1,0:T(8,128)(2,1)S(1)}, u32[]{:S(2)}, u32[]{:S(2)}) %collective-permute-start.2) | collective-permute-done | bytes 131104 | tf_op jit(solution)/shard_map/ppermute | solution.py:51
  20.7 0.0 collective-permute-done.3.refs_1_
  20.7 0.0 collective-permute-done.5.refs_3_
  20.7 0.0 copy-done.2
  20.7 0.0 copy-done.3
  20.7 1.3 %shard_map.70 = (bf16[4,256,256]{2,1,0:T(8,128)(2,1)S(1)}, bf16[4,256,256]{2,1,0:T(8,128)(2,1)S(1)}, bf16[2,256,256]{2,1,0:T(8,128)(2,1)S(1)}) custom-call(s32[6]{0:T(128)S(1)} %stack.27.place_ref, s32[4,8]{1,0:T(4,128)S(1)} %copy-done.3, bf16[4,2,32,256]{3,2,1,0:T(8,128)(2,1)S(1)} %bitcast.28, bf16[4,2,32,256]{3,2,1,0:T(8,128)(2,1)S(1)} %collective-permute-done.3.refs_1_, ...), custom_call_target="tpu_custom_call" | custom-call | flops 2500000000 | tf_op jit(solution)/shard_map/pallas_call | solution.py:254
  22.0 1.6 %collective-permute-start.12 = (bf16[2,2,4,32,256]{4,3,2,1,0:T(8,128)(2,1)S(1)}, bf16[2,2,4,32,256]{4,3,2,1,0:T(8,128)(2,1)S(1)}, u32[]{:S(2)}, u32[]{:S(2)}) collective-permute-start(bf16[2,2,4,32,256]{4,3,2,1,0:T(8,128)(2,1)S(1)} %bitcast.21), channel_id=1, source_target_pairs={{0,16},{1,17},{2,18},{3,19},{4,20},{5,21},{6,22},{7,23},{8,24},{9,... | collective-permute-start | bytes 786440 | tf_op jit(solution)/shard_map/ppermute | solution.py:51
  23.6 0.4 collective-permute-start.11
  24.0 1.5 %collective-permute-start.6 = (bf16[2,2,4,32,256]{4,3,2,1,0:T(8,128)(2,1)S(1)}, bf16[2,2,4,32,256]{4,3,2,1,0:T(8,128)(2,1)S(1)}, u32[]{:S(2)}, u32[]{:S(2)}) collective-permute-start(bf16[2,2,4,32,256]{4,3,2,1,0:T(8,128)(2,1)S(1)} %bitcast.23), channel_id=1, source_target_pairs={{0,18},{1,19},{2,16},{3,17},{4,22},{5,23},{6,20},{7,21},{8,26},{9,... | collective-permute-start | bytes 786440 | tf_op jit(solution)/shard_map/ppermute | solution.py:51
  25.6 0.0 collective-permute-done.9.refs_14_
  25.6 1.5 %collective-permute-start.10 = (bf16[256,256]{1,0:T(8,128)(2,1)S(1)}, bf16[256,256]{1,0:T(8,128)(2,1)S(1)}, u32[]{:S(2)}, u32[]{:S(2)}) collective-permute-start(bf16[256,256]{1,0:T(8,128)(2,1)S(1)} %collective-permute-done.9.refs_14_), channel_id=1, source_target_pairs={{0,1},{1,0},{2,3},{3,2},{4,5},{5,4},{6,7},{7,6},{8,9},{9,8},{10,11... | collective-permute-start | bytes 393224 | tf_op jit(solution)/shard_map/ppermute | solution.py:51
  27.1 0.0 collective-permute-done.7.refs_12_
  27.1 0.5 collective-permute-start.8
  27.6 2.9 %collective-permute-done.10.refs_15_ = bf16[256,256]{1,0:T(8,128)(2,1)S(1)} collective-permute-done((bf16[256,256]{1,0:T(8,128)(2,1)S(1)}, bf16[256,256]{1,0:T(8,128)(2,1)S(1)}, u32[]{:S(2)}, u32[]{:S(2)}) %collective-permute-start.10) | collective-permute-done | bytes 131104 | tf_op jit(solution)/shard_map/ppermute | solution.py:51
  30.6 0.0 collective-permute-start.13
  30.6 1.5 %collective-permute-done.8.refs_13_ = bf16[256,256]{1,0:T(8,128)(2,1)S(1)} collective-permute-done((bf16[256,256]{1,0:T(8,128)(2,1)S(1)}, bf16[256,256]{1,0:T(8,128)(2,1)S(1)}, u32[]{:S(2)}, u32[]{:S(2)}) %collective-permute-start.8) | collective-permute-done | bytes 131104 | tf_op jit(solution)/shard_map/ppermute | solution.py:51
  32.1 0.0 collective-permute-done.12.refs_3_
  32.1 0.0 collective-permute-start.16
  32.1 0.6 %collective-permute-done.11.refs_2_ = bf16[2,2,4,32,256]{4,3,2,1,0:T(8,128)(2,1)S(1)} collective-permute-done((bf16[2,2,4,32,256]{4,3,2,1,0:T(8,128)(2,1)S(1)}, bf16[2,2,4,32,256]{4,3,2,1,0:T(8,128)(2,1)S(1)}, u32[]{:S(2)}, u32[]{:S(2)}) %collective-permute-start.11) | collective-permute-done | bytes 262176 | tf_op jit(solution)/shard_map/ppermute | solution.py:51
  32.7 0.0 collective-permute-start.15
  32.7 4.1 %collective-permute-done.6.refs_1_ = bf16[2,2,4,32,256]{4,3,2,1,0:T(8,128)(2,1)S(1)} collective-permute-done((bf16[2,2,4,32,256]{4,3,2,1,0:T(8,128)(2,1)S(1)}, bf16[2,2,4,32,256]{4,3,2,1,0:T(8,128)(2,1)S(1)}, u32[]{:S(2)}, u32[]{:S(2)}) %collective-permute-start.6) | collective-permute-done | bytes 262176 | tf_op jit(solution)/shard_map/ppermute | solution.py:51
  36.8 0.0 collective-permute-start.14
  36.8 0.0 collective-permute-done.13.refs_4_
  36.8 0.0 collective-permute-done.16.refs_7_
  36.8 0.0 collective-permute-done.15.refs_6_
  36.8 1.5 %collective-permute-done.14.refs_5_ = bf16[2,2,4,32,256]{4,3,2,1,0:T(8,128)(2,1)S(1)} collective-permute-done((bf16[2,2,4,32,256]{4,3,2,1,0:T(8,128)(2,1)S(1)}, bf16[2,2,4,32,256]{4,3,2,1,0:T(8,128)(2,1)S(1)}, u32[]{:S(2)}, u32[]{:S(2)}) %collective-permute-start.14) | collective-permute-done | bytes 262176 | tf_op jit(solution)/shard_map/ppermute | solution.py:51
  38.3 1.4 %shard_map.71 = (f32[2,32,256]{2,1,0:T(8,128)S(1)}, f32[2,32,256]{2,1,0:T(8,128)S(1)}, f32[2,32,256]{2,1,0:T(8,128)S(1)}, f32[2,32,256]{2,1,0:T(8,128)S(1)}, bf1...) custom-call(s32[6]{0:T(128)S(1)} %stack.27.place_ref, s32[4,8]{1,0:T(4,128)S(1)} %copy-done.3, ...), custom_call_target="tpu_custom_call" | custom-call | flops 1700000000 | tf_op jit(solution)/shard_map/pallas_call | solution.py:254
  39.8 1.2 %shard_map.73 = (f32[2,2,256,128]{3,2,1,0:T(8,128)S(1)}, f32[2,2,256,128]{3,2,1,0:T(8,128)S(1)}) custom-call(s32[6]{0:T(128)S(1)} %stack.27.place_ref, bf16[4,256,256]{2,1,0:T(8,128)(2,1)S(1)} %get-tuple-element.34.left_high_ref, bf16[4,256,256]{2,1,0:T(8,128)(2,1)S(1)} %get-tuple-element.35.left_low_ref, bf16[256,256]{1,0:T(8,128)(2,1)S(1)} %get-tuple-element.36.high_ref, ...), custom_call_target="tpu_custom_call" | custom-call | flops 1400000000 | tf_op jit(solution)/shard_map/pallas_call | solution.py:254
  41.0 0.2 collective-permute-start.20
  41.2 1.3 %collective-permute-start.17 = (f32[2,32,256]{2,1,0:T(8,128)S(1)}, f32[2,32,256]{2,1,0:T(8,128)S(1)}, u32[]{:S(2)}, u32[]{:S(2)}) collective-permute-start(f32[2,32,256]{2,1,0:T(8,128)S(1)} %get-tuple-element.29), channel_id=1, source_target_pairs={{0,1},{1,0},{2,3},{3,2},{4,5},{5,4},{6,7},{7,6},{8,9},{9,8},{10,11... | collective-permute-start | bytes 196616 | tf_op jit(solution)/shard_map/ppermute | solution.py:51
  42.5 1.4 %collective-permute-start.18 = (f32[2,32,256]{2,1,0:T(8,128)S(1)}, f32[2,32,256]{2,1,0:T(8,128)S(1)}, u32[]{:S(2)}, u32[]{:S(2)}) collective-permute-start(f32[2,32,256]{2,1,0:T(8,128)S(1)} %get-tuple-element.30), channel_id=1, source_target_pairs={{0,4},{1,5},{2,6},{3,7},{4,0},{5,1},{6,2},{7,3},{8,12},{9,13},{10,... | collective-permute-start | bytes 196616 | tf_op jit(solution)/shard_map/ppermute | solution.py:51
  43.8 1.8 %collective-permute-start.19 = (f32[2,32,256]{2,1,0:T(8,128)S(1)}, f32[2,32,256]{2,1,0:T(8,128)S(1)}, u32[]{:S(2)}, u32[]{:S(2)}) collective-permute-start(f32[2,32,256]{2,1,0:T(8,128)S(1)} %get-tuple-element.31), channel_id=1, source_target_pairs={{0,5},{1,4},{2,7},{3,6},{4,1},{5,0},{6,3},{7,2},{8,13},{9,12},{10,... | collective-permute-start | bytes 196616 | tf_op jit(solution)/shard_map/ppermute | solution.py:51
  45.6 0.0 collective-permute-done.20.received_ref
  45.6 0.1 shard_map.74
  45.7 0.8 %collective-permute-start.21 = (f32[256,128]{1,0:T(8,128)S(1)}, f32[256,128]{1,0:T(8,128)S(1)}, u32[]{:S(2)}, u32[]{:S(2)}) collective-permute-start(f32[256,128]{1,0:T(8,128)S(1)} %get-tuple-element.41), channel_id=1, source_target_pairs={{0,2},{1,3},{2,0},{3,1},{4,6},{5,7},{6,4},{7,5},{8,10},{9,11},{10,... | collective-permute-start | bytes 393224 | tf_op jit(solution)/shard_map/ppermute | solution.py:51
  46.4 1.0 %collective-permute-start.22 = (f32[256,128]{1,0:T(8,128)S(1)}, f32[256,128]{1,0:T(8,128)S(1)}, u32[]{:S(2)}, u32[]{:S(2)}) collective-permute-start(f32[256,128]{1,0:T(8,128)S(1)} %get-tuple-element.42), channel_id=1, source_target_pairs={{0,16},{1,17},{2,18},{3,19},{4,20},{5,21},{6,22},{7,23},{8,24},{9,... | collective-permute-start | bytes 393224 | tf_op jit(solution)/shard_map/ppermute | solution.py:51
  47.4 0.0 collective-permute-done.17.refs_1_
  47.4 1.8 %collective-permute-start.23 = (f32[256,128]{1,0:T(8,128)S(1)}, f32[256,128]{1,0:T(8,128)S(1)}, u32[]{:S(2)}, u32[]{:S(2)}) collective-permute-start(f32[256,128]{1,0:T(8,128)S(1)} %get-tuple-element.43), channel_id=1, source_target_pairs={{0,18},{1,19},{2,16},{3,17},{4,22},{5,23},{6,20},{7,21},{8,26},{9,... | collective-permute-start | bytes 393224 | tf_op jit(solution)/shard_map/ppermute | solution.py:51
  49.2 1.0 %collective-permute-done.18.refs_2_ = f32[2,32,256]{2,1,0:T(8,128)S(1)} collective-permute-done((f32[2,32,256]{2,1,0:T(8,128)S(1)}, f32[2,32,256]{2,1,0:T(8,128)S(1)}, u32[]{:S(2)}, u32[]{:S(2)}) %collective-permute-start.18) | collective-permute-done | bytes 65568 | tf_op jit(solution)/shard_map/ppermute | solution.py:51
  50.3 1.0 %collective-permute-done.19.refs_3_ = f32[2,32,256]{2,1,0:T(8,128)S(1)} collective-permute-done((f32[2,32,256]{2,1,0:T(8,128)S(1)}, f32[2,32,256]{2,1,0:T(8,128)S(1)}, u32[]{:S(2)}, u32[]{:S(2)}) %collective-permute-start.19) | collective-permute-done | bytes 65568 | tf_op jit(solution)/shard_map/ppermute | solution.py:51
  51.3 1.3 %shard_map.72 = (f32[4,2,32,256]{3,2,1,0:T(8,128)}, f32[8,128]{1,0:T(8,128)S(1)}) custom-call(s32[6]{0:T(128)S(1)} %stack.27.place_ref, f32[2,32,256]{2,1,0:T(8,128)S(1)} %get-tuple-element.28.refs_0_, f32[2,32,256]{2,1,0:T(8,128)S(1)} %collective-permute-done.17.refs_1_, f32[2,32,256]{2,1,0:T(8,128)S(1)} %collective-permute-done.18.refs_2_, ...), custom_call_target="tpu_custom_call" | custom-call | flops 12000000000 | tf_op jit(solution)/shard_map/pallas_call | solution.py:254
  52.6 0.7 %collective-permute-done.21.refs_1_ = f32[256,128]{1,0:T(8,128)S(1)} collective-permute-done((f32[256,128]{1,0:T(8,128)S(1)}, f32[256,128]{1,0:T(8,128)S(1)}, u32[]{:S(2)}, u32[]{:S(2)}) %collective-permute-start.21) | collective-permute-done | bytes 131104 | tf_op jit(solution)/shard_map/ppermute | solution.py:51
  53.3 0.0 collective-permute-done.22.refs_2_
  53.3 1.5 %collective-permute-done.23.refs_3_ = f32[256,128]{1,0:T(8,128)S(1)} collective-permute-done((f32[256,128]{1,0:T(8,128)S(1)}, f32[256,128]{1,0:T(8,128)S(1)}, u32[]{:S(2)}, u32[]{:S(2)}) %collective-permute-start.23) | collective-permute-done | bytes 131104 | tf_op jit(solution)/shard_map/ppermute | solution.py:51
  54.8 0.7 %shard_map.75 = f32[256,128]{1,0:T(8,128)} custom-call(f32[8,128]{1,0:T(8,128)S(1)} %get-tuple-element.33._, f32[256,128]{1,0:T(8,128)S(1)} %get-tuple-element.40.refs_0_, f32[256,128]{1,0:T(8,128)S(1)} %collective-permute-done.21.refs_1_, f32[256,128]{1,0:T(8,128)S(1)} %collective-permute-done.22.refs_2_, f32[256,128]{1,0:T(8,128)S(1)} %collective-permute-done.23.refs_3_, ...), custom_call_target="tpu_custom_call" | custom-call | flops 500000000 | tf_op jit(solution)/shard_map/pallas_call | solution.py:254
  (2 shorter events, 0.0 us)
Async XLA Ops:
  0.6 11.3 %collective-permute-start.4 = (bf16[4,2,32,256]{3,2,1,0:T(8,128)(2,1)}, bf16[4,2,32,256]{3,2,1,0:T(8,128)(2,1)S(1)}, u32[]{:S(2)}, u32[]{:S(2)}) collective-permute-start(bf16[4,2,32,256]{3,2,1,0:T(8,128)(2,1)} %bitcast.26), channel_id=1, source_target_pairs={{0,4},{1,5},{2,6},{3,7},{4,0},{5,1},{6,2},{7,3},{8,12},{9,13},{10,... | collective-permute-start | bytes 393224 | tf_op jit(solution)/shard_map/ppermute | solution.py:51
  5.7 9.3 %collective-permute-start.1 = (bf16[256,256]{1,0:T(8,128)(2,1)S(1)}, bf16[256,256]{1,0:T(8,128)(2,1)S(1)}, u32[]{:S(2)}, u32[]{:S(2)}) collective-permute-start(bf16[256,256]{1,0:T(8,128)(2,1)S(1)} %bitcast.30), channel_id=1, source_target_pairs={{0,2},{1,3},{2,0},{3,1},{4,6},{5,7},{6,4},{7,5},{8,10},{9,11},{10,... | collective-permute-start | bytes 393224 | tf_op jit(solution)/shard_map/ppermute | solution.py:51
  7.4 13.3 %collective-permute-start.3 = (bf16[4,2,32,256]{3,2,1,0:T(8,128)(2,1)}, bf16[4,2,32,256]{3,2,1,0:T(8,128)(2,1)S(1)}, u32[]{:S(2)}, u32[]{:S(2)}) collective-permute-start(bf16[4,2,32,256]{3,2,1,0:T(8,128)(2,1)} %bitcast.27), channel_id=1, source_target_pairs={{0,1},{1,0},{2,3},{3,2},{4,5},{5,4},{6,7},{7,6},{8,9},{9,8},{10,11... | collective-permute-start | bytes 393224 | tf_op jit(solution)/shard_map/ppermute | solution.py:51
  8.9 16.7 %collective-permute-start.9 = (bf16[256,256]{1,0:T(8,128)(2,1)S(1)}, bf16[256,256]{1,0:T(8,128)(2,1)S(1)}, u32[]{:S(2)}, u32[]{:S(2)}) collective-permute-start(bf16[256,256]{1,0:T(8,128)(2,1)S(1)} %bitcast.31), channel_id=1, source_target_pairs={{0,6},{1,7},{2,4},{3,5},{4,2},{5,3},{6,0},{7,1},{8,14},{9,15},{10,... | collective-permute-start | bytes 393224 | tf_op jit(solution)/shard_map/ppermute | solution.py:51
  9.1 7.7 %collective-permute-start = (bf16[256,256]{1,0:T(8,128)(2,1)S(1)}, bf16[256,256]{1,0:T(8,128)(2,1)S(1)}, u32[]{:S(2)}, u32[]{:S(2)}) collective-permute-start(bf16[256,256]{1,0:T(8,128)(2,1)S(1)} %bitcast.18), channel_id=1, source_target_pairs={{0,1},{1,0},{2,3},{3,2},{4,5},{5,4},{6,7},{7,6},{8,9},{9,8},{10,11... | collective-permute-start | bytes 393224 | tf_op jit(solution)/shard_map/ppermute | solution.py:51
  9.5 1.1 %copy-start = (bf16[6,256,256]{2,1,0:T(8,128)(2,1)S(1)}, bf16[6,256,256]{2,1,0:T(8,128)(2,1)}, u32[]{:S(2)}) copy-start(bf16[6,256,256]{2,1,0:T(8,128)(2,1)} %factor_ref.1) | copy-start | bytes 2359300
  10.6 4.4 %copy-start.1 = (bf16[4,256,256]{2,1,0:T(8,128)(2,1)S(1)}, bf16[4,256,256]{2,1,0:T(8,128)(2,1)}, u32[]{:S(2)}) copy-start(bf16[4,256,256]{2,1,0:T(8,128)(2,1)} %diag_ref.1) | copy-start | bytes 1572868
  11.2 9.4 %copy-start.2 = (bf16[4,2,1,32,256]{4,3,2,1,0:T(8,128)(2,1)S(1)}, bf16[4,2,1,32,256]{4,3,2,1,0:T(8,128)(2,1)}, u32[]{:S(2)}) copy-start(bf16[4,2,1,32,256]{4,3,2,1,0:T(8,128)(2,1)} %param.6) | copy-start | bytes 393220
  11.3 9.4 %copy-start.3 = (s32[4,8]{1,0:T(4,128)S(1)}, s32[4,8]{1,0:T(4,128)}, u32[]{:S(2)}) copy-start(s32[4,8]{1,0:T(4,128)} %flags_ref.3) | copy-start | bytes 388
  11.9 8.8 %collective-permute-start.5 = (bf16[4,2,32,256]{3,2,1,0:T(8,128)(2,1)S(1)}, bf16[4,2,32,256]{3,2,1,0:T(8,128)(2,1)S(1)}, u32[]{:S(2)}, u32[]{:S(2)}) collective-permute-start(bf16[4,2,32,256]{3,2,1,0:T(8,128)(2,1)S(1)} %collective-permute-done.4.refs_2_), channel_id=1, source_target_pairs={{0,1},{1,0},{2,3},{3,2},{4,5},{5,4},{6,7},{7,6},{8,9},{9,8},{10,11... | collective-permute-start | bytes 393224 | tf_op jit(solution)/shard_map/ppermute | solution.py:51
  15.0 5.7 %collective-permute-start.2 = (bf16[256,256]{1,0:T(8,128)(2,1)S(1)}, bf16[256,256]{1,0:T(8,128)(2,1)S(1)}, u32[]{:S(2)}, u32[]{:S(2)}) collective-permute-start(bf16[256,256]{1,0:T(8,128)(2,1)S(1)} %collective-permute-done.1.refs_10_), channel_id=1, source_target_pairs={{0,1},{1,0},{2,3},{3,2},{4,5},{5,4},{6,7},{7,6},{8,9},{9,8},{10,11... | collective-permute-start | bytes 393224 | tf_op jit(solution)/shard_map/ppermute | solution.py:51
  16.8 10.3 %collective-permute-start.7 = (bf16[256,256]{1,0:T(8,128)(2,1)S(1)}, bf16[256,256]{1,0:T(8,128)(2,1)S(1)}, u32[]{:S(2)}, u32[]{:S(2)}) collective-permute-start(bf16[256,256]{1,0:T(8,128)(2,1)S(1)} %bitcast.19), channel_id=1, source_target_pairs={{0,4},{1,5},{2,6},{3,7},{4,0},{5,1},{6,2},{7,3},{8,12},{9,13},{10,... | collective-permute-start | bytes 393224 | tf_op jit(solution)/shard_map/ppermute | solution.py:51
  22.0 10.1 %collective-permute-start.12 = (bf16[2,2,4,32,256]{4,3,2,1,0:T(8,128)(2,1)S(1)}, bf16[2,2,4,32,256]{4,3,2,1,0:T(8,128)(2,1)S(1)}, u32[]{:S(2)}, u32[]{:S(2)}) collective-permute-start(bf16[2,2,4,32,256]{4,3,2,1,0:T(8,128)(2,1)S(1)} %bitcast.21), channel_id=1, source_target_pairs={{0,16},{1,17},{2,18},{3,19},{4,20},{5,21},{6,22},{7,23},{8,24},{9,... | collective-permute-start | bytes 786440 | tf_op jit(solution)/shard_map/ppermute | solution.py:51
  23.6 9.1 %collective-permute-start.11 = (bf16[2,2,4,32,256]{4,3,2,1,0:T(8,128)(2,1)S(1)}, bf16[2,2,4,32,256]{4,3,2,1,0:T(8,128)(2,1)S(1)}, u32[]{:S(2)}, u32[]{:S(2)}) collective-permute-start(bf16[2,2,4,32,256]{4,3,2,1,0:T(8,128)(2,1)S(1)} %bitcast.22), channel_id=1, source_target_pairs={{0,2},{1,3},{2,0},{3,1},{4,6},{5,7},{6,4},{7,5},{8,10},{9,11},{10,... | collective-permute-start | bytes 786440 | tf_op jit(solution)/shard_map/ppermute | solution.py:51
  24.0 12.7 %collective-permute-start.6 = (bf16[2,2,4,32,256]{4,3,2,1,0:T(8,128)(2,1)S(1)}, bf16[2,2,4,32,256]{4,3,2,1,0:T(8,128)(2,1)S(1)}, u32[]{:S(2)}, u32[]{:S(2)}) collective-permute-start(bf16[2,2,4,32,256]{4,3,2,1,0:T(8,128)(2,1)S(1)} %bitcast.23), channel_id=1, source_target_pairs={{0,18},{1,19},{2,16},{3,17},{4,22},{5,23},{6,20},{7,21},{8,26},{9,... | collective-permute-start | bytes 786440 | tf_op jit(solution)/shard_map/ppermute | solution.py:51
  25.6 5.0 %collective-permute-start.10 = (bf16[256,256]{1,0:T(8,128)(2,1)S(1)}, bf16[256,256]{1,0:T(8,128)(2,1)S(1)}, u32[]{:S(2)}, u32[]{:S(2)}) collective-permute-start(bf16[256,256]{1,0:T(8,128)(2,1)S(1)} %collective-permute-done.9.refs_14_), channel_id=1, source_target_pairs={{0,1},{1,0},{2,3},{3,2},{4,5},{5,4},{6,7},{7,6},{8,9},{9,8},{10,11... | collective-permute-start | bytes 393224 | tf_op jit(solution)/shard_map/ppermute | solution.py:51
  27.1 5.0 %collective-permute-start.8 = (bf16[256,256]{1,0:T(8,128)(2,1)S(1)}, bf16[256,256]{1,0:T(8,128)(2,1)S(1)}, u32[]{:S(2)}, u32[]{:S(2)}) collective-permute-start(bf16[256,256]{1,0:T(8,128)(2,1)S(1)} %collective-permute-done.7.refs_12_), channel_id=1, source_target_pairs={{0,1},{1,0},{2,3},{3,2},{4,5},{5,4},{6,7},{7,6},{8,9},{9,8},{10,11... | collective-permute-start | bytes 393224 | tf_op jit(solution)/shard_map/ppermute | solution.py:51
  30.6 6.2 %collective-permute-start.13 = (bf16[2,2,4,32,256]{4,3,2,1,0:T(8,128)(2,1)S(1)}, bf16[2,2,4,32,256]{4,3,2,1,0:T(8,128)(2,1)S(1)}, u32[]{:S(2)}, u32[]{:S(2)}) collective-permute-start(bf16[2,2,4,32,256]{4,3,2,1,0:T(8,128)(2,1)S(1)} %bitcast.24), channel_id=1, source_target_pairs={{0,8},{1,9},{2,10},{3,11},{4,12},{5,13},{6,14},{7,15},{8,0},{9,1},... | collective-permute-start | bytes 786440 | tf_op jit(solution)/shard_map/ppermute | solution.py:51
  32.1 4.7 %collective-permute-start.16 = (bf16[2,2,4,32,256]{4,3,2,1,0:T(8,128)(2,1)S(1)}, bf16[2,2,4,32,256]{4,3,2,1,0:T(8,128)(2,1)S(1)}, u32[]{:S(2)}, u32[]{:S(2)}) collective-permute-start(bf16[2,2,4,32,256]{4,3,2,1,0:T(8,128)(2,1)S(1)} %collective-permute-done.12.refs_3_), channel_id=1, source_target_pairs={{0,8},{1,9},{2,10},{3,11},{4,12},{5,13},{6,14},{7,15},{8,0},{9,1},... | collective-permute-start | bytes 786440 | tf_op jit(solution)/shard_map/ppermute | solution.py:51
  32.7 4.1 %collective-permute-start.15 = (bf16[2,2,4,32,256]{4,3,2,1,0:T(8,128)(2,1)S(1)}, bf16[2,2,4,32,256]{4,3,2,1,0:T(8,128)(2,1)S(1)}, u32[]{:S(2)}, u32[]{:S(2)}) collective-permute-start(bf16[2,2,4,32,256]{4,3,2,1,0:T(8,128)(2,1)S(1)} %collective-permute-done.11.refs_2_), channel_id=1, source_target_pairs={{0,8},{1,9},{2,10},{3,11},{4,12},{5,13},{6,14},{7,15},{8,0},{9,1},... | collective-permute-start | bytes 786440 | tf_op jit(solution)/shard_map/ppermute | solution.py:51
  36.8 1.5 %collective-permute-start.14 = (bf16[2,2,4,32,256]{4,3,2,1,0:T(8,128)(2,1)S(1)}, bf16[2,2,4,32,256]{4,3,2,1,0:T(8,128)(2,1)S(1)}, u32[]{:S(2)}, u32[]{:S(2)}) collective-permute-start(bf16[2,2,4,32,256]{4,3,2,1,0:T(8,128)(2,1)S(1)} %collective-permute-done.6.refs_1_), channel_id=1, source_target_pairs={{0,8},{1,9},{2,10},{3,11},{4,12},{5,13},{6,14},{7,15},{8,0},{9,1},... | collective-permute-start | bytes 786440 | tf_op jit(solution)/shard_map/ppermute | solution.py:51
  41.0 4.6 %collective-permute-start.20 = (f32[2,2,256,128]{3,2,1,0:T(8,128)S(1)}, f32[2,2,256,128]{3,2,1,0:T(8,128)S(1)}, u32[]{:S(2)}, u32[]{:S(2)}) collective-permute-start(f32[2,2,256,128]{3,2,1,0:T(8,128)S(1)} %get-tuple-element.39), channel_id=1, source_target_pairs={{0,8},{1,9},{2,10},{3,11},{4,12},{5,13},{6,14},{7,15},{8,0},{9,1},... | collective-permute-start | bytes 1572872 | tf_op jit(solution)/shard_map/ppermute | solution.py:51
  41.2 6.2 %collective-permute-start.17 = (f32[2,32,256]{2,1,0:T(8,128)S(1)}, f32[2,32,256]{2,1,0:T(8,128)S(1)}, u32[]{:S(2)}, u32[]{:S(2)}) collective-permute-start(f32[2,32,256]{2,1,0:T(8,128)S(1)} %get-tuple-element.29), channel_id=1, source_target_pairs={{0,1},{1,0},{2,3},{3,2},{4,5},{5,4},{6,7},{7,6},{8,9},{9,8},{10,11... | collective-permute-start | bytes 196616 | tf_op jit(solution)/shard_map/ppermute | solution.py:51
  42.5 7.8 %collective-permute-start.18 = (f32[2,32,256]{2,1,0:T(8,128)S(1)}, f32[2,32,256]{2,1,0:T(8,128)S(1)}, u32[]{:S(2)}, u32[]{:S(2)}) collective-permute-start(f32[2,32,256]{2,1,0:T(8,128)S(1)} %get-tuple-element.30), channel_id=1, source_target_pairs={{0,4},{1,5},{2,6},{3,7},{4,0},{5,1},{6,2},{7,3},{8,12},{9,13},{10,... | collective-permute-start | bytes 196616 | tf_op jit(solution)/shard_map/ppermute | solution.py:51
  43.8 7.5 %collective-permute-start.19 = (f32[2,32,256]{2,1,0:T(8,128)S(1)}, f32[2,32,256]{2,1,0:T(8,128)S(1)}, u32[]{:S(2)}, u32[]{:S(2)}) collective-permute-start(f32[2,32,256]{2,1,0:T(8,128)S(1)} %get-tuple-element.31), channel_id=1, source_target_pairs={{0,5},{1,4},{2,7},{3,6},{4,1},{5,0},{6,3},{7,2},{8,13},{9,12},{10,... | collective-permute-start | bytes 196616 | tf_op jit(solution)/shard_map/ppermute | solution.py:51
  45.7 7.6 %collective-permute-start.21 = (f32[256,128]{1,0:T(8,128)S(1)}, f32[256,128]{1,0:T(8,128)S(1)}, u32[]{:S(2)}, u32[]{:S(2)}) collective-permute-start(f32[256,128]{1,0:T(8,128)S(1)} %get-tuple-element.41), channel_id=1, source_target_pairs={{0,2},{1,3},{2,0},{3,1},{4,6},{5,7},{6,4},{7,5},{8,10},{9,11},{10,... | collective-permute-start | bytes 393224 | tf_op jit(solution)/shard_map/ppermute | solution.py:51
  46.4 6.8 %collective-permute-start.22 = (f32[256,128]{1,0:T(8,128)S(1)}, f32[256,128]{1,0:T(8,128)S(1)}, u32[]{:S(2)}, u32[]{:S(2)}) collective-permute-start(f32[256,128]{1,0:T(8,128)S(1)} %get-tuple-element.42), channel_id=1, source_target_pairs={{0,16},{1,17},{2,18},{3,19},{4,20},{5,21},{6,22},{7,23},{8,24},{9,... | collective-permute-start | bytes 393224 | tf_op jit(solution)/shard_map/ppermute | solution.py:51
  47.4 7.4 %collective-permute-start.23 = (f32[256,128]{1,0:T(8,128)S(1)}, f32[256,128]{1,0:T(8,128)S(1)}, u32[]{:S(2)}, u32[]{:S(2)}) collective-permute-start(f32[256,128]{1,0:T(8,128)S(1)} %get-tuple-element.43), channel_id=1, source_target_pairs={{0,18},{1,19},{2,16},{3,17},{4,22},{5,23},{6,20},{7,21},{8,26},{9,... | collective-permute-start | bytes 393224 | tf_op jit(solution)/shard_map/ppermute | solution.py:51

commit v7 on v6

--- a/solution.py
+++ b/solution.py
@@ -192,17 +192,16 @@
     high, low = high_ref[...], low_ref[...]
     block = high.shape[1]
     pair = jnp.concatenate([high, low], 1)
+    x_count, _, cols_each, rows_each = keep_ref.shape
     for k in range(supernodes):
-        both = dot_rows(left_high_ref[k], pair)
-        window_ref[k * width : (k + 1) * width, :] = (
-            both[:, :block] + both[:, block:] + dot_rows(left_low_ref[k], high)
-        )
-    x_count, _, rows_each, cols_each = keep_ref.shape
+        both = dot_rows(pair, left_high_ref[k])
+        total = both[:block] + both[block:] + dot_rows(high, left_low_ref[k])
+        for first in range(0, width, rows_each):
+            window_ref[(k * width + first) // rows_each] = total[:, first : first + rows_each]
     for dx in range(x_count):
         for target, dc in ((keep_ref, 0), (send_ref, 1)):
-            row_block = 2 * lax.bitwise_xor(x, dx) + lax.bitwise_xor(core, dc)
-            rows = window_ref[pl.ds(pl.multiple_of(row_block * rows_each, rows_each), rows_each), :]
-            first, second = rows[:, :cols_each], rows[:, cols_each:]
+            part = window_ref[2 * lax.bitwise_xor(x, dx) + lax.bitwise_xor(core, dc)]
+            first, second = part[:cols_each], part[cols_each:]
             target[dx, 0] = jnp.where(half == 0, first, second)
             target[dx, 1] = jnp.where(half == 0, second, first)
 
@@ -215,11 +214,11 @@
 
 
 def last_kernel(_, *refs):
-    *part_refs, window_ref = refs
+    *part_refs, own_ref, window_ref = refs
     total = part_refs[0][...]
     for ref in part_refs[1:]:
         total = total + ref[...]
-    window_ref[...] = total
+    window_ref[...] = total.T + own_ref[...]
 
 
 def ys_kernel(place_ref, *refs):
@@ -374,8 +373,8 @@
         window_kernel,
         [place, high, low, sums_high, sums_low],
         1,
-        [shape((x_count, 2, rows_each, cols_each), f32)] * 2,
-        [pltpu.VMEM((order, block), f32)],
+        [shape((x_count, 2, cols_each, rows_each), f32)] * 2,
+        [pltpu.VMEM((prow_count, block, rows_each), f32)],
         cost=1_400_000_000,
     )
     received = move(send, 0, 1, 0, 0)
@@ -383,7 +382,7 @@
         add_kernel,
         [keep, received],
         0,
-        [shape((rows_each, cols_each), f32)] * (2 * x_count),
+        [shape((cols_each, rows_each), f32)] * (2 * x_count),
         [],
         cost=100_000_000,
     )

time: 55.7 us -> 55.7 us (level)
  no operation moved by 1% of the time
where the time goes in v7:
time: 55.7 us; the launch traced here: 55.5 us
  starting transfers between devices  24.9 us (45%)
  waiting for transfers between devices  19.7 us (35%)
  Pallas kernels  7.93 us (14%)
  local copies, waits for them, and re-layouts  2.22 us (4%)
  between operations  0.74 us (1%)
    ppermute x24, starting transfers between devices, move(): return lax.ppermute(value, AXES, pairs)  24.9 us
    ppermute x24, waiting for transfers between devices, move(): return lax.ppermute(value, AXES, pairs)  19.7 us
    pallas_call x8, Pallas kernels, call(): pl.pallas_call(kernel, out_shape=outs if last else [pltpu.VMEM(out.shape,...  7.93 us
    unnamed x8, local copies, waits for them, and re-layouts  1.15 us
  transfers between devices with their start and end apart: 24, of which 12 were waited for; matrix products, arithmetic and copies ran while one was open for 2% of the time, Pallas kernels for 8%

profile of v7, /device:TPU:0, one launch (start us, length us, event | category | flops | bytes accessed | tf_op | source)
XLA Modules:
  0.0 55.5 jit_solution(16547480468187570032)
XLA Ops:
  0.6 4.1 %collective-permute-start.4 = (bf16[4,2,32,256]{3,2,1,0:T(8,128)(2,1)}, bf16[4,2,32,256]{3,2,1,0:T(8,128)(2,1)S(1)}, u32[]{:S(2)}, u32[]{:S(2)}) collective-permute-start(bf16[4,2,32,256]{3,2,1,0:T(8,128)(2,1)} %bitcast.26), channel_id=1, source_target_pairs={{0,4},{1,5},{2,6},{3,7},{4,0},{5,1},{6,2},{7,3},{8,12},{9,13},{10,... | collective-permute-start | bytes 393224 | tf_op jit(solution)/shard_map/ppermute | solution.py:51
  4.7 1.0 %constant_dynamic-slice_fusion = (bf16[2,2,1,2,32,256]{5,4,3,2,1,0:T(8,128)(2,1)S(1)}, bf16[2,2,1,2,32,256]{5,4,3,2,1,0:T(8,128)(2,1)S(1)}) fusion(bf16[2,2,2,2,32,256]{5,4,3,2,1,0:T(8,128)(2,1)} %bitcast.29, s32[]{:T(128)S(6)} %select_n.39, s32[]{:T(128)S(6)} %select_n.38), kind=kLoop, calls=%fused_computation | loop fusion | bytes 524296 | tf_op jit(solution)/shard_map/jit(dynamic_index_in_dim)/dynamic_slice | solution.py:287
  5.7 1.6 %collective-permute-start.1 = (bf16[256,256]{1,0:T(8,128)(2,1)S(1)}, bf16[256,256]{1,0:T(8,128)(2,1)S(1)}, u32[]{:S(2)}, u32[]{:S(2)}) collective-permute-start(bf16[256,256]{1,0:T(8,128)(2,1)S(1)} %bitcast.30), channel_id=1, source_target_pairs={{0,2},{1,3},{2,0},{3,1},{4,6},{5,7},{6,4},{7,5},{8,10},{9,11},{10,... | collective-permute-start | bytes 393224 | tf_op jit(solution)/shard_map/ppermute | solution.py:51
  7.4 1.5 %collective-permute-start.3 = (bf16[4,2,32,256]{3,2,1,0:T(8,128)(2,1)}, bf16[4,2,32,256]{3,2,1,0:T(8,128)(2,1)S(1)}, u32[]{:S(2)}, u32[]{:S(2)}) collective-permute-start(bf16[4,2,32,256]{3,2,1,0:T(8,128)(2,1)} %bitcast.27), channel_id=1, source_target_pairs={{0,1},{1,0},{2,3},{3,2},{4,5},{5,4},{6,7},{7,6},{8,9},{9,8},{10,11... | collective-permute-start | bytes 393224 | tf_op jit(solution)/shard_map/ppermute | solution.py:51
  8.9 0.2 collective-permute-start.9
  9.1 0.3 collective-permute-start
  9.4 0.1 stack.27.place_ref
  9.5 1.1 %copy-done = bf16[6,256,256]{2,1,0:T(8,128)(2,1)S(1)} copy-done((bf16[6,256,256]{2,1,0:T(8,128)(2,1)S(1)}, bf16[6,256,256]{2,1,0:T(8,128)(2,1)}, u32[]{:S(2)}) %copy-start) | copy-done | bytes 786456
  10.6 0.6 %shard_map.68.inverse_ref.refs_4_ = f32[6,256,256]{2,1,0:T(8,128)S(1)} custom-call(bf16[6,256,256]{2,1,0:T(8,128)(2,1)S(1)} %copy-done), custom_call_target="tpu_custom_call" | custom-call | flops 1000000000 | tf_op jit(solution)/shard_map/pallas_call | solution.py:253
  11.2 0.0 copy-start.2
  11.3 0.0 copy-start.3
  11.3 0.7 %collective-permute-done.4.refs_2_ = bf16[4,2,32,256]{3,2,1,0:T(8,128)(2,1)S(1)} collective-permute-done((bf16[4,2,32,256]{3,2,1,0:T(8,128)(2,1)}, bf16[4,2,32,256]{3,2,1,0:T(8,128)(2,1)S(1)}, u32[]{:S(2)}, u32[]{:S(2)}) %collective-permute-start.4) | collective-permute-done | bytes 131104 | tf_op jit(solution)/shard_map/ppermute | solution.py:51
  11.9 3.1 %collective-permute-start.5 = (bf16[4,2,32,256]{3,2,1,0:T(8,128)(2,1)S(1)}, bf16[4,2,32,256]{3,2,1,0:T(8,128)(2,1)S(1)}, u32[]{:S(2)}, u32[]{:S(2)}) collective-permute-start(bf16[4,2,32,256]{3,2,1,0:T(8,128)(2,1)S(1)} %collective-permute-done.4.refs_2_), channel_id=1, source_target_pairs={{0,1},{1,0},{2,3},{3,2},{4,5},{5,4},{6,7},{7,6},{8,9},{9,8},{10,11... | collective-permute-start | bytes 393224 | tf_op jit(solution)/shard_map/ppermute | solution.py:51
  15.0 0.0 collective-permute-done.1.refs_10_
  15.0 0.0 collective-permute-start.2
  15.0 0.0 copy-done.1
  15.0 1.2 %shard_map.69.refs_4_ = f32[256,128]{1,0:T(8,128)S(1)} custom-call(s32[6]{0:T(128)S(1)} %stack.27.place_ref, f32[6,256,256]{2,1,0:T(8,128)S(1)} %shard_map.68.inverse_ref.refs_4_, bf16[4,256,256]{2,1,0:T(8,128)(2,1)S(1)} %copy-done.1), custom_call_target="tpu_custom_call" | custom-call | flops 3000000000 | tf_op jit(solution)/shard_map/pallas_call | solution.py:253
  16.2 0.6 %collective-permute-done.refs_9_ = bf16[256,256]{1,0:T(8,128)(2,1)S(1)} collective-permute-done((bf16[256,256]{1,0:T(8,128)(2,1)S(1)}, bf16[256,256]{1,0:T(8,128)(2,1)S(1)}, u32[]{:S(2)}, u32[]{:S(2)}) %collective-permute-start) | collective-permute-done | bytes 131104 | tf_op jit(solution)/shard_map/ppermute | solution.py:51
  16.8 0.3 collective-permute-start.7
  17.2 3.5 %collective-permute-done.2.refs_11_ = bf16[256,256]{1,0:T(8,128)(2,1)S(1)} collective-permute-done((bf16[256,256]{1,0:T(8,128)(2,1)S(1)}, bf16[256,256]{1,0:T(8,128)(2,1)S(1)}, u32[]{:S(2)}, u32[]{:S(2)}) %collective-permute-start.2) | collective-permute-done | bytes 131104 | tf_op jit(solution)/shard_map/ppermute | solution.py:51
  20.7 0.0 collective-permute-done.3.refs_1_
  20.7 0.0 collective-permute-done.5.refs_3_
  20.7 0.0 copy-done.2
  20.7 0.0 copy-done.3
  20.7 1.3 %shard_map.70 = (bf16[4,256,256]{2,1,0:T(8,128)(2,1)S(1)}, bf16[4,256,256]{2,1,0:T(8,128)(2,1)S(1)}, bf16[2,256,256]{2,1,0:T(8,128)(2,1)S(1)}) custom-call(s32[6]{0:T(128)S(1)} %stack.27.place_ref, s32[4,8]{1,0:T(4,128)S(1)} %copy-done.3, bf16[4,2,32,256]{3,2,1,0:T(8,128)(2,1)S(1)} %bitcast.28, bf16[4,2,32,256]{3,2,1,0:T(8,128)(2,1)S(1)} %collective-permute-done.3.refs_1_, ...), custom_call_target="tpu_custom_call" | custom-call | flops 2500000000 | tf_op jit(solution)/shard_map/pallas_call | solution.py:253
  22.0 1.6 %collective-permute-start.12 = (bf16[2,2,4,32,256]{4,3,2,1,0:T(8,128)(2,1)S(1)}, bf16[2,2,4,32,256]{4,3,2,1,0:T(8,128)(2,1)S(1)}, u32[]{:S(2)}, u32[]{:S(2)}) collective-permute-start(bf16[2,2,4,32,256]{4,3,2,1,0:T(8,128)(2,1)S(1)} %bitcast.21), channel_id=1, source_target_pairs={{0,16},{1,17},{2,18},{3,19},{4,20},{5,21},{6,22},{7,23},{8,24},{9,... | collective-permute-start | bytes 786440 | tf_op jit(solution)/shard_map/ppermute | solution.py:51
  23.6 0.4 collective-permute-start.11
  24.0 1.5 %collective-permute-start.6 = (bf16[2,2,4,32,256]{4,3,2,1,0:T(8,128)(2,1)S(1)}, bf16[2,2,4,32,256]{4,3,2,1,0:T(8,128)(2,1)S(1)}, u32[]{:S(2)}, u32[]{:S(2)}) collective-permute-start(bf16[2,2,4,32,256]{4,3,2,1,0:T(8,128)(2,1)S(1)} %bitcast.23), channel_id=1, source_target_pairs={{0,18},{1,19},{2,16},{3,17},{4,22},{5,23},{6,20},{7,21},{8,26},{9,... | collective-permute-start | bytes 786440 | tf_op jit(solution)/shard_map/ppermute | solution.py:51
  25.6 0.0 collective-permute-done.9.refs_14_
  25.6 1.5 %collective-permute-start.10 = (bf16[256,256]{1,0:T(8,128)(2,1)S(1)}, bf16[256,256]{1,0:T(8,128)(2,1)S(1)}, u32[]{:S(2)}, u32[]{:S(2)}) collective-permute-start(bf16[256,256]{1,0:T(8,128)(2,1)S(1)} %collective-permute-done.9.refs_14_), channel_id=1, source_target_pairs={{0,1},{1,0},{2,3},{3,2},{4,5},{5,4},{6,7},{7,6},{8,9},{9,8},{10,11... | collective-permute-start | bytes 393224 | tf_op jit(solution)/shard_map/ppermute | solution.py:51
  27.1 0.0 collective-permute-done.7.refs_12_
  27.1 0.5 collective-permute-start.8
  27.6 2.9 %collective-permute-done.10.refs_15_ = bf16[256,256]{1,0:T(8,128)(2,1)S(1)} collective-permute-done((bf16[256,256]{1,0:T(8,128)(2,1)S(1)}, bf16[256,256]{1,0:T(8,128)(2,1)S(1)}, u32[]{:S(2)}, u32[]{:S(2)}) %collective-permute-start.10) | collective-permute-done | bytes 131104 | tf_op jit(solution)/shard_map/ppermute | solution.py:51
  30.6 0.0 collective-permute-start.13
  30.6 1.5 %collective-permute-done.8.refs_13_ = bf16[256,256]{1,0:T(8,128)(2,1)S(1)} collective-permute-done((bf16[256,256]{1,0:T(8,128)(2,1)S(1)}, bf16[256,256]{1,0:T(8,128)(2,1)S(1)}, u32[]{:S(2)}, u32[]{:S(2)}) %collective-permute-start.8) | collective-permute-done | bytes 131104 | tf_op jit(solution)/shard_map/ppermute | solution.py:51
  32.1 0.0 collective-permute-done.12.refs_3_
  32.1 0.0 collective-permute-start.16
  32.1 0.6 %collective-permute-done.11.refs_2_ = bf16[2,2,4,32,256]{4,3,2,1,0:T(8,128)(2,1)S(1)} collective-permute-done((bf16[2,2,4,32,256]{4,3,2,1,0:T(8,128)(2,1)S(1)}, bf16[2,2,4,32,256]{4,3,2,1,0:T(8,128)(2,1)S(1)}, u32[]{:S(2)}, u32[]{:S(2)}) %collective-permute-start.11) | collective-permute-done | bytes 262176 | tf_op jit(solution)/shard_map/ppermute | solution.py:51
  32.7 0.0 collective-permute-start.15
  32.7 4.1 %collective-permute-done.6.refs_1_ = bf16[2,2,4,32,256]{4,3,2,1,0:T(8,128)(2,1)S(1)} collective-permute-done((bf16[2,2,4,32,256]{4,3,2,1,0:T(8,128)(2,1)S(1)}, bf16[2,2,4,32,256]{4,3,2,1,0:T(8,128)(2,1)S(1)}, u32[]{:S(2)}, u32[]{:S(2)}) %collective-permute-start.6) | collective-permute-done | bytes 262176 | tf_op jit(solution)/shard_map/ppermute | solution.py:51
  36.8 0.0 collective-permute-start.14
  36.8 0.0 collective-permute-done.13.refs_4_
  36.8 0.0 collective-permute-done.16.refs_7_
  36.8 0.0 collective-permute-done.15.refs_6_
  36.8 1.5 %collective-permute-done.14.refs_5_ = bf16[2,2,4,32,256]{4,3,2,1,0:T(8,128)(2,1)S(1)} collective-permute-done((bf16[2,2,4,32,256]{4,3,2,1,0:T(8,128)(2,1)S(1)}, bf16[2,2,4,32,256]{4,3,2,1,0:T(8,128)(2,1)S(1)}, u32[]{:S(2)}, u32[]{:S(2)}) %collective-permute-start.14) | collective-permute-done | bytes 262176 | tf_op jit(solution)/shard_map/ppermute | solution.py:51
  38.3 1.4 %shard_map.71 = (f32[2,32,256]{2,1,0:T(8,128)S(1)}, f32[2,32,256]{2,1,0:T(8,128)S(1)}, f32[2,32,256]{2,1,0:T(8,128)S(1)}, f32[2,32,256]{2,1,0:T(8,128)S(1)}, bf1...) custom-call(s32[6]{0:T(128)S(1)} %stack.27.place_ref, s32[4,8]{1,0:T(4,128)S(1)} %copy-done.3, ...), custom_call_target="tpu_custom_call" | custom-call | flops 1700000000 | tf_op jit(solution)/shard_map/pallas_call | solution.py:253
  39.8 1.2 %shard_map.73 = (f32[2,2,128,256]{3,2,1,0:T(8,128)S(1)}, f32[2,2,128,256]{3,2,1,0:T(8,128)S(1)}) custom-call(s32[6]{0:T(128)S(1)} %stack.27.place_ref, bf16[4,256,256]{2,1,0:T(8,128)(2,1)S(1)} %get-tuple-element.34.left_high_ref, bf16[4,256,256]{2,1,0:T(8,128)(2,1)S(1)} %get-tuple-element.35.left_low_ref, bf16[256,256]{1,0:T(8,128)(2,1)S(1)} %get-tuple-element.36.high_ref, ...), custom_call_target="tpu_custom_call" | custom-call | flops 1400000000 | tf_op jit(solution)/shard_map/pallas_call | solution.py:253
  41.0 0.2 collective-permute-start.20
  41.2 1.3 %collective-permute-start.17 = (f32[2,32,256]{2,1,0:T(8,128)S(1)}, f32[2,32,256]{2,1,0:T(8,128)S(1)}, u32[]{:S(2)}, u32[]{:S(2)}) collective-permute-start(f32[2,32,256]{2,1,0:T(8,128)S(1)} %get-tuple-element.29), channel_id=1, source_target_pairs={{0,1},{1,0},{2,3},{3,2},{4,5},{5,4},{6,7},{7,6},{8,9},{9,8},{10,11... | collective-permute-start | bytes 196616 | tf_op jit(solution)/shard_map/ppermute | solution.py:51
  42.4 1.4 %collective-permute-start.18 = (f32[2,32,256]{2,1,0:T(8,128)S(1)}, f32[2,32,256]{2,1,0:T(8,128)S(1)}, u32[]{:S(2)}, u32[]{:S(2)}) collective-permute-start(f32[2,32,256]{2,1,0:T(8,128)S(1)} %get-tuple-element.30), channel_id=1, source_target_pairs={{0,4},{1,5},{2,6},{3,7},{4,0},{5,1},{6,2},{7,3},{8,12},{9,13},{10,... | collective-permute-start | bytes 196616 | tf_op jit(solution)/shard_map/ppermute | solution.py:51
  43.8 1.8 %collective-permute-start.19 = (f32[2,32,256]{2,1,0:T(8,128)S(1)}, f32[2,32,256]{2,1,0:T(8,128)S(1)}, u32[]{:S(2)}, u32[]{:S(2)}) collective-permute-start(f32[2,32,256]{2,1,0:T(8,128)S(1)} %get-tuple-element.31), channel_id=1, source_target_pairs={{0,5},{1,4},{2,7},{3,6},{4,1},{5,0},{6,3},{7,2},{8,13},{9,12},{10,... | collective-permute-start | bytes 196616 | tf_op jit(solution)/shard_map/ppermute | solution.py:51
  45.6 0.0 collective-permute-done.20.received_ref
  45.6 0.1 shard_map.74
  45.6 0.8 %collective-permute-start.21 = (f32[128,256]{1,0:T(8,128)S(1)}, f32[128,256]{1,0:T(8,128)S(1)}, u32[]{:S(2)}, u32[]{:S(2)}) collective-permute-start(f32[128,256]{1,0:T(8,128)S(1)} %get-tuple-element.41), channel_id=1, source_target_pairs={{0,2},{1,3},{2,0},{3,1},{4,6},{5,7},{6,4},{7,5},{8,10},{9,11},{10,... | collective-permute-start | bytes 393224 | tf_op jit(solution)/shard_map/ppermute | solution.py:51
  46.4 1.0 %collective-permute-start.22 = (f32[128,256]{1,0:T(8,128)S(1)}, f32[128,256]{1,0:T(8,128)S(1)}, u32[]{:S(2)}, u32[]{:S(2)}) collective-permute-start(f32[128,256]{1,0:T(8,128)S(1)} %get-tuple-element.42), channel_id=1, source_target_pairs={{0,16},{1,17},{2,18},{3,19},{4,20},{5,21},{6,22},{7,23},{8,24},{9,... | collective-permute-start | bytes 393224 | tf_op jit(solution)/shard_map/ppermute | solution.py:51
  47.4 0.0 collective-permute-done.17.refs_1_
  47.4 1.8 %collective-permute-start.23 = (f32[128,256]{1,0:T(8,128)S(1)}, f32[128,256]{1,0:T(8,128)S(1)}, u32[]{:S(2)}, u32[]{:S(2)}) collective-permute-start(f32[128,256]{1,0:T(8,128)S(1)} %get-tuple-element.43), channel_id=1, source_target_pairs={{0,18},{1,19},{2,16},{3,17},{4,22},{5,23},{6,20},{7,21},{8,26},{9,... | collective-permute-start | bytes 393224 | tf_op jit(solution)/shard_map/ppermute | solution.py:51
  49.2 1.0 %collective-permute-done.18.refs_2_ = f32[2,32,256]{2,1,0:T(8,128)S(1)} collective-permute-done((f32[2,32,256]{2,1,0:T(8,128)S(1)}, f32[2,32,256]{2,1,0:T(8,128)S(1)}, u32[]{:S(2)}, u32[]{:S(2)}) %collective-permute-start.18) | collective-permute-done | bytes 65568 | tf_op jit(solution)/shard_map/ppermute | solution.py:51
  50.2 1.0 %collective-permute-done.19.refs_3_ = f32[2,32,256]{2,1,0:T(8,128)S(1)} collective-permute-done((f32[2,32,256]{2,1,0:T(8,128)S(1)}, f32[2,32,256]{2,1,0:T(8,128)S(1)}, u32[]{:S(2)}, u32[]{:S(2)}) %collective-permute-start.19) | collective-permute-done | bytes 65568 | tf_op jit(solution)/shard_map/ppermute | solution.py:51
  51.3 1.3 %shard_map.72 = (f32[4,2,32,256]{3,2,1,0:T(8,128)}, f32[8,128]{1,0:T(8,128)S(1)}) custom-call(s32[6]{0:T(128)S(1)} %stack.27.place_ref, f32[2,32,256]{2,1,0:T(8,128)S(1)} %get-tuple-element.28.refs_0_, f32[2,32,256]{2,1,0:T(8,128)S(1)} %collective-permute-done.17.refs_1_, f32[2,32,256]{2,1,0:T(8,128)S(1)} %collective-permute-done.18.refs_2_, ...), custom_call_target="tpu_custom_call" | custom-call | flops 12000000000 | tf_op jit(solution)/shard_map/pallas_call | solution.py:253
  52.6 0.7 %collective-permute-done.21.refs_1_ = f32[128,256]{1,0:T(8,128)S(1)} collective-permute-done((f32[128,256]{1,0:T(8,128)S(1)}, f32[128,256]{1,0:T(8,128)S(1)}, u32[]{:S(2)}, u32[]{:S(2)}) %collective-permute-start.21) | collective-permute-done | bytes 131104 | tf_op jit(solution)/shard_map/ppermute | solution.py:51
  53.3 0.0 collective-permute-done.22.refs_2_
  53.3 1.5 %collective-permute-done.23.refs_3_ = f32[128,256]{1,0:T(8,128)S(1)} collective-permute-done((f32[128,256]{1,0:T(8,128)S(1)}, f32[128,256]{1,0:T(8,128)S(1)}, u32[]{:S(2)}, u32[]{:S(2)}) %collective-permute-start.23) | collective-permute-done | bytes 131104 | tf_op jit(solution)/shard_map/ppermute | solution.py:51
  54.8 0.8 %shard_map.75 = f32[256,128]{1,0:T(8,128)} custom-call(f32[8,128]{1,0:T(8,128)S(1)} %get-tuple-element.33._, f32[128,256]{1,0:T(8,128)S(1)} %get-tuple-element.40.refs_0_, f32[128,256]{1,0:T(8,128)S(1)} %collective-permute-done.21.refs_1_, f32[128,256]{1,0:T(8,128)S(1)} %collective-permute-done.22.refs_2_, f32[128,256]{1,0:T(8,128)S(1)} %collective-permute-done.23.refs_3_, ...), custom_call_target="tpu_custom_call" | custom-call | flops 500000000 | tf_op jit(solution)/shard_map/pallas_call | solution.py:253
  (2 shorter events, 0.0 us)
Async XLA Ops:
  0.6 11.3 %collective-permute-start.4 = (bf16[4,2,32,256]{3,2,1,0:T(8,128)(2,1)}, bf16[4,2,32,256]{3,2,1,0:T(8,128)(2,1)S(1)}, u32[]{:S(2)}, u32[]{:S(2)}) collective-permute-start(bf16[4,2,32,256]{3,2,1,0:T(8,128)(2,1)} %bitcast.26), channel_id=1, source_target_pairs={{0,4},{1,5},{2,6},{3,7},{4,0},{5,1},{6,2},{7,3},{8,12},{9,13},{10,... | collective-permute-start | bytes 393224 | tf_op jit(solution)/shard_map/ppermute | solution.py:51
  5.7 9.3 %collective-permute-start.1 = (bf16[256,256]{1,0:T(8,128)(2,1)S(1)}, bf16[256,256]{1,0:T(8,128)(2,1)S(1)}, u32[]{:S(2)}, u32[]{:S(2)}) collective-permute-start(bf16[256,256]{1,0:T(8,128)(2,1)S(1)} %bitcast.30), channel_id=1, source_target_pairs={{0,2},{1,3},{2,0},{3,1},{4,6},{5,7},{6,4},{7,5},{8,10},{9,11},{10,... | collective-permute-start | bytes 393224 | tf_op jit(solution)/shard_map/ppermute | solution.py:51
  7.4 13.3 %collective-permute-start.3 = (bf16[4,2,32,256]{3,2,1,0:T(8,128)(2,1)}, bf16[4,2,32,256]{3,2,1,0:T(8,128)(2,1)S(1)}, u32[]{:S(2)}, u32[]{:S(2)}) collective-permute-start(bf16[4,2,32,256]{3,2,1,0:T(8,128)(2,1)} %bitcast.27), channel_id=1, source_target_pairs={{0,1},{1,0},{2,3},{3,2},{4,5},{5,4},{6,7},{7,6},{8,9},{9,8},{10,11... | collective-permute-start | bytes 393224 | tf_op jit(solution)/shard_map/ppermute | solution.py:51
  8.9 16.7 %collective-permute-start.9 = (bf16[256,256]{1,0:T(8,128)(2,1)S(1)}, bf16[256,256]{1,0:T(8,128)(2,1)S(1)}, u32[]{:S(2)}, u32[]{:S(2)}) collective-permute-start(bf16[256,256]{1,0:T(8,128)(2,1)S(1)} %bitcast.31), channel_id=1, source_target_pairs={{0,6},{1,7},{2,4},{3,5},{4,2},{5,3},{6,0},{7,1},{8,14},{9,15},{10,... | collective-permute-start | bytes 393224 | tf_op jit(solution)/shard_map/ppermute | solution.py:51
  9.1 7.7 %collective-permute-start = (bf16[256,256]{1,0:T(8,128)(2,1)S(1)}, bf16[256,256]{1,0:T(8,128)(2,1)S(1)}, u32[]{:S(2)}, u32[]{:S(2)}) collective-permute-start(bf16[256,256]{1,0:T(8,128)(2,1)S(1)} %bitcast.18), channel_id=1, source_target_pairs={{0,1},{1,0},{2,3},{3,2},{4,5},{5,4},{6,7},{7,6},{8,9},{9,8},{10,11... | collective-permute-start | bytes 393224 | tf_op jit(solution)/shard_map/ppermute | solution.py:51
  9.5 1.1 %copy-start = (bf16[6,256,256]{2,1,0:T(8,128)(2,1)S(1)}, bf16[6,256,256]{2,1,0:T(8,128)(2,1)}, u32[]{:S(2)}) copy-start(bf16[6,256,256]{2,1,0:T(8,128)(2,1)} %factor_ref.1) | copy-start | bytes 2359300
  10.6 4.4 %copy-start.1 = (bf16[4,256,256]{2,1,0:T(8,128)(2,1)S(1)}, bf16[4,256,256]{2,1,0:T(8,128)(2,1)}, u32[]{:S(2)}) copy-start(bf16[4,256,256]{2,1,0:T(8,128)(2,1)} %diag_ref.1) | copy-start | bytes 1572868
  11.2 9.4 %copy-start.2 = (bf16[4,2,1,32,256]{4,3,2,1,0:T(8,128)(2,1)S(1)}, bf16[4,2,1,32,256]{4,3,2,1,0:T(8,128)(2,1)}, u32[]{:S(2)}) copy-start(bf16[4,2,1,32,256]{4,3,2,1,0:T(8,128)(2,1)} %param.6) | copy-start | bytes 393220
  11.3 9.4 %copy-start.3 = (s32[4,8]{1,0:T(4,128)S(1)}, s32[4,8]{1,0:T(4,128)}, u32[]{:S(2)}) copy-start(s32[4,8]{1,0:T(4,128)} %flags_ref.3) | copy-start | bytes 388
  11.9 8.8 %collective-permute-start.5 = (bf16[4,2,32,256]{3,2,1,0:T(8,128)(2,1)S(1)}, bf16[4,2,32,256]{3,2,1,0:T(8,128)(2,1)S(1)}, u32[]{:S(2)}, u32[]{:S(2)}) collective-permute-start(bf16[4,2,32,256]{3,2,1,0:T(8,128)(2,1)S(1)} %collective-permute-done.4.refs_2_), channel_id=1, source_target_pairs={{0,1},{1,0},{2,3},{3,2},{4,5},{5,4},{6,7},{7,6},{8,9},{9,8},{10,11... | collective-permute-start | bytes 393224 | tf_op jit(solution)/shard_map/ppermute | solution.py:51
  15.0 5.7 %collective-permute-start.2 = (bf16[256,256]{1,0:T(8,128)(2,1)S(1)}, bf16[256,256]{1,0:T(8,128)(2,1)S(1)}, u32[]{:S(2)}, u32[]{:S(2)}) collective-permute-start(bf16[256,256]{1,0:T(8,128)(2,1)S(1)} %collective-permute-done.1.refs_10_), channel_id=1, source_target_pairs={{0,1},{1,0},{2,3},{3,2},{4,5},{5,4},{6,7},{7,6},{8,9},{9,8},{10,11... | collective-permute-start | bytes 393224 | tf_op jit(solution)/shard_map/ppermute | solution.py:51
  16.8 10.3 %collective-permute-start.7 = (bf16[256,256]{1,0:T(8,128)(2,1)S(1)}, bf16[256,256]{1,0:T(8,128)(2,1)S(1)}, u32[]{:S(2)}, u32[]{:S(2)}) collective-permute-start(bf16[256,256]{1,0:T(8,128)(2,1)S(1)} %bitcast.19), channel_id=1, source_target_pairs={{0,4},{1,5},{2,6},{3,7},{4,0},{5,1},{6,2},{7,3},{8,12},{9,13},{10,... | collective-permute-start | bytes 393224 | tf_op jit(solution)/shard_map/ppermute | solution.py:51
  22.0 10.1 %collective-permute-start.12 = (bf16[2,2,4,32,256]{4,3,2,1,0:T(8,128)(2,1)S(1)}, bf16[2,2,4,32,256]{4,3,2,1,0:T(8,128)(2,1)S(1)}, u32[]{:S(2)}, u32[]{:S(2)}) collective-permute-start(bf16[2,2,4,32,256]{4,3,2,1,0:T(8,128)(2,1)S(1)} %bitcast.21), channel_id=1, source_target_pairs={{0,16},{1,17},{2,18},{3,19},{4,20},{5,21},{6,22},{7,23},{8,24},{9,... | collective-permute-start | bytes 786440 | tf_op jit(solution)/shard_map/ppermute | solution.py:51
  23.6 9.1 %collective-permute-start.11 = (bf16[2,2,4,32,256]{4,3,2,1,0:T(8,128)(2,1)S(1)}, bf16[2,2,4,32,256]{4,3,2,1,0:T(8,128)(2,1)S(1)}, u32[]{:S(2)}, u32[]{:S(2)}) collective-permute-start(bf16[2,2,4,32,256]{4,3,2,1,0:T(8,128)(2,1)S(1)} %bitcast.22), channel_id=1, source_target_pairs={{0,2},{1,3},{2,0},{3,1},{4,6},{5,7},{6,4},{7,5},{8,10},{9,11},{10,... | collective-permute-start | bytes 786440 | tf_op jit(solution)/shard_map/ppermute | solution.py:51
  24.0 12.7 %collective-permute-start.6 = (bf16[2,2,4,32,256]{4,3,2,1,0:T(8,128)(2,1)S(1)}, bf16[2,2,4,32,256]{4,3,2,1,0:T(8,128)(2,1)S(1)}, u32[]{:S(2)}, u32[]{:S(2)}) collective-permute-start(bf16[2,2,4,32,256]{4,3,2,1,0:T(8,128)(2,1)S(1)} %bitcast.23), channel_id=1, source_target_pairs={{0,18},{1,19},{2,16},{3,17},{4,22},{5,23},{6,20},{7,21},{8,26},{9,... | collective-permute-start | bytes 786440 | tf_op jit(solution)/shard_map/ppermute | solution.py:51
  25.6 5.0 %collective-permute-start.10 = (bf16[256,256]{1,0:T(8,128)(2,1)S(1)}, bf16[256,256]{1,0:T(8,128)(2,1)S(1)}, u32[]{:S(2)}, u32[]{:S(2)}) collective-permute-start(bf16[256,256]{1,0:T(8,128)(2,1)S(1)} %collective-permute-done.9.refs_14_), channel_id=1, source_target_pairs={{0,1},{1,0},{2,3},{3,2},{4,5},{5,4},{6,7},{7,6},{8,9},{9,8},{10,11... | collective-permute-start | bytes 393224 | tf_op jit(solution)/shard_map/ppermute | solution.py:51
  27.1 5.0 %collective-permute-start.8 = (bf16[256,256]{1,0:T(8,128)(2,1)S(1)}, bf16[256,256]{1,0:T(8,128)(2,1)S(1)}, u32[]{:S(2)}, u32[]{:S(2)}) collective-permute-start(bf16[256,256]{1,0:T(8,128)(2,1)S(1)} %collective-permute-done.7.refs_12_), channel_id=1, source_target_pairs={{0,1},{1,0},{2,3},{3,2},{4,5},{5,4},{6,7},{7,6},{8,9},{9,8},{10,11... | collective-permute-start | bytes 393224 | tf_op jit(solution)/shard_map/ppermute | solution.py:51
  30.6 6.2 %collective-permute-start.13 = (bf16[2,2,4,32,256]{4,3,2,1,0:T(8,128)(2,1)S(1)}, bf16[2,2,4,32,256]{4,3,2,1,0:T(8,128)(2,1)S(1)}, u32[]{:S(2)}, u32[]{:S(2)}) collective-permute-start(bf16[2,2,4,32,256]{4,3,2,1,0:T(8,128)(2,1)S(1)} %bitcast.24), channel_id=1, source_target_pairs={{0,8},{1,9},{2,10},{3,11},{4,12},{5,13},{6,14},{7,15},{8,0},{9,1},... | collective-permute-start | bytes 786440 | tf_op jit(solution)/shard_map/ppermute | solution.py:51
  32.1 4.7 %collective-permute-start.16 = (bf16[2,2,4,32,256]{4,3,2,1,0:T(8,128)(2,1)S(1)}, bf16[2,2,4,32,256]{4,3,2,1,0:T(8,128)(2,1)S(1)}, u32[]{:S(2)}, u32[]{:S(2)}) collective-permute-start(bf16[2,2,4,32,256]{4,3,2,1,0:T(8,128)(2,1)S(1)} %collective-permute-done.12.refs_3_), channel_id=1, source_target_pairs={{0,8},{1,9},{2,10},{3,11},{4,12},{5,13},{6,14},{7,15},{8,0},{9,1},... | collective-permute-start | bytes 786440 | tf_op jit(solution)/shard_map/ppermute | solution.py:51
  32.7 4.1 %collective-permute-start.15 = (bf16[2,2,4,32,256]{4,3,2,1,0:T(8,128)(2,1)S(1)}, bf16[2,2,4,32,256]{4,3,2,1,0:T(8,128)(2,1)S(1)}, u32[]{:S(2)}, u32[]{:S(2)}) collective-permute-start(bf16[2,2,4,32,256]{4,3,2,1,0:T(8,128)(2,1)S(1)} %collective-permute-done.11.refs_2_), channel_id=1, source_target_pairs={{0,8},{1,9},{2,10},{3,11},{4,12},{5,13},{6,14},{7,15},{8,0},{9,1},... | collective-permute-start | bytes 786440 | tf_op jit(solution)/shard_map/ppermute | solution.py:51
  36.8 1.5 %collective-permute-start.14 = (bf16[2,2,4,32,256]{4,3,2,1,0:T(8,128)(2,1)S(1)}, bf16[2,2,4,32,256]{4,3,2,1,0:T(8,128)(2,1)S(1)}, u32[]{:S(2)}, u32[]{:S(2)}) collective-permute-start(bf16[2,2,4,32,256]{4,3,2,1,0:T(8,128)(2,1)S(1)} %collective-permute-done.6.refs_1_), channel_id=1, source_target_pairs={{0,8},{1,9},{2,10},{3,11},{4,12},{5,13},{6,14},{7,15},{8,0},{9,1},... | collective-permute-start | bytes 786440 | tf_op jit(solution)/shard_map/ppermute | solution.py:51
  41.0 4.6 %collective-permute-start.20 = (f32[2,2,128,256]{3,2,1,0:T(8,128)S(1)}, f32[2,2,128,256]{3,2,1,0:T(8,128)S(1)}, u32[]{:S(2)}, u32[]{:S(2)}) collective-permute-start(f32[2,2,128,256]{3,2,1,0:T(8,128)S(1)} %get-tuple-element.39), channel_id=1, source_target_pairs={{0,8},{1,9},{2,10},{3,11},{4,12},{5,13},{6,14},{7,15},{8,0},{9,1},... | collective-permute-start | bytes 1572872 | tf_op jit(solution)/shard_map/ppermute | solution.py:51
  41.2 6.2 %collective-permute-start.17 = (f32[2,32,256]{2,1,0:T(8,128)S(1)}, f32[2,32,256]{2,1,0:T(8,128)S(1)}, u32[]{:S(2)}, u32[]{:S(2)}) collective-permute-start(f32[2,32,256]{2,1,0:T(8,128)S(1)} %get-tuple-element.29), channel_id=1, source_target_pairs={{0,1},{1,0},{2,3},{3,2},{4,5},{5,4},{6,7},{7,6},{8,9},{9,8},{10,11... | collective-permute-start | bytes 196616 | tf_op jit(solution)/shard_map/ppermute | solution.py:51
  42.4 7.8 %collective-permute-start.18 = (f32[2,32,256]{2,1,0:T(8,128)S(1)}, f32[2,32,256]{2,1,0:T(8,128)S(1)}, u32[]{:S(2)}, u32[]{:S(2)}) collective-permute-start(f32[2,32,256]{2,1,0:T(8,128)S(1)} %get-tuple-element.30), channel_id=1, source_target_pairs={{0,4},{1,5},{2,6},{3,7},{4,0},{5,1},{6,2},{7,3},{8,12},{9,13},{10,... | collective-permute-start | bytes 196616 | tf_op jit(solution)/shard_map/ppermute | solution.py:51
  43.8 7.5 %collective-permute-start.19 = (f32[2,32,256]{2,1,0:T(8,128)S(1)}, f32[2,32,256]{2,1,0:T(8,128)S(1)}, u32[]{:S(2)}, u32[]{:S(2)}) collective-permute-start(f32[2,32,256]{2,1,0:T(8,128)S(1)} %get-tuple-element.31), channel_id=1, source_target_pairs={{0,5},{1,4},{2,7},{3,6},{4,1},{5,0},{6,3},{7,2},{8,13},{9,12},{10,... | collective-permute-start | bytes 196616 | tf_op jit(solution)/shard_map/ppermute | solution.py:51
  45.6 7.6 %collective-permute-start.21 = (f32[128,256]{1,0:T(8,128)S(1)}, f32[128,256]{1,0:T(8,128)S(1)}, u32[]{:S(2)}, u32[]{:S(2)}) collective-permute-start(f32[128,256]{1,0:T(8,128)S(1)} %get-tuple-element.41), channel_id=1, source_target_pairs={{0,2},{1,3},{2,0},{3,1},{4,6},{5,7},{6,4},{7,5},{8,10},{9,11},{10,... | collective-permute-start | bytes 393224 | tf_op jit(solution)/shard_map/ppermute | solution.py:51
  46.4 6.8 %collective-permute-start.22 = (f32[128,256]{1,0:T(8,128)S(1)}, f32[128,256]{1,0:T(8,128)S(1)}, u32[]{:S(2)}, u32[]{:S(2)}) collective-permute-start(f32[128,256]{1,0:T(8,128)S(1)} %get-tuple-element.42), channel_id=1, source_target_pairs={{0,16},{1,17},{2,18},{3,19},{4,20},{5,21},{6,22},{7,23},{8,24},{9,... | collective-permute-start | bytes 393224 | tf_op jit(solution)/shard_map/ppermute | solution.py:51
  47.4 7.4 %collective-permute-start.23 = (f32[128,256]{1,0:T(8,128)S(1)}, f32[128,256]{1,0:T(8,128)S(1)}, u32[]{:S(2)}, u32[]{:S(2)}) collective-permute-start(f32[128,256]{1,0:T(8,128)S(1)} %get-tuple-element.43), channel_id=1, source_target_pairs={{0,18},{1,19},{2,16},{3,17},{4,22},{5,23},{6,20},{7,21},{8,26},{9,... | collective-permute-start | bytes 393224 | tf_op jit(solution)/shard_map/ppermute | solution.py:51
